TPU v7x, 256 devices: a whole 4x4x8 slice. The times are simulated.
256 devices in a mesh: ctx: 4 (over z_lo), zero: 64 (over z_hi, x, y, core).
Axes of the slice: x: 4, y: 4, z: 8 (z_hi: 2, z_lo: 4; z = z_hi * 4 + z_lo), core: 2. Of those that a mesh axis runs over, the one named last changes fastest.
Arguments:
- proj: bfloat16 [64, 512, 3, 4096], P('zero', 'ctx'), may hold values from -6 to 6
- short_weight: float32 [3, 3, 4096], P(None, None, ('ctx', 'zero')), may hold values from -3 to 3
- residue: float32 [16, 4096], P(None, ('ctx', 'zero')), may hold values from -0.125 to 0.125
- log_decay: float32 [16, 4096], P(None, ('ctx', 'zero')), as said below
- cotangent: bfloat16 [64, 512, 4096], P('zero', 'ctx'), may hold values from -6 to 6
Outputs:
- output: bfloat16 [64, 512, 4096], P('zero', 'ctx')
- proj_grad: bfloat16 [64, 512, 3, 4096], P('zero', 'ctx')
- tap_grad: float32 [3, 3, 4096], P(None, None, ('ctx', 'zero'))
- residue_grad: float32 [16, 4096], P(None, ('ctx', 'zero'))
- decay_grad: float32 [16, 4096], P(None, ('ctx', 'zero'))
Inputs may be any that keep to these rules, and one draw needn't show every extreme that they name: exp(log_decay) lies between 0.3 / 512 and max(1 / 30, 2 / 512).
All inputs are finite; a program needn't handle non-finite values.
Results may differ from a plain program's by a relative error of at most 0.0058.
Values may be sent and summed in bfloat16 or wider, within the bound.
No kernel may reach another device: no remote copies, remote signals or barrier semaphores. Data moves between devices by JAX's collectives and lax.ppermute only.
A program may use at most 256 MiB of HBM per device.

v0:
```python
import math

import jax
import jax.numpy as jnp
from jax import lax
from jax.sharding import PartitionSpec as P

SHORT = 3


def rounded(values_in):
    return lax.optimization_barrier(values_in.astype(jnp.bfloat16)).astype(jnp.float32)


def taps_forward(extended, weights, length):
    margin = weights.shape[1] - 1
    summed = jnp.zeros(extended.shape[:1] + (length,) + extended.shape[2:], jnp.float32)
    for offset in range(weights.shape[1]):
        window = lax.slice_in_dim(extended, margin - offset, margin - offset + length, axis=1)
        summed = summed + weights[:, offset, :] * window.astype(jnp.float32)
    return summed


def taps_backward(extended_grad, weights, length):
    summed = jnp.zeros(extended_grad.shape[:1] + (length,) + extended_grad.shape[2:], jnp.float32)
    for offset in range(weights.shape[1]):
        window = lax.slice_in_dim(extended_grad, offset, offset + length, axis=1)
        summed = summed + weights[:, offset, :] * window
    return summed


def taps_weight_grad(grads, extended, length):
    margin = extended.shape[1] - length
    columns = []
    for offset in range(margin + 1):
        window = lax.slice_in_dim(extended, margin - offset, margin - offset + length, axis=1)
        columns.append(jnp.sum(grads * window.astype(jnp.float32), axis=(0, 1)))
    return jnp.stack(columns, axis=1)


def modal_filter(residues, log_rates, length):
    decay_rate = jnp.exp(log_rates)
    positions = lax.iota(jnp.int32, length).astype(jnp.float32)
    decay = jnp.exp(-decay_rate[:, None, :] * positions[None, :, None])
    return (jnp.sum(residues[:, None, :] * decay, axis=0), decay, decay_rate, positions)


def modal_grads(kernel_grad, residues, decay, decay_rate, positions):
    weighted = kernel_grad[None] * decay
    residue_part = jnp.sum(weighted, axis=1)
    decay_part = -jnp.sum(weighted * positions[None, :, None], axis=1) * residues * decay_rate
    return (residue_part, decay_part)


def spectral_tables(length):
    padded = 2 * length
    index = lax.iota(jnp.int32, length)
    product = index[:, None] * index[None, :] % padded
    angle = product.astype(jnp.float32) * (2.0 * math.pi / padded)
    cosine = jnp.cos(angle)
    sine = jnp.sin(angle)
    weight = jnp.where(index == 0, 1.0, 2.0).astype(jnp.float32) / padded
    parity = jnp.where(index % 2 == 0, 1.0, -1.0).astype(jnp.float32)
    return (cosine, sine, cosine * weight[None, :], sine * weight[None, :], parity)


def transform(signal, tables):
    highest = lax.Precision.HIGHEST
    real_part = jnp.einsum("ft,btc->bfc", tables[0], signal, precision=highest)
    sine_part = jnp.einsum("ft,btc->bfc", tables[1], signal, precision=highest)
    top_part = jnp.einsum("t,btc->bc", tables[4], signal, precision=highest)
    return (real_part, sine_part, top_part)


def inverse(real_part, sine_part, top_part, tables):
    highest = lax.Precision.HIGHEST
    padded = 2 * real_part.shape[1]
    summed = jnp.einsum("tf,bfc->btc", tables[2], real_part, precision=highest)
    summed = summed + jnp.einsum("tf,bfc->btc", tables[3], sine_part, precision=highest)
    return summed + tables[4][None, :, None] * top_part[:, None, :] / padded


def spectral_core(gated, gate_grad, kernel):
    tables = spectral_tables(kernel.shape[0])
    gated_re, gated_im, gated_top = transform(gated, tables)
    grad_re, grad_im, grad_top = transform(gate_grad, tables)
    kernel_re, kernel_im, kernel_top = transform(kernel[None], tables)
    convolved = inverse(
        gated_re * kernel_re - gated_im * kernel_im,
        gated_re * kernel_im + gated_im * kernel_re,
        gated_top * kernel_top,
        tables,
    )
    gated_grad = inverse(
        kernel_re * grad_re + kernel_im * grad_im,
        kernel_re * grad_im - kernel_im * grad_re,
        kernel_top * grad_top,
        tables,
    )
    cross_re = jnp.sum(gated_re * grad_re + gated_im * grad_im, axis=0)
    cross_im = jnp.sum(gated_re * grad_im - gated_im * grad_re, axis=0)
    cross_top = jnp.sum(gated_top * grad_top, axis=0)
    kernel_grad = inverse(cross_re[None], cross_im[None], cross_top[None], tables)[0]
    return (convolved, gated_grad, kernel_grad)


def body(proj, short_weight, residue, log_decay, cotangent):
    margin = SHORT - 1
    weights, residues, log_rates = (
        lax.all_gather(short_weight, "zero", axis=2, tiled=True),
        lax.all_gather(residue, "zero", axis=1, tiled=True),
        lax.all_gather(log_decay, "zero", axis=1, tiled=True),
    )
    inputs, upstream = (
        lax.all_to_all(proj, "ctx", split_axis=3, concat_axis=1, tiled=True),
        lax.all_to_all(cotangent[:, :, None, :], "ctx", split_axis=3, concat_axis=1, tiled=True),
    )
    length = inputs.shape[1]
    extended = jnp.pad(inputs, ((0, 0), (margin, 0), (0, 0), (0, 0)))
    filtered = taps_forward(extended, weights, length)
    queries = filtered[:, :, 0]
    keys_part = filtered[:, :, 1]
    values = filtered[:, :, 2]
    upstream = upstream[:, :, 0].astype(jnp.float32)
    gated = rounded(keys_part * values)
    gate_grad = rounded(upstream * queries)
    kernel, decay, decay_rate, positions = modal_filter(residues, log_rates, length)
    convolved, gated_grad, kernel_grad = spectral_core(gated, gate_grad, kernel)
    convolved = rounded(convolved)
    gated_grad = rounded(gated_grad)
    outputs = (queries * convolved).astype(jnp.bfloat16)
    filtered_grad = jnp.stack(
        [upstream * convolved, gated_grad * values, gated_grad * keys_part], axis=2
    )
    extended_grad = jnp.pad(filtered_grad, ((0, 0), (0, margin), (0, 0), (0, 0)))
    proj_grad = taps_backward(extended_grad, weights, length).astype(jnp.bfloat16)
    factor = 1.0 / length
    tap_part = taps_weight_grad(filtered_grad, extended, length) * factor
    residue_part, decay_part = modal_grads(
        kernel_grad * factor, residues, decay, decay_rate, positions
    )
    out_rows, grad_rows = (
        lax.all_to_all(outputs[:, :, None, :], "ctx", split_axis=1, concat_axis=3, tiled=True),
        lax.all_to_all(proj_grad, "ctx", split_axis=1, concat_axis=3, tiled=True),
    )
    tap_grad, residue_grad, decay_grad = (
        lax.psum_scatter(tap_part, "zero", scatter_dimension=2, tiled=True),
        lax.psum_scatter(residue_part, "zero", scatter_dimension=1, tiled=True),
        lax.psum_scatter(decay_part, "zero", scatter_dimension=1, tiled=True),
    )
    return (out_rows[:, :, 0, :], grad_rows, tap_grad, residue_grad, decay_grad)


def solution(mesh):
    in_specs = (
        P("zero", "ctx", None, None),
        P(None, None, ("ctx", "zero")),
        P(None, ("ctx", "zero")),
        P(None, ("ctx", "zero")),
        P("zero", "ctx", None),
    )
    out_specs = (
        P("zero", "ctx", None),
        P("zero", "ctx", None, None),
        P(None, None, ("ctx", "zero")),
        P(None, ("ctx", "zero")),
        P(None, ("ctx", "zero")),
    )
    return jax.shard_map(body, mesh=mesh, in_specs=in_specs, out_specs=out_specs, check_vma=False)
```

profile of v0, /device:TPU:1, one launch (start us, length us, event | category | flops | bytes accessed | tf_op | source)
XLA Modules:
  0.0 1953.3 jit_solution(3579354941034634807)
XLA Ops:
  7.2 5.0 copy.90
  12.7 22.4 %reduce.1 = bf16[4096,128]{1,0:T(8,128)(2,1)S(1)} reduce(bf16[4096,1,1,128]{3,2,1,0:T(2,128)(2,1)S(1)} %bitcast.177, bf16[]{:T(256)} %broadcast.279), dimensions={1,2}, to_apply=%bitcast.154.reduce_sub_computation | reduce | bytes 2097154
  36.8 6.4 all-to-all-start.2
  43.2 7.2 copy.80
  50.4 18.1 all-to-all-done.2
  68.4 4.9 all-to-all-start
  73.6 176.1 %all_gather.11 = f32[16,1024]{0,1:T(8,128)S(1)} all-gather(f32[16,16]{0,1:T(8,128)S(1)} %copy.86), channel_id=1, replica_groups=mesh['ctx'=4,'zero'=64] {'zero'}, dimensions={1}, use_global_device_ids=true | all-gather | bytes 66560 | tf_op jit(solution)/shard_map/all_gather | solution.py:112
  249.8 110.6 %all_gather.10 = f32[16,1024]{0,1:T(8,128)S(1)} all-gather(f32[16,16]{0,1:T(8,128)S(1)} %copy.84), channel_id=1, replica_groups=mesh['ctx'=4,'zero'=64] {'zero'}, dimensions={1}, use_global_device_ids=true | all-gather | bytes 66560 | tf_op jit(solution)/shard_map/all_gather | solution.py:111
  360.6 113.8 %all_gather.9 = f32[3,3,1024]{1,0,2:T(4,128)S(1)} all-gather(f32[3,3,16]{1,0,2:T(4,128)S(1)} %copy.78), channel_id=1, replica_groups=mesh['ctx'=4,'zero'=64] {'zero'}, dimensions={2}, use_global_device_ids=true | all-gather | bytes 37440 | tf_op jit(solution)/shard_map/all_gather | solution.py:110
  474.4 4.5 fusion.153
  478.9 2.0 copy.79
  484.7 2.2 bitcast_convert_fusion
  490.2 6.8 copy.110
  497.0 4.0 all_to_all.47
  501.1 4.3 fusion.3
  508.0 6.9 fusion.65
  515.0 7.1 fusion.67
  523.9 6.9 fusion.59
  530.9 7.3 fusion.61
  538.3 7.5 fusion.15
  545.8 9.2 fusion.14
  555.0 2.9 copy.94
  557.9 13.2 multiply_reduce_fusion
  572.2 10.9 fusion.97
  583.1 11.2 fusion.90
  594.4 7.5 fusion.20
  601.9 7.7 fusion.25
  609.6 7.6 fusion.19
  617.3 7.8 fusion.24
  625.2 3.3 convert_multiply_fusion.5
  628.5 2.4 copy.88
  630.9 7.8 reduce.2
  638.6 3.9 reshape.454
  642.5 4.2 all-to-all-start.1
  646.8 6.2 fusion.4
  653.0 5.3 fusion.9
  658.3 5.6 copy.92
  663.9 8.5 all-to-all-done.1
  672.4 4.8 all-to-all-start.3
  677.3 1.9 stack.37
  679.2 3.0 stack.38
  684.0 25.6 %fusion.11 = f32[3,1024]{1,0:T(4,128)S(1)} fusion(f32[1,4,128,1,1024]{2,1,4,3,0:T(4,128)} %stack.38, f32[1,4,128,1,1024]{2,1,4,3,0:T(4,128)} %stack.37, f32[1,4,128,1,1024]{2,1,4,3,0:T(4,128)} %stack.36, bf16[1,128,3,4,1024]{1,2,4,3,0:T(4,128)(2,1)} %bitcast.1), kind=kLoop, calls=%fused_computation.22 | loop fusion | flops 7861248 | bytes 9449472 | tf_op jit(solution)/shard_map/reduce_sum | solution.py:37
  714.2 398.4 %reduce-scatter.10.cloned.1.call-done = f32[16,9]{1,0:T(8,128)} async-done(((f32[1024,9]{1,0:T(8,128)}), f32[16,9]{1,0:T(8,128)}) %reduce-scatter.10.cloned.1.call-update) | async-done | bytes 592
  1114.1 409.9 %reduce-scatter.14.cloned.1.call-done = f32[16,16]{1,0:T(8,128)} async-done(((f32[1024,16]{1,0:T(8,128)}), f32[16,16]{1,0:T(8,128)}) %reduce-scatter.14.cloned.1.call-update) | async-done | bytes 1040
  1525.3 405.5 %reduce-scatter.12.cloned.1.call-done = f32[16,16]{1,0:T(8,128)} async-done(((f32[1024,16]{1,0:T(8,128)}), f32[16,16]{1,0:T(8,128)}) %reduce-scatter.12.cloned.1.call-update) | async-done | bytes 1040
  1932.2 2.8 reshape.455
  1937.4 5.2 copy.93
  1942.6 4.0 all_to_all.55
  (80 shorter events, 28.2 us)
Async XLA Ops:
  36.8 31.7 %all-to-all-start.2 = ((bf16[4,2,65536]{2,1,0:T(2,128)(2,1)}), bf16[4,2,65536]{2,1,0:T(2,128)(2,1)S(1)}, u32[]{:S(2)}, u32[]{:S(2)}) async-start(bf16[4,2,65536]{2,1,0:T(2,128)(2,1)} %reshape.452), calls=%async_computation.2 | async-start | bytes 2097152 | tf_op jit(solution)/shard_map/all_to_all | solution.py:116
  50.4 22.9 %copy-start.13 = (f32[16,16]{1,0:T(8,128)S(1)}, f32[16,16]{1,0:T(8,128)}, u32[]{:S(2)}) copy-start(f32[16,16]{1,0:T(8,128)} %param.7) | copy-start | bytes 3076
  50.4 23.0 %copy-start.14 = (f32[16,16]{1,0:T(8,128)S(1)}, f32[16,16]{1,0:T(8,128)}, u32[]{:S(2)}) copy-start(f32[16,16]{1,0:T(8,128)} %param.8) | copy-start | bytes 3076
  50.4 23.1 %copy-start.15 = (f32[3,3,16]{2,1,0:T(4,128)S(1)}, f32[3,3,16]{2,1,0:T(4,128)}, u32[]{:S(2)}) copy-start(f32[3,3,16]{2,1,0:T(4,128)} %param.6) | copy-start | bytes 1732
  68.4 421.8 %all-to-all-start = ((bf16[1,128,3,4096]{1,2,0,3:T(4,128)(2,1)}), bf16[1,128,3,4096]{1,2,0,3:T(4,128)(2,1)}, u32[]{:S(2)}, u32[]{:S(2)}) async-start(bf16[1,128,3,4096]{1,2,0,3:T(4,128)(2,1)} %copy.80), calls=%async_computation | async-start | bytes 8388608 | tf_op jit(solution)/shard_map/all_to_all | solution.py:115
  501.1 4.3 copy-start.7
  501.1 4.3 copy-start.9
  505.4 2.7 copy-start
  522.1 23.7 %copy-start.1 = (f32[1024,512]{1,0:T(8,128)}, f32[1024,512]{1,0:T(8,128)S(1)}, u32[]{:S(2)}) copy-start(f32[1024,512]{1,0:T(8,128)S(1)} %fusion.67) | copy-start | bytes 6291460
  530.9 14.9 copy-start.3
  538.2 7.6 copy-start.5
  583.1 11.3 copy-start.4
  583.1 11.3 copy-start.6
  594.4 7.5 copy-start.2
  609.6 15.5 slice-start
  617.3 7.9 slice-start.1
  617.3 7.9 copy-start.10
  638.6 8.1 copy-start.8
  642.5 29.9 %all-to-all-start.1 = ((bf16[4,2,65536]{2,1,0:T(2,128)(2,1)}), bf16[4,2,65536]{2,1,0:T(2,128)(2,1)}, u32[]{:S(2)}, u32[]{:S(2)}) async-start(bf16[4,2,65536]{2,1,0:T(2,128)(2,1)} %reshape.454), calls=%async_computation.1 | async-start | bytes 2097152 | tf_op jit(solution)/shard_map/all_to_all | solution.py:143
  663.9 13.4 copy-start.12
  672.4 1265.0 %all-to-all-start.3 = ((bf16[1,512,3,1024]{3,2,0,1:T(4,128)(2,1)}), bf16[1,512,3,1024]{3,2,0,1:T(4,128)(2,1)}, u32[]{:S(2)}, u32[]{:S(2)}) async-start(bf16[1,512,3,1024]{3,2,0,1:T(4,128)(2,1)} %copy.92), calls=%async_computation.3 | async-start | bytes 8388608 | tf_op jit(solution)/shard_map/all_to_all | solution.py:144
  677.2 435.4 %reduce-scatter.10.cloned.1.call-start = ((), (), s32[]{:S(2)}) async-start(), calls=%async_computation.7 | async-start | bytes 532480
  679.2 3.0 copy-start.11
  712.1 811.9 %reduce-scatter.14.cloned.1.call-start = ((), (), s32[]{:S(2)}) async-start(), calls=%async_computation.9 | async-start | bytes 532480
  713.2 1217.7 %reduce-scatter.12.cloned.1.call-start = ((), (), s32[]{:S(2)}) async-start(), calls=%async_computation.8 | async-start | bytes 532480
Sparse Core Ops, SparseCore 0:
  712.2 400.3 reduce-scatter.9
  1115.3 408.6 reduce-scatter.13
  1527.0 403.7 reduce-scatter.11
where the time goes:
time: 1970 us; the launch traced here: 1950 us
  waiting for transfers between devices  1240 us (63%)
  blocking collectives  401 us (20%)
  matrix products  101 us (5%)
  other arithmetic  91.3 us (5%)
  local copies, waits for them, and re-layouts  85.4 us (4%)
  starting transfers between devices  20.5 us (1%)
    unnamed x6, waiting for transfers between devices  1210 us
    all_gather x1, blocking collectives, body(): lax.all_gather(log_decay, 'zero', axis=1, tiled=True)  176 us
    all_gather x1, blocking collectives, body(): lax.all_gather(short_weight, 'zero', axis=2, tiled=True)  114 us
    all_gather x1, blocking collectives, body(): lax.all_gather(residue, 'zero', axis=1, tiled=True)  111 us
  transfers between devices with their start and end apart: 7, of which 5 were waited for; matrix products, arithmetic and copies ran while one was open for 4% of the time, Pallas kernels for 0%

commit v1 on v0

v1 whole, which is shorter than its diff:
```python
import functools

import jax
import jax.numpy as jnp
import ml_dtypes
import numpy as np
from jax import lax
from jax.experimental import pallas as pl
from jax.experimental.pallas import tpu as pltpu
from jax.sharding import PartitionSpec as P

SHORT = 3
ORDER = 16
GROUP = 4
LANES = 128
BF = jnp.bfloat16
F32 = jnp.float32


def split_table(table):
    high = table.astype(ml_dtypes.bfloat16)
    low = (table - high.astype(np.float64)).astype(ml_dtypes.bfloat16)
    return high, low


def tables(chunk):
    padded = 2 * chunk
    index = np.arange(chunk)
    angle = 2.0 * np.pi / padded * (np.outer(index, index) % padded)
    parity = np.where(index % 2 == 0, 1.0, -1.0)
    cosine, sine = np.cos(angle), np.sin(angle)
    sine[0] = parity
    forward = np.concatenate([cosine, sine], 0)
    weight = np.where(index == 0, 1.0, 2.0) / padded
    backward = np.concatenate([cosine * weight[:, None], sine * weight[:, None]], 0).T
    fwd_hi, fwd_lo = split_table(forward)
    inv_hi, inv_lo = split_table(backward)
    fwd2 = np.concatenate([fwd_hi, fwd_lo], 1)
    reverse = np.eye(chunk)[::-1].astype(ml_dtypes.bfloat16)
    rev2 = np.concatenate([reverse, reverse], 1)
    sums = np.kron(np.eye(ORDER), np.ones((1, 8))).astype(np.float32)
    ramp = np.kron(np.eye(ORDER), np.arange(8.0)[None]).astype(np.float32)
    return fwd2, inv_hi, inv_lo, rev2, sums, ramp


def mxu(left, right):
    return jnp.dot(left, right, preferred_element_type=F32)


def exact_dot(left, right):
    return jnp.dot(left, right, preferred_element_type=F32, precision=lax.Precision.HIGHEST)


def halves(values):
    high = values.astype(BF)
    return high, (values - high.astype(F32)).astype(BF)


def down(values, above, offset):
    if offset == 0:
        return values
    rows = values.shape[0]
    return jnp.concatenate([above, values], 0)[8 - offset : 8 - offset + rows]


def up(values, below, offset):
    if offset == 0:
        return values
    rows = values.shape[0]
    return jnp.concatenate([values, below], 0)[offset : offset + rows]


def taps(values, above, weights, which):
    total = weights[3 * which][None] * values
    for offset in range(1, SHORT):
        total = total + weights[3 * which + offset][None] * down(values, above, offset)
    return total


def first_powers(rate):
    steps = lax.broadcasted_iota(jnp.int32, (8, LANES), 0).astype(F32)
    rates = jnp.broadcast_to(rate, (8, LANES))
    return jnp.exp(-rates * steps), jnp.exp(-8.0 * rates)


def moments(par_ref, sources, accs, lanes, tiles):
    for group in range(0, ORDER, GROUP):
        modes = range(group, group + GROUP)
        rates = [jnp.exp(par_ref[ORDER + m : ORDER + m + 1, lanes]) for m in modes]
        powers, steps = map(list, zip(*[first_powers(r) for r in rates]))
        plain = [[None] * GROUP for _ in sources]
        summed = [[None] * GROUP for _ in sources]
        for tile in range(tiles):
            rows = slice(8 * tile, 8 * tile + 8)
            values = [s[rows, lanes] for s in sources]
            for g in range(GROUP):
                for s, value in enumerate(values):
                    term = powers[g] * value
                    if tile == 0:
                        plain[s][g] = term
                        summed[s][g] = term
                    else:
                        plain[s][g] = plain[s][g] + term
                        if tile < tiles - 1:
                            summed[s][g] = summed[s][g] + plain[s][g]
                if tile < tiles - 1:
                    powers[g] = powers[g] * steps[g]
        for s in range(len(sources)):
            for g, m in enumerate(modes):
                accs[2 * s][8 * m : 8 * m + 8, lanes] = plain[s][g]
                accs[2 * s + 1][8 * m : 8 * m + 8, lanes] = summed[s][g]


def finish(sums, ramp, plain, summed, tiles):
    zeroth = exact_dot(sums, plain)
    first = 8.0 * ((tiles - 1.0) * zeroth - exact_dot(sums, summed)) + exact_dot(ramp, plain)
    return zeroth, first


def state_kernel(
    proj, above, cot, par, rev2, sums, ramp, gated_out, grad_out, state_out, send_out, xrev, grads, *accs
):
    chunk, block = cot.shape
    tiles = chunk // 8
    weights = [par[2 * ORDER + i] for i in range(9)]
    filtered = [
        taps(proj[i].astype(F32), above[i].astype(F32), weights, i) for i in range(3)
    ]
    gated = (filtered[1] * filtered[2]).astype(BF)
    gate_grad = (cot[...].astype(F32) * filtered[0]).astype(BF)
    gated_out[...] = gated
    grad_out[...] = gate_grad
    grads[...] = gate_grad.astype(F32)
    xrev[...] = mxu(rev2[:, :chunk], gated)

    @pl.loop(0, block // LANES)
    def _(step):
        lanes = pl.ds(pl.multiple_of(step * LANES, LANES), LANES)
        moments(par, [xrev, grads], accs, lanes, tiles)

    s0, s1 = finish(sums[...], ramp[...], accs[0][...], accs[1][...], tiles)
    p0, p1 = finish(sums[...], ramp[...], accs[2][...], accs[3][...], tiles)
    state_out[0:16] = s0
    state_out[16:32] = s1
    state_out[32:48] = p0
    state_out[48:64] = p1
    send_out[0] = s0.astype(BF)
    send_out[1] = p0.astype(BF)


def local_kernel(
    gated, grad, par, fwd2, inv_hi, inv_lo, sums, ramp, conv_out, back_out, modal_out, kern, corr, *accs
):
    chunk, block = gated.shape
    tiles = chunk // 8

    @pl.loop(0, block // LANES)
    def _(step):
        lanes = pl.ds(pl.multiple_of(step * LANES, LANES), LANES)
        half = ORDER // 2
        for group in (0, half):
            modes = range(group, group + half)
            rates = [jnp.exp(par[ORDER + m : ORDER + m + 1, lanes]) for m in modes]
            powers, steps = map(list, zip(*[first_powers(r) for r in rates]))
            gains = [jnp.broadcast_to(par[m : m + 1, lanes], (8, LANES)) for m in modes]
            powers = [p * g for p, g in zip(powers, gains)]
            for tile in range(tiles):
                rows = slice(8 * tile, 8 * tile + 8)
                parts = list(powers)
                while len(parts) > 1:
                    parts = [a + b for a, b in zip(parts[::2], parts[1::2])]
                total = parts[0]
                if group:
                    total = total + kern[rows, lanes]
                kern[rows, lanes] = total
                powers = [p * s for p, s in zip(powers, steps)]

    def transform(values):
        return mxu(fwd2[...], jnp.concatenate([values, values], 0))

    def inverse(values):
        high, low = halves(values)
        return mxu(inv_hi[...], high) + mxu(inv_hi[...], low) + mxu(inv_lo[...], high)

    x, g = transform(gated[...]), transform(grad[...])
    k_hi, k_lo = halves(kern[...])
    k = transform(k_hi) + mxu(fwd2[:, :chunk], k_lo)
    first = lax.broadcasted_iota(jnp.int32, (chunk, block), 0) == 0

    def product(a, b, sign):
        a_re, a_im, b_re, b_im = a[:chunk], a[chunk:], b[:chunk], b[chunk:]
        both = a_im * b_im
        real = a_re * b_re + jnp.where(first, 0.0, -sign * both)
        imag = jnp.where(first, both, a_re * b_im + sign * (a_im * b_re))
        return jnp.concatenate([real, imag], 0)

    conv_out[...] = inverse(product(k, x, 1.0))
    back_out[...] = inverse(product(k, g, -1.0))
    corr[...] = inverse(product(x, g, -1.0))

    @pl.loop(0, block // LANES)
    def _(step):
        lanes = pl.ds(pl.multiple_of(step * LANES, LANES), LANES)
        moments(par, [corr], accs, lanes, tiles)

    m0, m1 = finish(sums[...], ramp[...], accs[0][...], accs[1][...], tiles)
    modal_out[0:16] = m0
    modal_out[16:32] = m1


def final_kernel(
    proj, above, below, cot, cot_below, par, state, before, after, modal, conv, back, rev2,
    out, proj_grad, grads, conv_x, back_x,
):
    chunk, block = cot.shape
    tiles = chunk // 8
    residue = par[0:ORDER]
    rate = jnp.exp(par[ORDER : 2 * ORDER])
    one = jnp.exp(-rate)
    whole = jnp.exp(-float(chunk) * rate)
    entering = before[0].astype(F32) + whole * (before[1].astype(F32) + whole * before[2].astype(F32))
    leaving = after[0].astype(F32) + whole * (after[1].astype(F32) + whole * after[2].astype(F32))
    s0, s1, p0, p1 = (state[16 * i : 16 * i + 16] for i in range(4))
    grads[0:16] = modal[0:16] + one * p0 * entering
    grads[16:32] = modal[16:32] + one * (
        p1 * entering + s1 * leaving + p0 * entering + chunk * whole * entering * leaving
    )
    in_gain = one * residue * entering
    out_gain = one * residue * leaving
    half = ORDER // 2
    for step in range(block // LANES):
        lanes = slice(step * LANES, step * LANES + LANES)
        for group in (0, half):
            modes = range(group, group + half)
            made = [first_powers(rate[m : m + 1, lanes]) for m in modes]
            powers, steps = map(list, zip(*made))
            gain_x = [jnp.broadcast_to(in_gain[m : m + 1, lanes], (8, LANES)) for m in modes]
            gain_g = [jnp.broadcast_to(out_gain[m : m + 1, lanes], (8, LANES)) for m in modes]
            for tile in range(tiles):
                rows = slice(8 * tile, 8 * tile + 8)
                sum_x = conv[rows, lanes] if group == 0 else conv_x[rows, lanes]
                sum_g = None if group == 0 else back_x[rows, lanes]
                for p, gx, gg in zip(powers, gain_x, gain_g):
                    sum_x = sum_x + gx * p
                    sum_g = gg * p if sum_g is None else sum_g + gg * p
                conv_x[rows, lanes] = sum_x
                back_x[rows, lanes] = sum_g
                if tile < tiles - 1:
                    powers = [p * s for p, s in zip(powers, steps)]

    weights = [par[2 * ORDER + i] for i in range(9)]
    signal = [proj[i].astype(F32) for i in range(3)]
    halo = [above[i].astype(F32) for i in range(3)]
    upstream = cot[...].astype(F32)
    queries, keys, values = (taps(signal[i], halo[i], weights, i) for i in range(3))
    convolved = conv_x[...].astype(BF).astype(F32)
    b_hi, b_lo = halves(back_x[...])
    crossed = mxu(rev2[...], jnp.concatenate([b_hi, b_lo], 0))
    gated_grad = (back[...] + crossed).astype(BF).astype(F32)
    out[...] = (queries * convolved).astype(BF)
    fgrad = [upstream * convolved, gated_grad * values, gated_grad * keys]

    tails = [below[i].astype(F32) for i in range(3)]
    q_r, k_r, v_r = (taps(tails[i], signal[i][chunk - 8 :], weights, i) for i in range(3))
    cot_r = cot_below[...].astype(F32)
    x_r = (k_r * v_r).astype(BF).astype(F32)
    g_r = (cot_r * q_r).astype(BF).astype(F32)
    h0 = one * (whole * entering + s0) + x_r[0:1]
    h1 = one * h0 + x_r[1:2]
    e1 = (leaving - g_r[0:1]) / one
    rows8 = lax.broadcasted_iota(jnp.int32, (8, block), 0)

    def two_rows(a, b):
        a = jnp.sum(residue * a, axis=0, keepdims=True)
        b = jnp.sum(residue * b, axis=0, keepdims=True)
        both = jnp.where(rows8 == 0, a, jnp.where(rows8 == 1, b, 0.0))
        return both.astype(BF).astype(F32)

    conv_r, back_r = two_rows(h0, h1), two_rows(leaving, e1)
    fgrad_r = [cot_r * conv_r, back_r * v_r, back_r * k_r]

    lines = []
    for i in range(3):
        total = weights[3 * i][None] * fgrad[i]
        for offset in range(1, SHORT):
            total = total + weights[3 * i + offset][None] * up(fgrad[i], fgrad_r[i], offset)
        proj_grad[i] = total.astype(BF)
        for offset in range(SHORT):
            moved = down(signal[i], halo[i], offset)
            lines.append(jnp.sum(fgrad[i] * moved, axis=0, keepdims=True))
    for i in range(9):
        grads[2 * ORDER + i : 2 * ORDER + i + 1] = lines[i]


def body(names, proj, short_weight, residue, log_decay, cotangent):
    ctx, devices, n_ctx = names
    chunk, channels = cotangent.shape[1:]
    own = residue.shape[1]
    seq = chunk * n_ctx
    n_dev = channels // own
    rows = 2 * ORDER + 9
    block = 512 if channels % 512 == 0 else channels
    grid = (channels // block,)
    fwd2, inv_hi, inv_lo, rev2, sums, ramp = (jnp.asarray(t) for t in tables(chunk))

    packed = jnp.concatenate([residue, log_decay, short_weight.reshape(9, own)], 0)
    spread = jnp.broadcast_to(packed[None], (n_dev, rows, own))
    gathered = lax.all_to_all(spread, devices, 0, 0, tiled=True)
    par = gathered.transpose(1, 0, 2).reshape(rows, channels)

    signal = proj[0].transpose(1, 0, 2)
    upstream = cotangent[0]
    right = lambda k: [(i, i + k) for i in range(n_ctx - k)]
    left = lambda k: [(i + k, i) for i in range(n_ctx - k)]
    above = lax.ppermute(signal[:, chunk - 8 :], ctx, right(1))
    below = lax.ppermute(signal[:, :8], ctx, left(1))
    cot_below = lax.ppermute(upstream[:8], ctx, left(1))

    def spec(*shape):
        lead = len(shape) - 1
        return pl.BlockSpec(shape[:-1] + (block,), lambda i, lead=lead: (0,) * lead + (i,))

    def fixed(array):
        return pl.BlockSpec(array.shape, lambda i: (0, 0))

    def shape(dims, kind):
        return jax.ShapeDtypeStruct(dims, kind)

    wide = lambda n=chunk: pltpu.VMEM((n, block), F32)
    params = pltpu.CompilerParams(vmem_limit_bytes=48 * 1024 * 1024)
    gated, gate_grad, state, sent = pl.pallas_call(
        state_kernel,
        grid=grid,
        in_specs=[spec(3, chunk, 0), spec(3, 8, 0), spec(chunk, 0), spec(rows, 0)]
        + [fixed(rev2), fixed(sums), fixed(ramp)],
        out_specs=[spec(chunk, 0), spec(chunk, 0), spec(4 * ORDER, 0), spec(2, ORDER, 0)],
        out_shape=[
            shape((chunk, channels), BF),
            shape((chunk, channels), BF),
            shape((4 * ORDER, channels), F32),
            shape((2, ORDER, channels), BF),
        ],
        scratch_shapes=[wide(), wide()] + [wide(8 * ORDER)] * 4,
        compiler_params=params,
        name="states",
    )(signal, above, upstream, par, rev2, sums, ramp)

    before = jnp.stack([lax.ppermute(sent[0], ctx, right(k)) for k in range(1, n_ctx)])
    after = jnp.stack([lax.ppermute(sent[1], ctx, left(k)) for k in range(1, n_ctx)])

    conv, back, modal = pl.pallas_call(
        local_kernel,
        grid=grid,
        in_specs=[spec(chunk, 0), spec(chunk, 0), spec(rows, 0)]
        + [fixed(t) for t in (fwd2, inv_hi, inv_lo, sums, ramp)],
        out_specs=[spec(chunk, 0), spec(chunk, 0), spec(2 * ORDER, 0)],
        out_shape=[
            shape((chunk, channels), F32),
            shape((chunk, channels), F32),
            shape((2 * ORDER, channels), F32),
        ],
        scratch_shapes=[wide(), wide()] + [wide(8 * ORDER)] * 2,
        compiler_params=params,
        name="local",
    )(gated, gate_grad, par, fwd2, inv_hi, inv_lo, sums, ramp)

    out, proj_grad, grads = pl.pallas_call(
        final_kernel,
        grid=grid,
        in_specs=[
            spec(3, chunk, 0), spec(3, 8, 0), spec(3, 8, 0), spec(chunk, 0), spec(8, 0), spec(rows, 0),
            spec(4 * ORDER, 0), spec(n_ctx - 1, ORDER, 0), spec(n_ctx - 1, ORDER, 0),
            spec(2 * ORDER, 0), spec(chunk, 0), spec(chunk, 0), fixed(rev2),
        ],
        out_specs=[spec(chunk, 0), spec(3, chunk, 0), spec(rows, 0)],
        out_shape=[
            shape((chunk, channels), BF),
            shape((3, chunk, channels), BF),
            shape((rows, channels), F32),
        ],
        scratch_shapes=[wide(), wide()],
        compiler_params=params,
        name="final",
    )(signal, above, below, upstream, cot_below, par, state, before, after, modal, conv, back, rev2)

    parts = grads.reshape(rows, n_dev, own).transpose(1, 0, 2)
    arrived = lax.all_to_all(parts, devices, 0, 0, tiled=True)
    total = jnp.sum(arrived, axis=0) * (1.0 / seq)
    residue_grad = total[:ORDER]
    decay_grad = -residue * jnp.exp(log_decay) * total[ORDER : 2 * ORDER]
    tap_grad = total[2 * ORDER :].reshape(3, SHORT, own)
    return (
        out[None],
        proj_grad.transpose(1, 0, 2)[None],
        tap_grad,
        residue_grad,
        decay_grad,
    )


def solution(mesh):
    both = ("ctx", "zero")
    specs = (
        P("zero", "ctx", None, None),
        P(None, None, both),
        P(None, both),
        P(None, both),
        P("zero", "ctx", None),
    )
    out_specs = (specs[4], specs[0], specs[1], specs[2], specs[2])
    names = ("ctx", both, mesh.shape["ctx"])
    return jax.shard_map(
        functools.partial(body, names), mesh=mesh, in_specs=specs, out_specs=out_specs, check_vma=False
    )
```

time: 1970 us -> 195 us (0.10)
  waiting for transfers between devices: 1240 us -> 26.1 us
  blocking collectives: 401 us -> 38.2 us
  matrix products: 101 us -> 0 us
  other arithmetic: 91.3 us -> 5.57 us
  Pallas kernels: 0 us -> 63 us
  local copies, waits for them, and re-layouts: 85.4 us -> 23.5 us
    unnamed x6 -> x0, waiting for transfers between devices: 1210 us -> none
    all_gather x3 -> x0, blocking collectives: 401 us -> none  [the longest x1 176 us: body(): lax.all_gather(log_decay, 'zero', axis=1, tiled=True)]
    dot_general x15 -> x0, matrix products: 101 us -> none  [the longest x3 25.7 us: transform(): real_part = jnp.einsum('ft,btc->bfc', tables[0], signal, precision=highest)]
    pallas_call x0 -> x3, Pallas kernels: none -> 63 us  [the longest x1 22.3 us: body(): pl.pallas_call(local_kernel, grid=grid, in_specs=[spec(chunk, 0), spec(ch...]
    reduce_sum x3 -> x1, other arithmetic: 45.1 us -> 0.28 us  [body(): total = jnp.sum(arrived, axis=0) * (1.0 / seq)]
    all_to_all x0 -> x1, blocking collectives: none -> 38.2 us  [body(): arrived = lax.all_to_all(parts, devices, 0, 0, tiled=True)]
    unnamed x3 -> x0, other arithmetic: 30.1 us -> none
    ppermute x0 -> x9, starting transfers between devices: none -> 21.5 us  [the longest x3 11.6 us: body(): lax.ppermute(sent[0], ctx, right(k))]
  transfers between devices with their start and end apart: 7 -> 10, of which waited for: 5 -> 3; matrix products, arithmetic and copies ran while one was open for 4% -> 5% of each run, Pallas kernels for 0% -> 11%
where the time goes in v1:
time: 195 us; the launch traced here: 194 us
  Pallas kernels  63 us (32%)
  blocking collectives  38.2 us (20%)
  starting transfers between devices  37.2 us (19%)
  waiting for transfers between devices  26.1 us (13%)
  local copies, waits for them, and re-layouts  23.5 us (12%)
  other arithmetic  5.57 us (3%)
    all_to_all x1, blocking collectives, body(): arrived = lax.all_to_all(parts, devices, 0, 0, tiled=True)  38.2 us
    all_to_all x1, waiting for transfers between devices, body(): gathered = lax.all_to_all(spread, devices, 0, 0, tiled=True)  22.7 us
    pallas_call x1, Pallas kernels, body(): pl.pallas_call(local_kernel, grid=grid, in_specs=[spec(chunk, 0), spec(ch...  22.3 us
    pallas_call x1, Pallas kernels, body(): pl.pallas_call(state_kernel, grid=grid, in_specs=[spec(3, chunk, 0), spec...  20.6 us
    pallas_call x1, Pallas kernels, body(): pl.pallas_call(final_kernel, grid=grid, in_specs=[spec(3, chunk, 0), spec...  20 us
    unnamed x25, local copies, waits for them, and re-layouts  16 us
    all_to_all x1, starting transfers between devices, body(): gathered = lax.all_to_all(spread, devices, 0, 0, tiled=True)  15.7 us
    ppermute x3, starting transfers between devices, body(): lax.ppermute(sent[0], ctx, right(k))  11.6 us
  transfers between devices with their start and end apart: 10, of which 3 were waited for; matrix products, arithmetic and copies ran while one was open for 5% of the time, Pallas kernels for 11%

profile of v1, /device:TPU:1, one launch (start us, length us, event | category | flops | bytes accessed | tf_op | source)
XLA Modules:
  0.0 194.4 jit_solution(1397132625340388403)
XLA Ops:
  0.6 0.8 copy.33
  1.4 0.8 copy.34
  2.2 0.7 reshape.24
  2.9 0.1 copy.35
  3.0 0.1 pad_maximum_fusion.2
  3.0 0.1 broadcast_bitcast_fusion
  3.2 3.6 %reshape.28 = f32[256,1,656]{2,1,0:T(1,128)} reshape(f32[256,16,41]{2,1,0:T(8,128)S(1)} %broadcast_bitcast_fusion) | data formatting | bytes 1343488
  6.8 15.7 %all-to-all-start = ((f32[256,1,656]{2,1,0:T(1,128)}), f32[256,1,656]{2,1,0:T(1,128)S(1)}, u32[]{:S(2)}, u32[]{:S(2)}) async-start(f32[256,1,656]{2,1,0:T(1,128)} %reshape.28), calls=%async_computation | async-start | bytes 1572864 | tf_op jit(solution)/shard_map/all_to_all | solution.py:308
  22.5 1.1 fusion
  23.5 3.4 %collective-permute-start = (bf16[3,8,4096]{2,1,0:T(8,128)(2,1)S(1)}, bf16[3,8,4096]{2,1,0:T(8,128)(2,1)S(1)}, u32[]{:S(2)}, u32[]{:S(2)}) collective-permute-start(bf16[3,8,4096]{2,1,0:T(8,128)(2,1)S(1)} %get-tuple-element.36), channel_id=1, source_target_pairs={{0,64},{64,128},{128,192},{1,65},{65,129},{129,193},{2,66},{66,130... | collective-permute-start | bytes 589832 | tf_op jit(solution)/shard_map/ppermute | solution.py:315
  27.0 22.7 %all-to-all-done = f32[256,1,656]{2,1,0:T(1,128)S(1)} async-done(((f32[256,1,656]{2,1,0:T(1,128)}), f32[256,1,656]{2,1,0:T(1,128)S(1)}, u32[]{:S(2)}, u32[]{:S(2)}) %all-to-all-start) | async-done | bytes 671776 | tf_op jit(solution)/shard_map/all_to_all | solution.py:308
  49.6 0.5 broadcast.1
  50.1 2.5 %reduce = f32[256,656]{1,0:T(8,128)S(1)} reduce(f32[256,1,656]{2,1,0:T(1,128)S(1)} %all-to-all-done, f32[]{:T(128)} %broadcast.1), dimensions={1}, to_apply=%all_to_all.6.reduce_sub_computation | reduce | bytes 1343492 | tf_op jit(solution)/shard_map/all_to_all | solution.py:308
  52.7 2.8 %reshape.29 = f32[256,16,41]{2,1,0:T(8,128)} reshape(f32[256,656]{1,0:T(8,128)S(1)} %reduce) | data formatting | bytes 1343488
  55.5 2.3 %copy.38.par = f32[41,4096]{1,0:T(8,128)S(1)} copy(f32[41,4096]{0,1:T(8,128)} %bitcast.37) | data formatting | bytes 1343488 | tf_op jit(solution)/shard_map/reshape | solution.py:309
  57.9 0.0 collective-permute-done.above
  57.9 0.0 copy-start.3
  57.9 0.0 copy-start.4
  57.9 0.0 copy-start.5
  57.9 20.6 %states.1 = (bf16[128,4096]{1,0:T(8,128)(2,1)S(1)}, bf16[128,4096]{1,0:T(8,128)(2,1)S(1)}, f32[64,4096]{1,0:T(8,128)S(1)}, bf16[2,16,4096]{2,1,0:T(8,128)(2,1)S(1)}) custom-call(bf16[3,128,4096]{2,1,0:T(8,128)(2,1)} %bitcast.35, bf16[3,8,4096]{2,1,0:T(8,128)(2,1)S(1)} %collective-permute-done.above, bf16[128,4096]{1,0:T(8,128)(2,1)S(1)} %bitcast.32, ...), custom_call_target="tpu_custom_call" | custom-call | tf_op jit(solution)/shard_map/states/pallas_call | solution.py:331
  78.6 1.3 collective-permute-start.8
  79.9 1.3 collective-permute-start.7
  81.2 1.3 collective-permute-start.6
  82.5 1.3 collective-permute-start.2
  83.8 1.3 collective-permute-start.1
  85.2 22.3 %local.1 = (f32[128,4096]{1,0:T(8,128)S(1)}, f32[128,4096]{1,0:T(8,128)}, f32[32,4096]{1,0:T(8,128)S(1)}) custom-call(bf16[128,4096]{1,0:T(8,128)(2,1)S(1)} %get-tuple-element.17.gated, bf16[128,4096]{1,0:T(8,128)(2,1)S(1)} %get-tuple-element.18.grad, f32[41,4096]{1,0:T(8,128)S(1)} %copy.38.par, bf16[256,256]{1,0:T(8,128)(2,1)S(1)} %copy-done.3, ...), custom_call_target="tpu_custom_call" | custom-call | tf_op jit(solution)/shard_map/local/pallas_call | solution.py:351
  107.5 1.3 copy-done.1
  108.8 0.0 collective-permute-done.8
  108.8 7.9 %collective-permute-start.5 = (bf16[16,4096]{1,0:T(8,128)(2,1)S(1)}, bf16[16,4096]{1,0:T(8,128)(2,1)S(1)}, u32[]{:S(2)}, u32[]{:S(2)}) collective-permute-start(bf16[16,4096]{1,0:T(8,128)(2,1)S(1)} %get-tuple-element.38), channel_id=1, source_target_pairs={{0,192},{1,193},{2,194},{3,195},{4,196},{5,197},{6,198},{7,199},{8... | collective-permute-start | bytes 393224 | tf_op jit(solution)/shard_map/ppermute | solution.py:348
  116.8 0.0 collective-permute-done.7
  116.8 1.3 collective-permute-start.4
  118.1 2.4 %collective-permute-start.3 = (bf16[16,4096]{1,0:T(8,128)(2,1)S(1)}, bf16[16,4096]{1,0:T(8,128)(2,1)S(1)}, u32[]{:S(2)}, u32[]{:S(2)}) collective-permute-start(bf16[16,4096]{1,0:T(8,128)(2,1)S(1)} %get-tuple-element.38), channel_id=1, source_target_pairs={{0,64},{64,128},{128,192},{1,65},{65,129},{129,193},{2,66},{66,130... | collective-permute-start | bytes 393224 | tf_op jit(solution)/shard_map/ppermute | solution.py:348
  120.6 0.0 collective-permute-done.5
  120.6 0.7 collective-permute-done.4
  121.2 2.8 %collective-permute-done.3 = bf16[16,4096]{1,0:T(8,128)(2,1)S(1)} collective-permute-done((bf16[16,4096]{1,0:T(8,128)(2,1)S(1)}, bf16[16,4096]{1,0:T(8,128)(2,1)S(1)}, u32[]{:S(2)}, u32[]{:S(2)}) %collective-permute-start.3) | collective-permute-done | bytes 131104 | tf_op jit(solution)/shard_map/ppermute | solution.py:348
  124.1 20.0 %final.1 = (bf16[128,4096]{1,0:T(8,128)(2,1)}, bf16[3,128,4096]{2,1,0:T(8,128)(2,1)}, f32[41,4096]{1,0:T(8,128)S(1)}) custom-call(bf16[3,128,4096]{2,1,0:T(8,128)(2,1)} %bitcast.36, bf16[3,8,4096]{2,1,0:T(8,128)(2,1)S(1)} %collective-permute-done.above, bf16[3,8,4096]{2,1,0:T(8,128)(2,1)S(1)} %collective-permute-done.1.below, ...), custom_call_target="tpu_custom_call" | custom-call | tf_op jit(solution)/shard_map/final/pallas_call | solution.py:367
  144.1 2.0 %copy.39 = f32[41,4096]{0,1:T(8,128)} copy(f32[41,4096]{1,0:T(8,128)S(1)} %get-tuple-element.24) | data formatting | bytes 1343488 | tf_op jit(solution)/shard_map/final/pallas_call | solution.py:367
  146.1 3.6 %reshape.30 = f32[256,1,656]{2,1,0:T(1,128)S(1)} reshape(f32[256,16,41]{2,1,0:T(8,128)} %bitcast.38) | data formatting | bytes 1343488
  149.7 38.2 %all_to_all.10 = f32[256,1,656]{2,1,0:T(1,128)S(1)} all-to-all(f32[256,1,656]{2,1,0:T(1,128)S(1)} %reshape.30), channel_id=1, replica_groups=mesh['ctx'=4,'zero'=64] {'ctx','zero'}, dimensions={0} | all-to-all | bytes 1343488 | tf_op jit(solution)/shard_map/all_to_all | solution.py:387
  187.9 2.5 %reduce.1 = f32[256,656]{1,0:T(8,128)S(1)} reduce(f32[256,1,656]{2,1,0:T(1,128)S(1)} %all_to_all.10, f32[]{:T(128)} %broadcast.1), dimensions={1}, to_apply=%all_to_all.7.reduce_sub_computation | reduce | bytes 1343492 | tf_op jit(solution)/shard_map/all_to_all | solution.py:387
  190.4 1.5 reshape.31
  192.0 0.3 bitcast_reduce_fusion
  192.3 0.1 slice_multiply_fusion
  192.3 0.1 slice.42
  192.4 0.1 copy.40
  192.5 0.6 reshape.27
  193.1 0.7 copy.44
  193.8 0.7 copy.43
  (20 shorter events, 0.2 us)
Async XLA Ops:
  6.8 42.8 %all-to-all-start = ((f32[256,1,656]{2,1,0:T(1,128)}), f32[256,1,656]{2,1,0:T(1,128)S(1)}, u32[]{:S(2)}, u32[]{:S(2)}) async-start(f32[256,1,656]{2,1,0:T(1,128)} %reshape.28), calls=%async_computation | async-start | bytes 1572864 | tf_op jit(solution)/shard_map/all_to_all | solution.py:308
  23.5 34.3 %collective-permute-start = (bf16[3,8,4096]{2,1,0:T(8,128)(2,1)S(1)}, bf16[3,8,4096]{2,1,0:T(8,128)(2,1)S(1)}, u32[]{:S(2)}, u32[]{:S(2)}) collective-permute-start(bf16[3,8,4096]{2,1,0:T(8,128)(2,1)S(1)} %get-tuple-element.36), channel_id=1, source_target_pairs={{0,64},{64,128},{128,192},{1,65},{65,129},{129,193},{2,66},{66,130... | collective-permute-start | bytes 589832 | tf_op jit(solution)/shard_map/ppermute | solution.py:315
  55.5 2.3 %copy-start = (bf16[1,128,4096]{2,1,0:T(8,128)(2,1)S(1)}, bf16[1,128,4096]{2,1,0:T(8,128)(2,1)}, u32[]{:S(2)}) copy-start(bf16[1,128,4096]{2,1,0:T(8,128)(2,1)} %param.15) | copy-start | bytes 3145732
  55.5 2.4 %copy-start.2 = (bf16[128,256]{1,0:T(8,128)(2,1)S(1)}, bf16[128,256]{1,0:T(8,128)(2,1)}, u32[]{:S(2)}) copy-start(bf16[128,256]{1,0:T(8,128)(2,1)} %constant.19.clone.rev2) | copy-start | bytes 196612
  55.5 2.4 %copy-start.6 = (f32[16,128]{1,0:T(8,128)S(1)}, f32[16,128]{1,0:T(8,128)}, u32[]{:S(2)}) copy-start(f32[16,128]{1,0:T(8,128)} %constant.21.clone.ramp) | copy-start | bytes 24580
  55.5 2.4 %copy-start.7 = (f32[16,128]{1,0:T(8,128)S(1)}, f32[16,128]{1,0:T(8,128)}, u32[]{:S(2)}) copy-start(f32[16,128]{1,0:T(8,128)} %constant.20.clone.sums) | copy-start | bytes 24580
  57.9 27.2 %copy-start.3 = (bf16[256,256]{1,0:T(8,128)(2,1)S(1)}, bf16[256,256]{1,0:T(8,128)(2,1)}, u32[]{:S(2)}) copy-start(bf16[256,256]{1,0:T(8,128)(2,1)} %constant.16.clone.fwd2) | copy-start | bytes 393220
  57.9 27.2 %copy-start.4 = (bf16[128,256]{1,0:T(8,128)(2,1)S(1)}, bf16[128,256]{1,0:T(8,128)(2,1)}, u32[]{:S(2)}) copy-start(bf16[128,256]{1,0:T(8,128)(2,1)} %constant.18.clone.inv_lo) | copy-start | bytes 196612
  57.9 27.2 %copy-start.5 = (bf16[128,256]{1,0:T(8,128)(2,1)S(1)}, bf16[128,256]{1,0:T(8,128)(2,1)}, u32[]{:S(2)}) copy-start(bf16[128,256]{1,0:T(8,128)(2,1)} %constant.17.clone.inv_hi) | copy-start | bytes 196612
  78.6 30.2 %collective-permute-start.8 = (bf16[16,4096]{1,0:T(8,128)(2,1)S(1)}, bf16[16,4096]{1,0:T(8,128)(2,1)S(1)}, u32[]{:S(2)}, u32[]{:S(2)}) collective-permute-start(bf16[16,4096]{1,0:T(8,128)(2,1)S(1)} %get-tuple-element.37), channel_id=1, source_target_pairs={{192,0},{193,1},{194,2},{195,3},{196,4},{197,5},{198,6},{199,7},{2... | collective-permute-start | bytes 393224 | tf_op jit(solution)/shard_map/ppermute | solution.py:349
  79.9 36.9 %collective-permute-start.7 = (bf16[16,4096]{1,0:T(8,128)(2,1)S(1)}, bf16[16,4096]{1,0:T(8,128)(2,1)S(1)}, u32[]{:S(2)}, u32[]{:S(2)}) collective-permute-start(bf16[16,4096]{1,0:T(8,128)(2,1)S(1)} %get-tuple-element.37), channel_id=1, source_target_pairs={{128,0},{192,64},{129,1},{193,65},{130,2},{194,66},{131,3},{195,67... | collective-permute-start | bytes 393224 | tf_op jit(solution)/shard_map/ppermute | solution.py:349
  81.2 36.9 %collective-permute-start.6 = (bf16[16,4096]{1,0:T(8,128)(2,1)S(1)}, bf16[16,4096]{1,0:T(8,128)(2,1)S(1)}, u32[]{:S(2)}, u32[]{:S(2)}) collective-permute-start(bf16[16,4096]{1,0:T(8,128)(2,1)S(1)} %get-tuple-element.37), channel_id=1, source_target_pairs={{64,0},{128,64},{192,128},{65,1},{129,65},{193,129},{66,2},{130,66... | collective-permute-start | bytes 393224 | tf_op jit(solution)/shard_map/ppermute | solution.py:349
  82.5 41.5 %collective-permute-start.2 = (bf16[8,4096]{1,0:T(8,128)(2,1)S(1)}, bf16[8,4096]{1,0:T(8,128)(2,1)S(1)}, u32[]{:S(2)}, u32[]{:S(2)}) collective-permute-start(bf16[8,4096]{1,0:T(8,128)(2,1)S(1)} %slice_bitcast_fusion.2), channel_id=1, source_target_pairs={{64,0},{128,64},{192,128},{65,1},{129,65},{193,129},{66,2},{130,66... | collective-permute-start | bytes 196616 | tf_op jit(solution)/shard_map/ppermute | solution.py:317
  83.8 40.3 %collective-permute-start.1 = (bf16[3,8,4096]{2,1,0:T(8,128)(2,1)S(1)}, bf16[3,8,4096]{2,1,0:T(8,128)(2,1)S(1)}, u32[]{:S(2)}, u32[]{:S(2)}) collective-permute-start(bf16[3,8,4096]{2,1,0:T(8,128)(2,1)S(1)} %get-tuple-element.35), channel_id=1, source_target_pairs={{64,0},{128,64},{192,128},{65,1},{129,65},{193,129},{66,2},{130,66... | collective-permute-start | bytes 589832 | tf_op jit(solution)/shard_map/ppermute | solution.py:316
  107.5 1.3 copy-start.1
  108.8 11.7 %collective-permute-start.5 = (bf16[16,4096]{1,0:T(8,128)(2,1)S(1)}, bf16[16,4096]{1,0:T(8,128)(2,1)S(1)}, u32[]{:S(2)}, u32[]{:S(2)}) collective-permute-start(bf16[16,4096]{1,0:T(8,128)(2,1)S(1)} %get-tuple-element.38), channel_id=1, source_target_pairs={{0,192},{1,193},{2,194},{3,195},{4,196},{5,197},{6,198},{7,199},{8... | collective-permute-start | bytes 393224 | tf_op jit(solution)/shard_map/ppermute | solution.py:348
  116.8 4.4 %collective-permute-start.4 = (bf16[16,4096]{1,0:T(8,128)(2,1)S(1)}, bf16[16,4096]{1,0:T(8,128)(2,1)S(1)}, u32[]{:S(2)}, u32[]{:S(2)}) collective-permute-start(bf16[16,4096]{1,0:T(8,128)(2,1)S(1)} %get-tuple-element.38), channel_id=1, source_target_pairs={{0,128},{64,192},{1,129},{65,193},{2,130},{66,194},{3,131},{67,195... | collective-permute-start | bytes 393224 | tf_op jit(solution)/shard_map/ppermute | solution.py:348
  118.1 5.9 %collective-permute-start.3 = (bf16[16,4096]{1,0:T(8,128)(2,1)S(1)}, bf16[16,4096]{1,0:T(8,128)(2,1)S(1)}, u32[]{:S(2)}, u32[]{:S(2)}) collective-permute-start(bf16[16,4096]{1,0:T(8,128)(2,1)S(1)} %get-tuple-element.38), channel_id=1, source_target_pairs={{0,64},{64,128},{128,192},{1,65},{65,129},{129,193},{2,66},{66,130... | collective-permute-start | bytes 393224 | tf_op jit(solution)/shard_map/ppermute | solution.py:348

commit v2 on v1

--- a/solution.py
+++ b/solution.py
@@ -11,7 +11,8 @@
 
 SHORT = 3
 ORDER = 16
-GROUP = 4
+WIRE = 16
+WIRE_ROWS = 72
 LANES = 128
 BF = jnp.bfloat16
 F32 = jnp.float32
@@ -38,17 +39,19 @@
     fwd2 = np.concatenate([fwd_hi, fwd_lo], 1)
     reverse = np.eye(chunk)[::-1].astype(ml_dtypes.bfloat16)
     rev2 = np.concatenate([reverse, reverse], 1)
-    sums = np.kron(np.eye(ORDER), np.ones((1, 8))).astype(np.float32)
-    ramp = np.kron(np.eye(ORDER), np.arange(8.0)[None]).astype(np.float32)
-    return fwd2, inv_hi, inv_lo, rev2, sums, ramp
+    inv2 = np.concatenate([inv_hi, inv_lo], 0)
+    return fwd2, inv2, rev2
 
 
 def mxu(left, right):
     return jnp.dot(left, right, preferred_element_type=F32)
 
 
-def exact_dot(left, right):
-    return jnp.dot(left, right, preferred_element_type=F32, precision=lax.Precision.HIGHEST)
+def tree(parts):
+    parts = list(parts)
+    while len(parts) > 1:
+        parts = [a + b for a, b in zip(parts[::2], parts[1::2])]
+    return parts[0]
 
 
 def halves(values):
@@ -83,17 +86,45 @@
     return jnp.exp(-rates * steps), jnp.exp(-8.0 * rates)
 
 
-def moments(par_ref, sources, accs, lanes, tiles):
-    for group in range(0, ORDER, GROUP):
-        modes = range(group, group + GROUP)
-        rates = [jnp.exp(par_ref[ORDER + m : ORDER + m + 1, lanes]) for m in modes]
+def fold(values):
+    row = lax.broadcasted_iota(jnp.int32, (8, LANES), 0)
+    for bit in (4, 2, 1):
+        low = (row & bit) == 0
+        made = []
+        for one, two in zip(values[:bit], values[bit:]):
+            kept = jnp.where(low, one, two)
+            other = jnp.where(low, two, one)
+            if bit == 4:
+                moved = pltpu.roll(other, 4, 0)
+            else:
+                moved = jnp.where(low, pltpu.roll(other, 8 - bit, 0), pltpu.roll(other, bit, 0))
+            made.append(kept + moved)
+        values = made
+    return values[0]
+
+
+def swap_blocks(tile):
+    row = lax.broadcasted_iota(jnp.int32, (8, LANES), 0)
+    column = lax.broadcasted_iota(jnp.int32, (8, LANES), 1) // WIRE
+    for bit in (1, 2, 4):
+        row_bit, column_bit = row & bit, column & bit
+        ahead = pltpu.roll(pltpu.roll(tile, 8 - bit, 0), WIRE * bit, 1)
+        back = pltpu.roll(pltpu.roll(tile, bit, 0), LANES - WIRE * bit, 1)
+        tile = jnp.where(row_bit == column_bit, tile, jnp.where(row_bit < column_bit, ahead, back))
+    return tile
+
+
+def moments(par_ref, sources, outs, lanes, tiles):
+    place = lax.broadcasted_iota(jnp.int32, (8, LANES), 0).astype(F32) + 8.0 * (tiles - 1)
+    for group in range(0, ORDER, 8):
+        rates = [jnp.exp(par_ref[ORDER + m : ORDER + m + 1, lanes]) for m in range(group, group + 8)]
         powers, steps = map(list, zip(*[first_powers(r) for r in rates]))
-        plain = [[None] * GROUP for _ in sources]
-        summed = [[None] * GROUP for _ in sources]
+        plain = [[None] * 8 for _ in sources]
+        summed = [[None] * 8 for _ in sources]
         for tile in range(tiles):
             rows = slice(8 * tile, 8 * tile + 8)
             values = [s[rows, lanes] for s in sources]
-            for g in range(GROUP):
+            for g in range(8):
                 for s, value in enumerate(values):
                     term = powers[g] * value
                     if tile == 0:
@@ -105,23 +136,30 @@
                             summed[s][g] = summed[s][g] + plain[s][g]
                 if tile < tiles - 1:
                     powers[g] = powers[g] * steps[g]
-        for s in range(len(sources)):
-            for g, m in enumerate(modes):
-                accs[2 * s][8 * m : 8 * m + 8, lanes] = plain[s][g]
-                accs[2 * s + 1][8 * m : 8 * m + 8, lanes] = summed[s][g]
-
-
-def finish(sums, ramp, plain, summed, tiles):
-    zeroth = exact_dot(sums, plain)
-    first = 8.0 * ((tiles - 1.0) * zeroth - exact_dot(sums, summed)) + exact_dot(ramp, plain)
-    return zeroth, first
+        for s, (ref, first_row) in enumerate(outs):
+            ref[first_row + group : first_row + group + 8, lanes] = fold(plain[s])
+            weighted = [place * p - 8.0 * q for p, q in zip(plain[s], summed[s])]
+            ref[first_row + ORDER + group : first_row + ORDER + group + 8, lanes] = fold(weighted)
 
 
 def state_kernel(
-    proj, above, cot, par, rev2, sums, ramp, gated_out, grad_out, state_out, send_out, xrev, grads, *accs
+    where, proj, above, cot, wire, rev2, gated_out, grad_out, par, state_out, send1, send2, send3, xrev, grads
 ):
     chunk, block = cot.shape
     tiles = chunk // 8
+    arrived = wire[...].astype(F32)
+    for group in range(block // LANES):
+        lanes = slice(group * LANES, group * LANES + LANES)
+        parts = [
+            swap_blocks(arrived[8 * group : 8 * group + 8, q * LANES : q * LANES + LANES])
+            for q in range(WIRE_ROWS // 8)
+        ]
+        par[0:8, lanes] = parts[4]
+        par[8:16, lanes] = parts[5]
+        par[16:24, lanes] = parts[0] + parts[2]
+        par[24:32, lanes] = parts[1] + parts[3]
+        par[32:40, lanes] = parts[6] + parts[8]
+        par[40:48, lanes] = jnp.broadcast_to(parts[7][0:1] + parts[7][1:2], (8, LANES))
     weights = [par[2 * ORDER + i] for i in range(9)]
     filtered = [
         taps(proj[i].astype(F32), above[i].astype(F32), weights, i) for i in range(3)
@@ -136,20 +174,15 @@
     @pl.loop(0, block // LANES)
     def _(step):
         lanes = pl.ds(pl.multiple_of(step * LANES, LANES), LANES)
-        moments(par, [xrev, grads], accs, lanes, tiles)
-
-    s0, s1 = finish(sums[...], ramp[...], accs[0][...], accs[1][...], tiles)
-    p0, p1 = finish(sums[...], ramp[...], accs[2][...], accs[3][...], tiles)
-    state_out[0:16] = s0
-    state_out[16:32] = s1
-    state_out[32:48] = p0
-    state_out[48:64] = p1
-    send_out[0] = s0.astype(BF)
-    send_out[1] = p0.astype(BF)
+        moments(par, [xrev, grads], [(state_out, 0), (state_out, 32)], lanes, tiles)
+
+    forward, backward = state_out[0:16], state_out[32:48]
+    for away, send in zip((1, 2, 3), (send1, send2, send3)):
+        send[...] = jnp.where(where[0] + away < 4, forward, backward).astype(BF)
 
 
 def local_kernel(
-    gated, grad, par, fwd2, inv_hi, inv_lo, sums, ramp, conv_out, back_out, modal_out, kern, corr, *accs
+    gated, grad, par, fwd2, inv2, conv_out, back_out, modal_out, kern, corr
 ):
     chunk, block = gated.shape
     tiles = chunk // 8
@@ -166,10 +199,7 @@
             powers = [p * g for p, g in zip(powers, gains)]
             for tile in range(tiles):
                 rows = slice(8 * tile, 8 * tile + 8)
-                parts = list(powers)
-                while len(parts) > 1:
-                    parts = [a + b for a, b in zip(parts[::2], parts[1::2])]
-                total = parts[0]
+                total = tree(powers)
                 if group:
                     total = total + kern[rows, lanes]
                 kern[rows, lanes] = total
@@ -180,7 +210,8 @@
 
     def inverse(values):
         high, low = halves(values)
-        return mxu(inv_hi[...], high) + mxu(inv_hi[...], low) + mxu(inv_lo[...], high)
+        both = mxu(inv2[...], high)
+        return both[:chunk] + both[chunk:] + mxu(inv2[:chunk], low)
 
     x, g = transform(gated[...]), transform(grad[...])
     k_hi, k_lo = halves(kern[...])
@@ -201,16 +232,12 @@
     @pl.loop(0, block // LANES)
     def _(step):
         lanes = pl.ds(pl.multiple_of(step * LANES, LANES), LANES)
-        moments(par, [corr], accs, lanes, tiles)
-
-    m0, m1 = finish(sums[...], ramp[...], accs[0][...], accs[1][...], tiles)
-    modal_out[0:16] = m0
-    modal_out[16:32] = m1
+        moments(par, [corr], [(modal_out, 0)], lanes, tiles)
 
 
 def final_kernel(
-    proj, above, below, cot, cot_below, par, state, before, after, modal, conv, back, rev2,
-    out, proj_grad, grads, conv_x, back_x,
+    where, proj, above, below, cot, par, state, got1, got2, got3, modal, conv, back, rev2,
+    out, proj_grad, sums_out, conv_x, back_x, grads,
 ):
     chunk, block = cot.shape
     tiles = chunk // 8
@@ -218,8 +245,13 @@
     rate = jnp.exp(par[ORDER : 2 * ORDER])
     one = jnp.exp(-rate)
     whole = jnp.exp(-float(chunk) * rate)
-    entering = before[0].astype(F32) + whole * (before[1].astype(F32) + whole * before[2].astype(F32))
-    leaving = after[0].astype(F32) + whole * (after[1].astype(F32) + whole * after[2].astype(F32))
+    entering = jnp.zeros_like(rate)
+    leaving = jnp.zeros_like(rate)
+    scales = [jnp.ones_like(rate), whole, whole * whole]
+    for away, got in zip((1, 2, 3), (got1, got2, got3)):
+        state_got = got[...].astype(F32)
+        entering = entering + jnp.where(where[0] >= away, scales[away - 1] * state_got, 0.0)
+        leaving = leaving + jnp.where(where[0] < away, scales[3 - away] * state_got, 0.0)
     s0, s1, p0, p1 = (state[16 * i : 16 * i + 16] for i in range(4))
     grads[0:16] = modal[0:16] + one * p0 * entering
     grads[16:32] = modal[16:32] + one * (
@@ -240,11 +272,10 @@
                 rows = slice(8 * tile, 8 * tile + 8)
                 sum_x = conv[rows, lanes] if group == 0 else conv_x[rows, lanes]
                 sum_g = None if group == 0 else back_x[rows, lanes]
-                for p, gx, gg in zip(powers, gain_x, gain_g):
-                    sum_x = sum_x + gx * p
-                    sum_g = gg * p if sum_g is None else sum_g + gg * p
-                conv_x[rows, lanes] = sum_x
-                back_x[rows, lanes] = sum_g
+                new_x = tree([gx * p for p, gx in zip(powers, gain_x)])
+                new_g = tree([gg * p for p, gg in zip(powers, gain_g)])
+                conv_x[rows, lanes] = sum_x + new_x
+                back_x[rows, lanes] = new_g if sum_g is None else sum_g + new_g
                 if tile < tiles - 1:
                     powers = [p * s for p, s in zip(powers, steps)]
 
@@ -262,7 +293,7 @@
 
     tails = [below[i].astype(F32) for i in range(3)]
     q_r, k_r, v_r = (taps(tails[i], signal[i][chunk - 8 :], weights, i) for i in range(3))
-    cot_r = cot_below[...].astype(F32)
+    cot_r = below[3].astype(F32)
     x_r = (k_r * v_r).astype(BF).astype(F32)
     g_r = (cot_r * q_r).astype(BF).astype(F32)
     h0 = one * (whole * entering + s0) + x_r[0:1]
@@ -290,6 +321,14 @@
             lines.append(jnp.sum(fgrad[i] * moved, axis=0, keepdims=True))
     for i in range(9):
         grads[2 * ORDER + i : 2 * ORDER + i + 1] = lines[i]
+    grads[2 * ORDER + 9 :] = jnp.zeros((7, block), F32)
+    rows_out = []
+    for group in range(block // LANES):
+        lanes = slice(group * LANES, group * LANES + LANES)
+        rows_out.append(
+            jnp.concatenate([swap_blocks(grads[8 * q : 8 * q + 8, lanes]) for q in range(6)], 1)
+        )
+    sums_out[...] = jnp.concatenate(rows_out, 0).astype(BF)
 
 
 def body(names, proj, short_weight, residue, log_decay, cotangent):
@@ -298,97 +337,112 @@
     own = residue.shape[1]
     seq = chunk * n_ctx
     n_dev = channels // own
-    rows = 2 * ORDER + 9
     block = 512 if channels % 512 == 0 else channels
     grid = (channels // block,)
-    fwd2, inv_hi, inv_lo, rev2, sums, ramp = (jnp.asarray(t) for t in tables(chunk))
-
-    packed = jnp.concatenate([residue, log_decay, short_weight.reshape(9, own)], 0)
-    spread = jnp.broadcast_to(packed[None], (n_dev, rows, own))
-    gathered = lax.all_to_all(spread, devices, 0, 0, tiled=True)
-    par = gathered.transpose(1, 0, 2).reshape(rows, channels)
+    fwd2, inv2, rev2 = (jnp.asarray(t) for t in tables(chunk))
+    where = lax.axis_index(ctx).astype(jnp.int32).reshape(1)
+
+    weights = short_weight.reshape(9, own)
+    exact = jnp.concatenate([log_decay, weights], 0)
+    high = lax.optimization_barrier(exact.astype(BF))
+    low = (exact - high.astype(F32)).astype(BF)
+    packed = jnp.concatenate(
+        [
+            high[:16], low[:16], residue.astype(BF), high[16:24],
+            high[24:], low[24:], jnp.zeros((6, own), BF), low[16:24],
+        ],
+        0,
+    ).reshape(1, WIRE_ROWS * own)
+    spread = jnp.broadcast_to(packed, (n_dev, WIRE_ROWS * own))
+    wire = lax.all_to_all(spread, devices, 0, 0, tiled=True)
 
     signal = proj[0].transpose(1, 0, 2)
     upstream = cotangent[0]
-    right = lambda k: [(i, i + k) for i in range(n_ctx - k)]
-    left = lambda k: [(i + k, i) for i in range(n_ctx - k)]
-    above = lax.ppermute(signal[:, chunk - 8 :], ctx, right(1))
-    below = lax.ppermute(signal[:, :8], ctx, left(1))
-    cot_below = lax.ppermute(upstream[:8], ctx, left(1))
+    right = [(i, i + 1) for i in range(n_ctx - 1)]
+    left = [(i + 1, i) for i in range(n_ctx - 1)]
+    above = lax.ppermute(signal[:, chunk - 8 :], ctx, right)
+    below = lax.ppermute(jnp.concatenate([signal[:, :8], upstream[None, :8]], 0), ctx, left)
 
     def spec(*shape):
         lead = len(shape) - 1
         return pl.BlockSpec(shape[:-1] + (block,), lambda i, lead=lead: (0,) * lead + (i,))
 
+    def rows(count):
+        return pl.BlockSpec((block // own, count), lambda i: (i, 0))
+
     def fixed(array):
         return pl.BlockSpec(array.shape, lambda i: (0, 0))
 
     def shape(dims, kind):
         return jax.ShapeDtypeStruct(dims, kind)
 
+    scalar = pl.BlockSpec(memory_space=pltpu.SMEM)
     wide = lambda n=chunk: pltpu.VMEM((n, block), F32)
     params = pltpu.CompilerParams(vmem_limit_bytes=48 * 1024 * 1024)
-    gated, gate_grad, state, sent = pl.pallas_call(
+    sent = [shape((ORDER, channels), BF)] * 3
+    gated, gate_grad, par, state, *sent = pl.pallas_call(
         state_kernel,
         grid=grid,
-        in_specs=[spec(3, chunk, 0), spec(3, 8, 0), spec(chunk, 0), spec(rows, 0)]
-        + [fixed(rev2), fixed(sums), fixed(ramp)],
-        out_specs=[spec(chunk, 0), spec(chunk, 0), spec(4 * ORDER, 0), spec(2, ORDER, 0)],
+        in_specs=[scalar, spec(3, chunk, 0), spec(3, 8, 0), spec(chunk, 0), rows(WIRE_ROWS * own), fixed(rev2)],
+        out_specs=[spec(chunk, 0), spec(chunk, 0), spec(48, 0), spec(4 * ORDER, 0)] + [spec(ORDER, 0)] * 3,
         out_shape=[
             shape((chunk, channels), BF),
             shape((chunk, channels), BF),
+            shape((48, channels), F32),
             shape((4 * ORDER, channels), F32),
-            shape((2, ORDER, channels), BF),
-        ],
-        scratch_shapes=[wide(), wide()] + [wide(8 * ORDER)] * 4,
+        ]
+        + sent,
+        scratch_shapes=[wide(), wide()],
         compiler_params=params,
         name="states",
-    )(signal, above, upstream, par, rev2, sums, ramp)
-
-    before = jnp.stack([lax.ppermute(sent[0], ctx, right(k)) for k in range(1, n_ctx)])
-    after = jnp.stack([lax.ppermute(sent[1], ctx, left(k)) for k in range(1, n_ctx)])
+    )(where, signal, above, upstream, wire, rev2)
+
+    got = [
+        lax.ppermute(values, ctx, [(i, (i + k) % n_ctx) for i in range(n_ctx)])
+        for k, values in zip((1, 2, 3), sent)
+    ]
 
     conv, back, modal = pl.pallas_call(
         local_kernel,
         grid=grid,
-        in_specs=[spec(chunk, 0), spec(chunk, 0), spec(rows, 0)]
-        + [fixed(t) for t in (fwd2, inv_hi, inv_lo, sums, ramp)],
+        in_specs=[spec(chunk, 0), spec(chunk, 0), spec(48, 0), fixed(fwd2), fixed(inv2)],
         out_specs=[spec(chunk, 0), spec(chunk, 0), spec(2 * ORDER, 0)],
         out_shape=[
             shape((chunk, channels), F32),
             shape((chunk, channels), F32),
             shape((2 * ORDER, channels), F32),
         ],
-        scratch_shapes=[wide(), wide()] + [wide(8 * ORDER)] * 2,
+        scratch_shapes=[wide(), wide()],
         compiler_params=params,
+        cost_estimate=pl.CostEstimate(flops=8 * 10**9, bytes_accessed=10**7, transcendentals=0),
         name="local",
-    )(gated, gate_grad, par, fwd2, inv_hi, inv_lo, sums, ramp)
-
-    out, proj_grad, grads = pl.pallas_call(
+    )(gated, gate_grad, par, fwd2, inv2)
+
+    out, proj_grad, parts = pl.pallas_call(
         final_kernel,
         grid=grid,
         in_specs=[
-            spec(3, chunk, 0), spec(3, 8, 0), spec(3, 8, 0), spec(chunk, 0), spec(8, 0), spec(rows, 0),
-            spec(4 * ORDER, 0), spec(n_ctx - 1, ORDER, 0), spec(n_ctx - 1, ORDER, 0),
+            scalar, spec(3, chunk, 0), spec(3, 8, 0), spec(4, 8, 0), spec(chunk, 0), spec(48, 0),
+            spec(4 * ORDER, 0), spec(ORDER, 0), spec(ORDER, 0), spec(ORDER, 0),
             spec(2 * ORDER, 0), spec(chunk, 0), spec(chunk, 0), fixed(rev2),
         ],
-        out_specs=[spec(chunk, 0), spec(3, chunk, 0), spec(rows, 0)],
+        out_specs=[spec(chunk, 0), spec(3, chunk, 0), rows(48 * own)],
         out_shape=[
             shape((chunk, channels), BF),
             shape((3, chunk, channels), BF),
-            shape((rows, channels), F32),
+            shape((n_dev, 48 * own), BF),
         ],
-        scratch_shapes=[wide(), wide()],
+        scratch_shapes=[wide(), wide(), wide(48)],
         compiler_params=params,
         name="final",
-    )(signal, above, below, upstream, cot_below, par, state, before, after, modal, conv, back, rev2)
-
-    parts = grads.reshape(rows, n_dev, own).transpose(1, 0, 2)
+    )(where, signal, above, below, upstream, par, state, *got, modal, conv, back, rev2)
+
     arrived = lax.all_to_all(parts, devices, 0, 0, tiled=True)
-    total = jnp.sum(arrived, axis=0) * (1.0 / seq)
+    total = jnp.sum(arrived.astype(F32), axis=0) * (1.0 / seq)
+    total = total.reshape(48, own)
     residue_grad = total[:ORDER]
     decay_grad = -residue * jnp.exp(log_decay) * total[ORDER : 2 * ORDER]
-    tap_grad = total[2 * ORDER :].reshape(3, SHORT, own)
+    tap_grad = total[2 * ORDER : 2 * ORDER + 9].reshape(3, SHORT, own)
     return (
         out[None],
         proj_grad.transpose(1, 0, 2)[None],

time: 195 us -> 147 us (0.75)
  starting transfers between devices: 37.2 us -> 23.7 us
  local copies, waits for them, and re-layouts: 23.5 us -> 10.8 us
  blocking collectives: 38.2 us -> 26.1 us
  waiting for transfers between devices: 26.1 us -> 18.6 us
  Pallas kernels: 63 us -> 59.6 us
    ppermute x9 -> x5, starting transfers between devices: 21.5 us -> 8.06 us  [the longest x1 3.42 us: body(): above = lax.ppermute(signal[:, chunk - 8:], ctx, right)]
    all_to_all x1, blocking collectives: 38.2 us -> 26.1 us  [body(): arrived = lax.all_to_all(parts, devices, 0, 0, tiled=True)]
    unnamed x25 -> x21, local copies, waits for them, and re-layouts: 16 us -> 5.82 us
    broadcast_in_dim x0 -> x1, other arithmetic: none -> 4.21 us  [body(): spread = jnp.broadcast_to(packed, (n_dev, WIRE_ROWS * own))]
    all_to_all x1, waiting for transfers between devices: 22.7 us -> 18.6 us  [body(): wire = lax.all_to_all(spread, devices, 0, 0, tiled=True)]
    ppermute x9 -> x5, waiting for transfers between devices: 3.48 us -> 0.01 us  [the longest x3 0.01 us: body(): lax.ppermute(values, ctx, [(i, (i + k) % n_ctx) for i in range(n_ctx)])]
    pallas_call x1, Pallas kernels: 22.3 us -> 19.3 us  [body(): pl.pallas_call(local_kernel, grid=grid, in_specs=[spec(chunk, 0), spec(ch...]
    all_to_all x1 -> x0, other arithmetic: 2.52 us -> none  [body(): gathered = lax.all_to_all(spread, devices, 0, 0, tiled=True)]
  transfers between devices with their start and end apart: 10 -> 6, of which waited for: 3 -> 1; matrix products, arithmetic and copies ran while one was open for 5% -> 1% of each run, Pallas kernels for 11% -> 27%
where the time goes in v2:
time: 147 us; the launch traced here: 146 us
  Pallas kernels  59.6 us (41%)
  blocking collectives  26.1 us (18%)
  starting transfers between devices  23.7 us (16%)
  waiting for transfers between devices  18.6 us (13%)
  local copies, waits for them, and re-layouts  10.8 us (7%)
  other arithmetic  6.68 us (5%)
    all_to_all x1, blocking collectives, body(): arrived = lax.all_to_all(parts, devices, 0, 0, tiled=True)  26.1 us
    pallas_call x1, Pallas kernels, body(): pl.pallas_call(state_kernel, grid=grid, in_specs=[scalar, spec(3, chunk,...  20.5 us
    pallas_call x1, Pallas kernels, body(): pl.pallas_call(final_kernel, grid=grid, in_specs=[scalar, spec(3, chunk,...  19.8 us
    pallas_call x1, Pallas kernels, body(): pl.pallas_call(local_kernel, grid=grid, in_specs=[spec(chunk, 0), spec(ch...  19.3 us
    all_to_all x1, waiting for transfers between devices, body(): wire = lax.all_to_all(spread, devices, 0, 0, tiled=True)  18.6 us
    all_to_all x1, starting transfers between devices, body(): wire = lax.all_to_all(spread, devices, 0, 0, tiled=True)  15.7 us
    unnamed x21, local copies, waits for them, and re-layouts  5.82 us
    broadcast_in_dim x1, other arithmetic, body(): spread = jnp.broadcast_to(packed, (n_dev, WIRE_ROWS * own))  4.21 us
  transfers between devices with their start and end apart: 6, of which 1 were waited for; matrix products, arithmetic and copies ran while one was open for 1% of the time, Pallas kernels for 27%

profile of v2, /device:TPU:1, one launch (start us, length us, event | category | flops | bytes accessed | tf_op | source)
XLA Modules:
  0.0 146.3 jit_solution(16116958543083490184)
XLA Ops:
  0.6 0.8 copy.18
  1.4 0.7 reshape.47
  2.1 0.1 copy.19
  2.2 0.1 fusion
  2.3 0.1 subtract_convert_fusion
  2.3 0.1 slice.66
  2.4 0.1 slice.65
  2.5 0.1 slice.64
  2.6 0.8 copy.20
  3.3 0.1 concatenate.12
  3.4 0.1 copy.21
  3.5 0.1 broadcast_in_dim.18
  3.6 0.6 broadcast_in_dim.19
  4.3 0.5 broadcast.7
  4.8 4.2 %reduce.1 = bf16[256,1152]{1,0:T(8,128)(2,1)S(1)} reduce(bf16[256,1,1152]{2,1,0:T(2,128)(2,1)S(1)} %broadcast_in_dim.19, bf16[]{:T(256)} %broadcast.7), dimensions={1}, to_apply=%broadcast_in_dim.19.reduce_sub_computation | reduce | bytes 1179650 | tf_op jit(solution)/shard_map/broadcast_in_dim | solution.py:356
  9.0 0.0 slice-start
  9.0 1.5 %reshape.49 = bf16[256,2,576]{2,1,0:T(2,128)(2,1)} reshape(bf16[256,1152]{1,0:T(8,128)(2,1)S(1)} %reduce.1) | data formatting | bytes 1179648
  10.5 15.7 %all-to-all-start = ((bf16[256,2,576]{2,1,0:T(2,128)(2,1)}), bf16[256,2,576]{2,1,0:T(2,128)(2,1)S(1)}, u32[]{:S(2)}, u32[]{:S(2)}) async-start(bf16[256,2,576]{2,1,0:T(2,128)(2,1)} %reshape.49), calls=%async_computation | async-start | bytes 1310720 | tf_op jit(solution)/shard_map/all_to_all | solution.py:357
  26.2 1.1 fusion.1
  27.2 3.4 %collective-permute-start = (bf16[3,8,4096]{2,1,0:T(8,128)(2,1)S(1)}, bf16[3,8,4096]{2,1,0:T(8,128)(2,1)S(1)}, u32[]{:S(2)}, u32[]{:S(2)}) collective-permute-start(bf16[3,8,4096]{2,1,0:T(8,128)(2,1)S(1)} %get-tuple-element.32), channel_id=1, source_target_pairs={{0,64},{64,128},{128,192},{1,65},{65,129},{129,193},{2,66},{66,130... | collective-permute-start | bytes 589832 | tf_op jit(solution)/shard_map/ppermute | solution.py:363
  30.6 0.0 copy-start.2
  30.7 1.3 collective-permute-start.1
  32.0 18.6 %all-to-all-done = bf16[256,2,576]{2,1,0:T(2,128)(2,1)S(1)} async-done(((bf16[256,2,576]{2,1,0:T(2,128)(2,1)}), bf16[256,2,576]{2,1,0:T(2,128)(2,1)S(1)}, u32[]{:S(2)}, u32[]{:S(2)}) %all-to-all-start) | async-done | bytes 589856 | tf_op jit(solution)/shard_map/all_to_all | solution.py:357
  50.6 1.0 reshape.50
  51.6 0.1 copy.25
  51.7 0.0 collective-permute-done.above
  51.7 0.0 copy-start.3
  51.7 0.0 copy-start.4
  51.7 20.5 %states.1 = (bf16[128,4096]{1,0:T(8,128)(2,1)S(1)}, bf16[128,4096]{1,0:T(8,128)(2,1)S(1)}, f32[48,4096]{1,0:T(8,128)S(1)}, f32[64,4096]{1,0:T(8,128)S(1)}, bf16[...) custom-call(s32[1]{0:T(128)} %bitcast.where, bf16[3,128,4096]{2,1,0:T(8,128)(2,1)} %bitcast.20, ...), custom_call_target="tpu_custom_call" | custom-call | tf_op jit(solution)/shard_map/states/pallas_call | solution.py:383
  72.2 0.9 collective-permute-start.2
  73.1 0.1 collective-permute-start.3
  73.1 2.4 %collective-permute-start.4 = (bf16[16,4096]{1,0:T(8,128)(2,1)S(1)}, bf16[16,4096]{1,0:T(8,128)(2,1)S(1)}, u32[]{:S(2)}, u32[]{:S(2)}) collective-permute-start(bf16[16,4096]{1,0:T(8,128)(2,1)S(1)} %get-tuple-element.22), channel_id=1, source_target_pairs={{0,192},{64,0},{128,64},{192,128},{1,193},{65,1},{129,65},{193,129... | collective-permute-start | bytes 393224 | tf_op jit(solution)/shard_map/ppermute | solution.py:401
  75.6 19.3 %local.1 = (f32[128,4096]{1,0:T(8,128)S(1)}, f32[128,4096]{1,0:T(8,128)}, f32[32,4096]{1,0:T(8,128)S(1)}) custom-call(bf16[128,4096]{1,0:T(8,128)(2,1)S(1)} %get-tuple-element.23.gated, bf16[128,4096]{1,0:T(8,128)(2,1)S(1)} %get-tuple-element.24.grad, f32[48,4096]{1,0:T(8,128)S(1)} %get-tuple-element.18.par, bf16[256,256]{1,0:T(8,128)(2,1)S(1)} %copy-done.4, ...), custom_call_target="tpu_custom_call" | custom-call | flops 8000000000 | bytes 10000000 | tf_op jit(solution)/shard_map/local/pallas_call | solution.py:405
  94.9 1.3 copy-done.1
  96.2 0.0 collective-permute-done.1.below
  96.2 0.0 collective-permute-done.2.got1
  96.2 0.0 collective-permute-done.3.got2
  96.2 0.0 collective-permute-done.4.got3
  96.2 19.8 %final.1 = (bf16[128,4096]{1,0:T(8,128)(2,1)}, bf16[3,128,4096]{2,1,0:T(8,128)(2,1)}, bf16[256,768]{1,0:T(8,128)(2,1)S(1)}) custom-call(s32[1]{0:T(128)} %bitcast.where, bf16[3,128,4096]{2,1,0:T(8,128)(2,1)} %bitcast.21, bf16[3,8,4096]{2,1,0:T(8,128)(2,1)S(1)} %collective-permute-done.above, bf16[4,8,4096]{2,1,0:T(8,128)(2,1)S(1)} %collective-permute-done.1.below, ...), custom_call_target="tpu_custom_call" | custom-call | tf_op jit(solution)/shard_map/final/pallas_call | solution.py:421
  116.0 0.9 reduce.2
  117.0 0.1 reshape.51
  117.0 26.1 %all_to_all.17 = bf16[256,2,384]{2,1,0:T(2,128)(2,1)S(1)} all-to-all(bf16[256,2,384]{2,1,0:T(2,128)(2,1)S(1)} %reshape.51), channel_id=1, replica_groups=mesh['ctx'=4,'zero'=64] {'ctx','zero'}, dimensions={0} | all-to-all | bytes 786432 | tf_op jit(solution)/shard_map/all_to_all | solution.py:440
  143.2 0.3 reshape.52
  143.5 0.7 convert_reduce_fusion
  144.2 0.7 reshape.48
  144.9 0.1 slice.59
  145.0 0.6 multiply_multiply_fusion
  145.6 0.7 slice.57
  (16 shorter events, 0.1 us)
Async XLA Ops:
  9.0 21.7 %slice-start = ((bf16[1,128,4096]{2,1,0:T(8,128)(2,1)}), bf16[1,8,4096]{2,1,0:T(8,128)(2,1)S(1)}, s32[]{:S(2)}) async-start(bf16[1,128,4096]{2,1,0:T(8,128)(2,1)} %param.12), calls=%async_computation.2 | async-start | bytes 131072 | tf_op jit(solution)/shard_map/slice | solution.py:364
  10.5 40.1 %all-to-all-start = ((bf16[256,2,576]{2,1,0:T(2,128)(2,1)}), bf16[256,2,576]{2,1,0:T(2,128)(2,1)S(1)}, u32[]{:S(2)}, u32[]{:S(2)}) async-start(bf16[256,2,576]{2,1,0:T(2,128)(2,1)} %reshape.49), calls=%async_computation | async-start | bytes 1310720 | tf_op jit(solution)/shard_map/all_to_all | solution.py:357
  27.2 24.5 %collective-permute-start = (bf16[3,8,4096]{2,1,0:T(8,128)(2,1)S(1)}, bf16[3,8,4096]{2,1,0:T(8,128)(2,1)S(1)}, u32[]{:S(2)}, u32[]{:S(2)}) collective-permute-start(bf16[3,8,4096]{2,1,0:T(8,128)(2,1)S(1)} %get-tuple-element.32), channel_id=1, source_target_pairs={{0,64},{64,128},{128,192},{1,65},{65,129},{129,193},{2,66},{66,130... | collective-permute-start | bytes 589832 | tf_op jit(solution)/shard_map/ppermute | solution.py:363
  30.6 21.0 %copy-start.2 = (bf16[128,256]{1,0:T(8,128)(2,1)S(1)}, bf16[128,256]{1,0:T(8,128)(2,1)}, u32[]{:S(2)}) copy-start(bf16[128,256]{1,0:T(8,128)(2,1)} %constant.20.clone.rev2) | copy-start | bytes 196612
  30.7 65.5 %collective-permute-start.1 = (bf16[4,8,4096]{2,1,0:T(8,128)(2,1)S(1)}, bf16[4,8,4096]{2,1,0:T(8,128)(2,1)S(1)}, u32[]{:S(2)}, u32[]{:S(2)}) collective-permute-start(bf16[4,8,4096]{2,1,0:T(8,128)(2,1)S(1)} %pad_maximum_fusion), channel_id=1, source_target_pairs={{64,0},{128,64},{192,128},{65,1},{129,65},{193,129},{66,2},{130,66... | collective-permute-start | bytes 786440 | tf_op jit(solution)/shard_map/ppermute | solution.py:364
  51.7 23.9 %copy-start.3 = (bf16[256,256]{1,0:T(8,128)(2,1)S(1)}, bf16[256,256]{1,0:T(8,128)(2,1)}, u32[]{:S(2)}) copy-start(bf16[256,256]{1,0:T(8,128)(2,1)} %constant.19.clone.inv2) | copy-start | bytes 393220
  51.7 23.9 %copy-start.4 = (bf16[256,256]{1,0:T(8,128)(2,1)S(1)}, bf16[256,256]{1,0:T(8,128)(2,1)}, u32[]{:S(2)}) copy-start(bf16[256,256]{1,0:T(8,128)(2,1)} %constant.18.clone.fwd2) | copy-start | bytes 393220
  72.2 24.0 %collective-permute-start.2 = (bf16[16,4096]{1,0:T(8,128)(2,1)S(1)}, bf16[16,4096]{1,0:T(8,128)(2,1)S(1)}, u32[]{:S(2)}, u32[]{:S(2)}) collective-permute-start(bf16[16,4096]{1,0:T(8,128)(2,1)S(1)} %get-tuple-element.20), channel_id=1, source_target_pairs={{0,64},{64,128},{128,192},{192,0},{1,65},{65,129},{129,193},{193,1... | collective-permute-start | bytes 393224 | tf_op jit(solution)/shard_map/ppermute | solution.py:401
  73.1 23.1 %collective-permute-start.3 = (bf16[16,4096]{1,0:T(8,128)(2,1)S(1)}, bf16[16,4096]{1,0:T(8,128)(2,1)S(1)}, u32[]{:S(2)}, u32[]{:S(2)}) collective-permute-start(bf16[16,4096]{1,0:T(8,128)(2,1)S(1)} %get-tuple-element.21), channel_id=1, source_target_pairs={{0,128},{64,192},{128,0},{192,64},{1,129},{65,193},{129,1},{193,65... | collective-permute-start | bytes 393224 | tf_op jit(solution)/shard_map/ppermute | solution.py:401
  73.1 23.1 %collective-permute-start.4 = (bf16[16,4096]{1,0:T(8,128)(2,1)S(1)}, bf16[16,4096]{1,0:T(8,128)(2,1)S(1)}, u32[]{:S(2)}, u32[]{:S(2)}) collective-permute-start(bf16[16,4096]{1,0:T(8,128)(2,1)S(1)} %get-tuple-element.22), channel_id=1, source_target_pairs={{0,192},{64,0},{128,64},{192,128},{1,193},{65,1},{129,65},{193,129... | collective-permute-start | bytes 393224 | tf_op jit(solution)/shard_map/ppermute | solution.py:401
  75.6 20.7 %copy-start = (bf16[1,128,4096]{2,1,0:T(8,128)(2,1)S(1)}, bf16[1,128,4096]{2,1,0:T(8,128)(2,1)}, u32[]{:S(2)}) copy-start(bf16[1,128,4096]{2,1,0:T(8,128)(2,1)} %param.12) | copy-start | bytes 3145732
  94.9 1.3 copy-start.1
  116.0 29.0 %copy-start.5 = (f32[16,16]{1,0:T(8,128)S(1)}, f32[16,16]{1,0:T(8,128)}, u32[]{:S(2)}) copy-start(f32[16,16]{1,0:T(8,128)} %param.11) | copy-start | bytes 3076
  116.0 29.0 %copy-start.6 = (f32[16,16]{1,0:T(8,128)S(1)}, f32[16,16]{1,0:T(8,128)}, u32[]{:S(2)}) copy-start(f32[16,16]{1,0:T(8,128)} %param.10) | copy-start | bytes 3076

commit v3 on v0

v3 whole, which is shorter than its diff:
```python
import functools

import jax
import jax.numpy as jnp
from jax import lax
from jax.experimental import pallas as pl
from jax.experimental.pallas import tpu as pltpu
from jax.sharding import PartitionSpec as P

SHORT = 3
ORDER = 16
LANES = 128
WIDE = 8 * LANES
WIRE = 16
WIRE_ROWS = 72
SUM_ROWS = 48
HALF = ORDER // 2
BF = jnp.bfloat16
F32 = jnp.float32


def tree(parts):
    parts = list(parts)
    while len(parts) > 1:
        parts = [a + b for a, b in zip(parts[::2], parts[1::2])]
    return parts[0]


def rounded(values):
    return values.astype(BF).astype(F32)


def swap_blocks(tile):
    row = lax.broadcasted_iota(jnp.int32, (8, LANES), 0)
    column = lax.broadcasted_iota(jnp.int32, (8, LANES), 1) // WIRE
    for bit in (1, 2, 4):
        row_bit, column_bit = row & bit, column & bit
        ahead = pltpu.roll(pltpu.roll(tile, 8 - bit, 0), WIRE * bit, 1)
        back = pltpu.roll(pltpu.roll(tile, bit, 0), LANES - WIRE * bit, 1)
        tile = jnp.where(row_bit == column_bit, tile, jnp.where(row_bit < column_bit, ahead, back))
    return tile


def tile_rows(tile, lane):
    start = (tile * 8 + lane) * 8
    return pl.ds(start if isinstance(start, int) else pl.multiple_of(start, 8), 8)


def line_rows(row):
    return pl.ds((row // 8) * 64 + row % 8, 8, stride=8)


def tap_weights(par, lane):
    first = par[tile_rows(4, lane), :]
    last = par[tile_rows(5, lane), :]
    return [first[i : i + 1] for i in range(8)] + [last[0:1]]


def column(lane):
    return pl.ds(pl.multiple_of(lane * LANES, LANES), LANES)


def load_signal(which, proj, above, signal, lane):
    rows = proj.shape[1]
    signal[which, 0:8] = above[which, :, column(lane)].astype(F32)
    signal[which, 8 : 8 + rows] = proj[which, :, column(lane)].astype(F32)


def taps(which, signal, weights, start, rows):
    return tree(
        [weights[3 * which + j] * signal[which, 8 + start - j : 8 + start - j + rows] for j in range(2)]
    ) + weights[3 * which + 2] * signal[which, 6 + start : 6 + start + rows]


def decay_of(par):
    return [jnp.exp(-jnp.exp(par[line_rows(ORDER + m), :])) for m in range(ORDER)]


def flat_row(rows):
    padded = jnp.concatenate([rows, jnp.zeros((8, LANES - WIRE), F32)], 1)
    return swap_blocks(padded)[0:1]


def spread_kernel(short_weight, residue, log_decay, out):
    weights = jnp.concatenate([short_weight[i] for i in range(3)], 0)
    rates = log_decay[...]
    rates_high, weights_high = rounded(rates), rounded(weights)
    rates_low, weights_low = rates - rates_high, weights - weights_high
    last = jnp.concatenate([weights_high[8:], weights_low[8:], jnp.zeros((6, WIRE), F32)], 0)
    tiles = [
        rates_high[:8], rates_high[8:], rates_low[:8], rates_low[8:], residue[:8], residue[8:],
        weights_high[:8], last, weights_low[:8],
    ]
    for q, tile in enumerate(tiles):
        row = jnp.broadcast_to(flat_row(tile), (out.shape[0], LANES))
        out[:, q * LANES : q * LANES + LANES] = row.astype(BF)


def collect_kernel(scale, arrived, residue, log_decay, tap_grad, residue_grad, decay_grad):
    total = jnp.sum(arrived[...].astype(F32), axis=0, keepdims=True) * scale
    first = lax.broadcasted_iota(jnp.int32, (8, LANES), 0) == 0
    tiles = [
        swap_blocks(jnp.where(first, total[:, q * LANES : q * LANES + LANES], 0.0))[:, :WIRE]
        for q in range(SUM_ROWS // 8)
    ]
    residue_grad[...] = jnp.concatenate(tiles[0:2], 0)
    decay_grad[...] = -residue[...] * jnp.exp(log_decay[...]) * jnp.concatenate(tiles[2:4], 0)
    lines = jnp.concatenate(tiles[4:6], 0)
    for i in range(3):
        tap_grad[i] = lines[3 * i : 3 * i + 3]


def state_kernel(where, proj, above, cot, wire, par, send1, send2, send3, signal, xs, gs):
    chunk = cot.shape[0]
    arrived = wire[...].astype(F32)
    for lane in range(8):
        parts = [
            swap_blocks(arrived[8 * lane : 8 * lane + 8, q * LANES : q * LANES + LANES])
            for q in range(WIRE_ROWS // 8)
        ]
        par[tile_rows(0, lane), :] = parts[4]
        par[tile_rows(1, lane), :] = parts[5]
        par[tile_rows(2, lane), :] = parts[0] + parts[2]
        par[tile_rows(3, lane), :] = parts[1] + parts[3]
        par[tile_rows(4, lane), :] = parts[6] + parts[8]
        par[tile_rows(5, lane), :] = jnp.broadcast_to(parts[7][0:1] + parts[7][1:2], (8, LANES))

    @pl.loop(0, 8)
    def _(lane):
        weights = tap_weights(par, lane)
        for i in range(3):
            load_signal(i, proj, above, signal, lane)
        queries, keys, values = (taps(i, signal, weights, 0, chunk) for i in range(3))
        gated = rounded(keys * values)
        gate_grad = rounded(cot[:, column(lane)].astype(F32) * queries)
        for tile in range(chunk // 8):
            xs[tile_rows(tile, lane), :] = gated[8 * tile : 8 * tile + 8]
            gs[tile_rows(tile, lane), :] = gate_grad[8 * tile : 8 * tile + 8]

    decay = decay_of(par)

    def step(tile, carry):
        forward, backward = map(list, carry)
        for i in range(8):
            x = xs[pl.ds(tile * 64 + i, 8, stride=8), :]
            g = gs[pl.ds((chunk // 8 - 1 - tile) * 64 + 7 - i, 8, stride=8), :]
            forward = [a * h + x for a, h in zip(decay, forward)]
            backward = [a * p + g for a, p in zip(decay, backward)]
        return tuple(forward), tuple(backward)

    zero = tuple(jnp.zeros((8, LANES), F32) for _ in range(ORDER))
    forward, backward = lax.fori_loop(0, chunk // 8, step, (zero, zero))
    for away, send in zip((1, 2, 3), (send1, send2, send3)):
        ahead = where[0] + away < 4
        for m in range(0, ORDER, 2):
            pair = [jnp.where(ahead, forward[n], backward[n]) for n in (m, m + 1)]
            send[8 * m : 8 * m + 16, :] = jnp.concatenate(pair, 0).astype(BF)


def final_kernel(*refs):
    (where, proj, above, below, cot, par, got1, got2, got3, *rest) = refs
    (out, proj_grad, sums_out, signal, tails, fgrads, xs, gs, ys, bs, queries_s, keys_s, values_s, held, sums) = rest[-15:]
    chunk = cot.shape[0]
    tiles = chunk // 8

    @pl.loop(0, 8)
    def _(lane):
        weights = tap_weights(par, lane)
        for i in range(3):
            load_signal(i, proj, above, signal.at[lane], lane)
            signal[lane, i, 8 + chunk :] = below[i, :, column(lane)].astype(F32)
        here = signal.at[lane]
        queries, keys, values = (taps(i, here, weights, 0, chunk + 8) for i in range(3))
        gated = rounded(keys * values)
        queries_s[lane] = queries
        keys_s[lane] = keys
        values_s[lane] = values
        for tile in range(tiles + 1):
            rows = slice(8 * tile, 8 * tile + 8)
            if tile < tiles:
                upstream = cot[rows, column(lane)].astype(F32)
            else:
                upstream = below[3, :, column(lane)].astype(F32)
            xs[tile_rows(tile, lane), :] = gated[rows]
            gs[tile_rows(tile, lane), :] = rounded(upstream * queries[rows])

    for group in range(0, ORDER, HALF):
        modes = range(group, group + HALF)
        rates = [jnp.exp(par[line_rows(ORDER + m), :]) for m in modes]
        decay = [jnp.exp(-r) for r in rates]
        gain = [par[line_rows(m), :] for m in modes]
        entering, leaving = [], []
        for n, m in enumerate(modes):
            whole = jnp.exp(-float(chunk) * rates[n])
            scales = [None, whole, whole * whole]
            enter, leave = jnp.zeros((8, LANES), F32), jnp.zeros((8, LANES), F32)
            for away, got in zip((1, 2, 3), (got1, got2, got3)):
                pair = got[16 * (m // 2) : 16 * (m // 2) + 16, :].astype(F32)
                state = pair[8 * (m % 2) : 8 * (m % 2) + 8]
                near = state if away == 1 else scales[away - 1] * state
                far = state if away == 3 else scales[3 - away] * state
                enter = enter + jnp.where(where[0] >= away, near, 0.0)
                leave = leave + jnp.where(where[0] < away, far, 0.0)
            entering.append(enter)
            leaving.append(leave)

        def store(ref, rows, value, group=group):
            if group:
                value = value + ref[rows, :]
            ref[rows, :] = value

        def forward(tile, carry):
            states, totals = map(list, carry)
            for i in range(8):
                rows = pl.ds(tile * 64 + i, 8, stride=8)
                x, g = xs[rows, :], gs[rows, :]
                for n in range(HALF):
                    held[tile * 8 + i, n] = states[n]
                states = [a * h + x for a, h in zip(decay, states)]
                totals = [t + g * h for t, h in zip(totals, states)]
                store(ys, rows, tree([r * h for r, h in zip(gain, states)]))
            return tuple(states), tuple(totals)

        zero = tuple(jnp.zeros((8, LANES), F32) for _ in modes)
        states, totals = lax.fori_loop(0, tiles, forward, (tuple(entering), zero))
        for i in range(2):
            rows = line_rows(chunk + i)
            states = [a * h + xs[rows, :] for a, h in zip(decay, states)]
            store(ys, rows, tree([r * h for r, h in zip(gain, states)]))

        def backward(step, carry):
            states, counts = map(list, carry)
            tile = tiles - 1 - step
            for i in range(7, -1, -1):
                rows = pl.ds(tile * 64 + i, 8, stride=8)
                g = gs[rows, :]
                states = [a * p + g for a, p in zip(decay, states)]
                counts = [c + p * held[tile * 8 + i, n] for n, (c, p) in enumerate(zip(counts, states))]
                store(bs, rows, tree([r * p for r, p in zip(gain, states)]))
            return tuple(states), tuple(counts)

        _, counts = lax.fori_loop(0, tiles, backward, (tuple(leaving), zero))
        store(bs, line_rows(chunk), tree([r * p for r, p in zip(gain, leaving)]))
        after = [(p - gs[line_rows(chunk), :]) / a for a, p in zip(decay, leaving)]
        store(bs, line_rows(chunk + 1), tree([r * p for r, p in zip(gain, after)]))
        for n, m in enumerate(modes):
            sums[line_rows(m), :] = totals[n]
            sums[line_rows(ORDER + m), :] = decay[n] * counts[n]

    two = lax.broadcasted_iota(jnp.int32, (8, LANES), 0) < 2

    @pl.loop(0, 8)
    def _(lane):
        weights = tap_weights(par, lane)
        upstream = cot[:, column(lane)].astype(F32)
        tail_up = below[3, :, column(lane)].astype(F32)
        convolved = rounded(jnp.concatenate([ys[tile_rows(t, lane), :] for t in range(tiles)], 0))
        gated_grad = rounded(jnp.concatenate([bs[tile_rows(t, lane), :] for t in range(tiles)], 0))
        tail_conv = rounded(jnp.where(two, ys[tile_rows(tiles, lane), :], 0.0))
        tail_back = rounded(jnp.where(two, bs[tile_rows(tiles, lane), :], 0.0))
        out[:, column(lane)] = (queries_s[lane, 0:chunk] * convolved).astype(BF)
        lines = []
        for i in range(3):
            if i == 0:
                grad, tail = upstream * convolved, tail_up * tail_conv
            else:
                other = values_s if i == 1 else keys_s
                grad = gated_grad * other[lane, 0:chunk]
                tail = tail_back * other[lane, chunk : chunk + 8]
            fgrads[i, 0:chunk] = grad
            fgrads[i, chunk:] = tail
            total = weights[3 * i] * grad
            for j in range(1, SHORT):
                total = total + weights[3 * i + j] * fgrads[i, j : j + chunk]
            proj_grad[i, :, column(lane)] = total.astype(BF)
            for j in range(SHORT):
                lines.append(jnp.sum(grad * signal[lane, i, 8 - j : 8 - j + chunk], axis=0, keepdims=True))
        sums[tile_rows(4, lane), :] = jnp.concatenate(lines[:8], 0)
        sums[tile_rows(5, lane), :] = jnp.concatenate([lines[8], jnp.zeros((7, LANES), F32)], 0)

    for lane in range(0, 8, 2):
        rows = [
            jnp.concatenate([swap_blocks(sums[tile_rows(q, k), :]) for q in range(SUM_ROWS // 8)], 1)
            for k in (lane, lane + 1)
        ]
        sums_out[8 * lane : 8 * lane + 16, :] = jnp.concatenate(rows, 0).astype(BF)


def body(names, proj, short_weight, residue, log_decay, cotangent):
    ctx, devices, n_ctx = names
    chunk, channels = cotangent.shape[1:]
    own = residue.shape[1]
    seq = chunk * n_ctx
    n_dev = channels // own
    blocks = channels // WIDE
    runs = 2 if blocks % 2 == 0 else 1
    steps = blocks // runs
    where = lax.axis_index(ctx).astype(jnp.int32).reshape(1)

    spread = pl.pallas_call(
        spread_kernel,
        out_shape=jax.ShapeDtypeStruct((n_dev, WIRE_ROWS * own), BF),
        name="spread",
    )(short_weight, residue, log_decay)
    wire = lax.all_to_all(spread, devices, 0, 0, tiled=True)

    signal = proj[0].transpose(1, 0, 2)
    upstream = cotangent[0]
    right = [(i, i + 1) for i in range(n_ctx - 1)]
    left = [(i + 1, i) for i in range(n_ctx - 1)]
    above = lax.ppermute(signal[:, chunk - 8 :], ctx, right)
    below = lax.ppermute(jnp.concatenate([signal[:, :8], upstream[None, :8]], 0), ctx, left)

    def shape(dims, kind):
        return jax.ShapeDtypeStruct(dims, kind)

    scalar = pl.BlockSpec(memory_space=pltpu.SMEM)
    anywhere = pl.BlockSpec(memory_space=pl.ANY)
    vmem = lambda *dims: pltpu.VMEM(dims, F32)
    params = pltpu.CompilerParams(vmem_limit_bytes=48 * 1024 * 1024)

    def specs(run):
        def wide(*dims):
            lead = len(dims)
            return pl.BlockSpec(dims + (WIDE,), lambda i: (0,) * lead + (i + run * steps,))

        def rows(count):
            return pl.BlockSpec((WIDE // own, count), lambda i: (i + run * steps, 0))

        def whole(count):
            return pl.BlockSpec((None, count, LANES), lambda i: (i, 0, 0))

        return wide, rows, whole

    pars, gots = [], []
    for run in range(runs):
        wide, rows, whole = specs(run)
        par, *sent = pl.pallas_call(
            state_kernel,
            grid=(steps,),
            in_specs=[scalar, wide(3, chunk), wide(3, 8), wide(chunk), rows(WIRE_ROWS * own)],
            out_specs=[whole(8 * SUM_ROWS)] + [whole(8 * ORDER)] * 3,
            out_shape=[shape((steps, 8 * SUM_ROWS, LANES), F32)]
            + [shape((steps, 8 * ORDER, LANES), BF)] * 3,
            scratch_shapes=[vmem(3, chunk + 8, LANES), vmem(chunk * 8, LANES), vmem(chunk * 8, LANES)],
            compiler_params=params,
            cost_estimate=pl.CostEstimate(flops=4 * 10**9, bytes_accessed=4 * 10**6, transcendentals=0),
            name="states",
        )(where, signal, above, upstream, wire)
        pars.append(par)
        gots.append(
            [
                lax.ppermute(values, ctx, [(i, (i + k) % n_ctx) for i in range(n_ctx)])
                for k, values in zip((1, 2, 3), sent)
            ]
        )

    results = [
        shape((chunk, channels), BF),
        shape((3, chunk, channels), BF),
        shape((n_dev, SUM_ROWS * own), BF),
    ]
    made = []
    longer = chunk + 8
    for run in range(runs):
        wide, rows, whole = specs(run)
        made = pl.pallas_call(
            final_kernel,
            grid=(steps,),
            in_specs=[scalar, wide(3, chunk), wide(3, 8), wide(4, 8), wide(chunk), whole(8 * SUM_ROWS)]
            + [whole(8 * ORDER)] * 3
            + [anywhere] * len(made),
            out_specs=[wide(chunk), wide(3, chunk), rows(SUM_ROWS * own)],
            out_shape=results,
            scratch_shapes=[
                vmem(8, 3, chunk + 16, LANES), vmem(8, LANES), vmem(3, longer, LANES),
                vmem(longer * 8, LANES), vmem(longer * 8, LANES),
                vmem(longer * 8, LANES), vmem(longer * 8, LANES),
                vmem(8, longer, LANES), vmem(8, longer, LANES), vmem(8, longer, LANES),
                vmem(chunk, HALF, 8, LANES), vmem(8 * SUM_ROWS, LANES),
            ],
            input_output_aliases={9 + i: i for i in range(len(made))},
            compiler_params=params,
            cost_estimate=pl.CostEstimate(flops=8 * 10**9, bytes_accessed=8 * 10**6, transcendentals=0),
            name="final",
        )(where, signal, above, below, upstream, pars[run], *gots[run], *made)
    out, proj_grad, parts = made

    arrived = lax.all_to_all(parts, devices, 0, 0, tiled=True)
    tap_grad, residue_grad, decay_grad = pl.pallas_call(
        functools.partial(collect_kernel, 1.0 / seq),
        out_shape=[shape((3, SHORT, own), F32), shape((ORDER, own), F32), shape((ORDER, own), F32)],
        name="collect",
    )(arrived, residue, log_decay)
    return (
        out[None],
        proj_grad.transpose(1, 0, 2)[None],
        tap_grad,
        residue_grad,
        decay_grad,
    )


def solution(mesh):
    both = ("ctx", "zero")
    specs = (
        P("zero", "ctx", None, None),
        P(None, None, both),
        P(None, both),
        P(None, both),
        P("zero", "ctx", None),
    )
    out_specs = (specs[4], specs[0], specs[1], specs[2], specs[2])
    names = ("ctx", both, mesh.shape["ctx"])
    return jax.shard_map(
        functools.partial(body, names), mesh=mesh, in_specs=specs, out_specs=out_specs, check_vma=False
    )
```

time: 1970 us -> 139 us (0.07)
  waiting for transfers between devices: 1240 us -> 16.8 us
  blocking collectives: 401 us -> 25.8 us
  matrix products: 101 us -> 0 us
  other arithmetic: 91.3 us -> 4.42 us
  local copies, waits for them, and re-layouts: 85.4 us -> 14.5 us
  Pallas kernels: 0 us -> 47.1 us
    unnamed x6 -> x0, waiting for transfers between devices: 1210 us -> none
    all_gather x3 -> x0, blocking collectives: 401 us -> none  [the longest x1 176 us: body(): lax.all_gather(log_decay, 'zero', axis=1, tiled=True)]
    dot_general x15 -> x0, matrix products: 101 us -> none  [the longest x3 25.7 us: transform(): real_part = jnp.einsum('ft,btc->bfc', tables[0], signal, precision=highest)]
    pallas_call x0 -> x6, Pallas kernels: none -> 47.1 us  [the longest x2 29.6 us: body(): pl.pallas_call(final_kernel, grid=(steps,), in_specs=[scalar, wide(3, chu...]
    reduce_sum x3 -> x0, other arithmetic: 45.1 us -> none  [the longest x2 31.8 us: taps_weight_grad(): columns.append(jnp.sum(grads * window.astype(jnp.float32), axis=(0, 1)))]
    unnamed x3 -> x0, other arithmetic: 30.1 us -> none
    all_to_all x0 -> x1, blocking collectives: none -> 25.8 us  [body(): arrived = lax.all_to_all(parts, devices, 0, 0, tiled=True)]
    all_to_all x5 -> x1, local copies, waits for them, and re-layouts: 20.6 us -> 0.51 us  [body(): wire = lax.all_to_all(spread, devices, 0, 0, tiled=True)]
  transfers between devices with their start and end apart: 7 -> 9, of which waited for: 5 -> 1; matrix products, arithmetic and copies ran while one was open for 4% -> 6% of each run, Pallas kernels for 0% -> 20%
where the time goes in v3:
time: 139 us
  Pallas kernels  47.1 us (34%)
  starting transfers between devices  29.1 us (21%)
  blocking collectives  25.8 us (19%)
  waiting for transfers between devices  16.8 us (12%)
  local copies, waits for them, and re-layouts  14.5 us (10%)
  other arithmetic  4.42 us (3%)
    pallas_call x2, Pallas kernels, body(): pl.pallas_call(final_kernel, grid=(steps,), in_specs=[scalar, wide(3, chu...  29.6 us
    all_to_all x1, blocking collectives, body(): arrived = lax.all_to_all(parts, devices, 0, 0, tiled=True)  25.8 us
    all_to_all x1, waiting for transfers between devices, body(): wire = lax.all_to_all(spread, devices, 0, 0, tiled=True)  16.8 us
    all_to_all x1, starting transfers between devices, body(): wire = lax.all_to_all(spread, devices, 0, 0, tiled=True)  16.5 us
    pallas_call x2, Pallas kernels, body(): pl.pallas_call(state_kernel, grid=(steps,), in_specs=[scalar, wide(3, chu...  13.6 us
    unnamed x14, local copies, waits for them, and re-layouts  13.3 us
    ppermute x6, starting transfers between devices, body(): lax.ppermute(values, ctx, [(i, (i + k) % n_ctx) for i in range(n_ctx)])  7.25 us
    ppermute x1, starting transfers between devices, body(): above = lax.ppermute(signal[:, chunk - 8:], ctx, right)  4.08 us
  transfers between devices with their start and end apart: 9, of which 1 were waited for; matrix products, arithmetic and copies ran while one was open for 6% of the time, Pallas kernels for 20%

profile of v3, /device:TPU:1, one launch (start us, length us, event | category | flops | bytes accessed | tf_op | source)
XLA Modules:
  0.0 138.6 jit_solution(11950172453388471451)
XLA Ops:
  0.6 0.0 copy-start
  0.6 0.0 slice-start
  0.7 2.0 %spread.1 = bf16[256,1152]{1,0:T(8,128)(2,1)} custom-call(f32[3,3,16]{2,1,0:T(4,128)} %short_weight.1, f32[16,16]{1,0:T(8,128)} %residue.3, f32[16,16]{1,0:T(8,128)} %log_decay.3), custom_call_target="tpu_custom_call" | custom-call | tf_op jit(solution)/shard_map/spread/pallas_call | solution.py:300
  2.6 0.5 broadcast
  3.1 2.8 %reduce = bf16[256,1152]{1,0:T(8,128)(2,1)} reduce(bf16[256,1,1152]{2,0,1:T(8,128)(2,1)} %bitcast.29, bf16[]{:T(256)} %broadcast), dimensions={1}, to_apply=%copy.15.reduce_sub_computation | reduce | bytes 1179650 | tf_op jit(solution)/shard_map/all_to_all | solution.py:305
  5.9 2.8 %reshape.20 = bf16[256,2,576]{2,1,0:T(2,128)(2,1)} reshape(bf16[256,1152]{1,0:T(8,128)(2,1)} %reduce) | data formatting | bytes 1179648
  8.8 16.5 %all-to-all-start = ((bf16[256,2,576]{2,1,0:T(2,128)(2,1)}), bf16[256,2,576]{2,1,0:T(2,128)(2,1)}, u32[]{:S(2)}, u32[]{:S(2)}) async-start(bf16[256,2,576]{2,1,0:T(2,128)(2,1)} %reshape.20), calls=%async_computation | async-start | bytes 1310720 | tf_op jit(solution)/shard_map/all_to_all | solution.py:305
  25.3 0.0 copy-done
  25.3 0.7 fusion
  26.1 4.1 %collective-permute-start = (bf16[3,8,4096]{2,1,0:T(8,128)(2,1)}, bf16[3,8,4096]{2,1,0:T(8,128)(2,1)}, u32[]{:S(2)}, u32[]{:S(2)}) collective-permute-start(bf16[3,8,4096]{2,1,0:T(8,128)(2,1)} %get-tuple-element.40), channel_id=1, source_target_pairs={{0,64},{64,128},{128,192},{1,65},{65,129},{129,193},{2,66},{66,130... | collective-permute-start | bytes 589832 | tf_op jit(solution)/shard_map/ppermute | solution.py:311
  30.1 0.0 slice-done
  30.1 0.7 pad_maximum_fusion
  30.9 1.3 collective-permute-start.1
  32.2 16.8 %all-to-all-done = bf16[256,2,576]{2,1,0:T(2,128)(2,1)} async-done(((bf16[256,2,576]{2,1,0:T(2,128)(2,1)}), bf16[256,2,576]{2,1,0:T(2,128)(2,1)}, u32[]{:S(2)}, u32[]{:S(2)}) %all-to-all-start) | async-done | bytes 589856 | tf_op jit(solution)/shard_map/all_to_all | solution.py:305
  49.0 5.0 %reshape.21 = bf16[256,1,1152]{2,1,0:T(2,128)(2,1)} reshape(bf16[256,2,576]{2,1,0:T(2,128)(2,1)} %all-to-all-done) | data formatting | bytes 1179648
  54.0 1.3 copy.21
  55.3 0.0 collective-permute-done.above.refs_2_
  55.3 0.0 copy-start.1
  55.3 1.2 copy-done.1
  56.5 6.8 %states.3 = (f32[2,384,128]{2,1,0:T(8,128)S(1)}, bf16[2,128,128]{2,1,0:T(8,128)(2,1)S(1)}, bf16[2,128,128]{2,1,0:T(8,128)(2,1)S(1)}, bf16[2,128,128]{2,1,0:T(8,128)(2,1)S(1)}) custom-call(s32[1]{0:T(128)} %bitcast.where.refs_0_, bf16[3,128,4096]{2,1,0:T(8,128)(2,1)S(1)} %bitcast.21, bf16[3,8,4096]{2,1,0:T(8,128)(2,1)} %collective-permute-done.above.refs_2_, ...), custom_call_target="tpu_custom_call" | custom-call | flops 4000000000 | bytes 4000000 | tf_op jit(solution)/shard_map/states/pallas_call | solution.py:338
  63.4 0.9 collective-permute-start.5
  64.2 0.1 collective-permute-start.6
  64.3 2.4 %collective-permute-start.7 = (bf16[2,128,128]{2,1,0:T(8,128)(2,1)S(1)}, bf16[2,128,128]{2,1,0:T(8,128)(2,1)S(1)}, u32[]{:S(2)}, u32[]{:S(2)}) collective-permute-start(bf16[2,128,128]{2,1,0:T(8,128)(2,1)S(1)} %get-tuple-element.29), channel_id=1, source_target_pairs={{0,192},{64,0},{128,64},{192,128},{1,193},{65,1},{129,65},{193,129... | collective-permute-start | bytes 196616 | tf_op jit(solution)/shard_map/ppermute | solution.py:353
  66.7 6.8 %states.2 = (f32[2,384,128]{2,1,0:T(8,128)S(1)}, bf16[2,128,128]{2,1,0:T(8,128)(2,1)S(1)}, bf16[2,128,128]{2,1,0:T(8,128)(2,1)S(1)}, bf16[2,128,128]{2,1,0:T(8,128)(2,1)S(1)}) custom-call(s32[1]{0:T(128)} %bitcast.where.refs_0_, bf16[3,128,4096]{2,1,0:T(8,128)(2,1)S(1)} %bitcast.22, bf16[3,8,4096]{2,1,0:T(8,128)(2,1)} %collective-permute-done.above.refs_2_, ...), custom_call_target="tpu_custom_call" | custom-call | flops 4000000000 | bytes 4000000 | tf_op jit(solution)/shard_map/states/pallas_call | solution.py:338
  73.5 0.4 collective-permute-start.2
  73.9 0.0 collective-permute-done.1.refs_3_
  73.9 0.0 copy-start.2
  73.9 0.7 copy-done.2
  74.6 1.2 collective-permute-start.3
  75.8 0.0 collective-permute-done.5.refs_6_
  75.8 2.3 %collective-permute-start.4 = (bf16[2,128,128]{2,1,0:T(8,128)(2,1)S(1)}, bf16[2,128,128]{2,1,0:T(8,128)(2,1)S(1)}, u32[]{:S(2)}, u32[]{:S(2)}) collective-permute-start(bf16[2,128,128]{2,1,0:T(8,128)(2,1)S(1)} %get-tuple-element.25), channel_id=1, source_target_pairs={{0,192},{64,0},{128,64},{192,128},{1,193},{65,1},{129,65},{193,129... | collective-permute-start | bytes 196616 | tf_op jit(solution)/shard_map/ppermute | solution.py:353
  78.1 0.0 collective-permute-done.6.refs_7_
  78.1 0.0 collective-permute-done.7.refs_8_
  78.1 0.0 copy-start.3
  78.1 0.9 copy-done.3
  79.1 14.8 %final.2 = (bf16[128,4096]{1,0:T(8,128)(2,1)}, bf16[3,128,4096]{2,1,0:T(8,128)(2,1)}, bf16[256,768]{1,0:T(8,128)(2,1)S(1)}) custom-call(s32[1]{0:T(128)} %bitcast.where.refs_0_, bf16[3,128,4096]{2,1,0:T(8,128)(2,1)S(1)} %bitcast.23, bf16[3,8,4096]{2,1,0:T(8,128)(2,1)} %collective-permute-done.above.refs_2_, bf16[4,8,4096]{2,1,0:T(8,128)(2,1)S(1)} %copy-done.3, ...), custom_call_target="tpu_custom_call" | custom-call | flops 8000000000 | bytes 8000000 | tf_op jit(solution)/shard_map/final/pallas_call | solution.py:367
  93.9 0.0 collective-permute-done.2.refs_6_
  93.9 0.0 collective-permute-done.3.refs_7_
  93.9 0.0 collective-permute-done.4.refs_8_
  93.9 14.8 %final.3 = (bf16[128,4096]{1,0:T(8,128)(2,1)}, bf16[3,128,4096]{2,1,0:T(8,128)(2,1)}, bf16[256,768]{1,0:T(8,128)(2,1)S(1)}) custom-call(s32[1]{0:T(128)} %bitcast.where.refs_0_, bf16[3,128,4096]{2,1,0:T(8,128)(2,1)S(1)} %bitcast.24, ...), custom_call_target="tpu_custom_call", output_to_operand_aliasing={{0}: (9, {}), {1}: (10, {}), {2}: (11, {})} | custom-call | flops 8000000000 | bytes 8000000 | tf_op jit(solution)/shard_map/final/pallas_call | solution.py:367
  108.7 0.9 reduce.1
  109.7 0.1 reshape.22
  109.8 25.8 %all_to_all.22 = bf16[256,2,384]{2,1,0:T(2,128)(2,1)S(1)} all-to-all(bf16[256,2,384]{2,1,0:T(2,128)(2,1)S(1)} %reshape.22), channel_id=1, replica_groups=mesh['ctx'=4,'zero'=64] {'ctx','zero'}, dimensions={0} | all-to-all | bytes 786432 | tf_op jit(solution)/shard_map/all_to_all | solution.py:389
  135.6 0.3 reshape.23
  135.9 0.8 copy.22
  136.7 1.9 %collect.1 = (f32[3,3,16]{2,1,0:T(4,128)}, f32[16,16]{1,0:T(8,128)}, f32[16,16]{1,0:T(8,128)}) custom-call(bf16[256,768]{1,0:T(8,128)(2,1)} %bitcast.30, f32[16,16]{1,0:T(8,128)} %residue.3, f32[16,16]{1,0:T(8,128)} %log_decay.3), custom_call_target="tpu_custom_call" | custom-call | tf_op jit(solution)/shard_map/collect/pallas_call | solution.py:390
Async XLA Ops:
  0.6 24.7 %copy-start = (bf16[1,128,3,4096]{3,1,2,0:T(8,128)(2,1)S(1)}, bf16[1,128,3,4096]{3,1,2,0:T(8,128)(2,1)}, u32[]{:S(2)}) copy-start(bf16[1,128,3,4096]{3,1,2,0:T(8,128)(2,1)} %param.5) | copy-start | bytes 9437188
  0.6 29.5 %slice-start = ((bf16[1,128,4096]{2,1,0:T(8,128)(2,1)}), bf16[1,8,4096]{2,1,0:T(8,128)(2,1)S(1)}, s32[]{:S(2)}) async-start(bf16[1,128,4096]{2,1,0:T(8,128)(2,1)} %param.9), calls=%async_computation.2 | async-start | bytes 131072 | tf_op jit(solution)/shard_map/slice | solution.py:312
  8.8 40.2 %all-to-all-start = ((bf16[256,2,576]{2,1,0:T(2,128)(2,1)}), bf16[256,2,576]{2,1,0:T(2,128)(2,1)}, u32[]{:S(2)}, u32[]{:S(2)}) async-start(bf16[256,2,576]{2,1,0:T(2,128)(2,1)} %reshape.20), calls=%async_computation | async-start | bytes 1310720 | tf_op jit(solution)/shard_map/all_to_all | solution.py:305
  26.1 29.3 %collective-permute-start = (bf16[3,8,4096]{2,1,0:T(8,128)(2,1)}, bf16[3,8,4096]{2,1,0:T(8,128)(2,1)}, u32[]{:S(2)}, u32[]{:S(2)}) collective-permute-start(bf16[3,8,4096]{2,1,0:T(8,128)(2,1)} %get-tuple-element.40), channel_id=1, source_target_pairs={{0,64},{64,128},{128,192},{1,65},{65,129},{129,193},{2,66},{66,130... | collective-permute-start | bytes 589832 | tf_op jit(solution)/shard_map/ppermute | solution.py:311
  30.9 43.0 %collective-permute-start.1 = (bf16[4,8,4096]{2,1,0:T(8,128)(2,1)}, bf16[4,8,4096]{2,1,0:T(8,128)(2,1)S(1)}, u32[]{:S(2)}, u32[]{:S(2)}) collective-permute-start(bf16[4,8,4096]{2,1,0:T(8,128)(2,1)} %pad_maximum_fusion), channel_id=1, source_target_pairs={{64,0},{128,64},{192,128},{65,1},{129,65},{193,129},{66,2},{130,66... | collective-permute-start | bytes 786440 | tf_op jit(solution)/shard_map/ppermute | solution.py:312
  55.3 1.2 copy-start.1
  63.4 12.4 %collective-permute-start.5 = (bf16[2,128,128]{2,1,0:T(8,128)(2,1)S(1)}, bf16[2,128,128]{2,1,0:T(8,128)(2,1)S(1)}, u32[]{:S(2)}, u32[]{:S(2)}) collective-permute-start(bf16[2,128,128]{2,1,0:T(8,128)(2,1)S(1)} %get-tuple-element.27), channel_id=1, source_target_pairs={{0,64},{64,128},{128,192},{192,0},{1,65},{65,129},{129,193},{193,1... | collective-permute-start | bytes 196616 | tf_op jit(solution)/shard_map/ppermute | solution.py:353
  64.2 13.9 %collective-permute-start.6 = (bf16[2,128,128]{2,1,0:T(8,128)(2,1)S(1)}, bf16[2,128,128]{2,1,0:T(8,128)(2,1)S(1)}, u32[]{:S(2)}, u32[]{:S(2)}) collective-permute-start(bf16[2,128,128]{2,1,0:T(8,128)(2,1)S(1)} %get-tuple-element.28), channel_id=1, source_target_pairs={{0,128},{64,192},{128,0},{192,64},{1,129},{65,193},{129,1},{193,65... | collective-permute-start | bytes 196616 | tf_op jit(solution)/shard_map/ppermute | solution.py:353
  64.3 13.9 %collective-permute-start.7 = (bf16[2,128,128]{2,1,0:T(8,128)(2,1)S(1)}, bf16[2,128,128]{2,1,0:T(8,128)(2,1)S(1)}, u32[]{:S(2)}, u32[]{:S(2)}) collective-permute-start(bf16[2,128,128]{2,1,0:T(8,128)(2,1)S(1)} %get-tuple-element.29), channel_id=1, source_target_pairs={{0,192},{64,0},{128,64},{192,128},{1,193},{65,1},{129,65},{193,129... | collective-permute-start | bytes 196616 | tf_op jit(solution)/shard_map/ppermute | solution.py:353
  73.5 20.4 %collective-permute-start.2 = (bf16[2,128,128]{2,1,0:T(8,128)(2,1)S(1)}, bf16[2,128,128]{2,1,0:T(8,128)(2,1)S(1)}, u32[]{:S(2)}, u32[]{:S(2)}) collective-permute-start(bf16[2,128,128]{2,1,0:T(8,128)(2,1)S(1)} %get-tuple-element.23), channel_id=1, source_target_pairs={{0,64},{64,128},{128,192},{192,0},{1,65},{65,129},{129,193},{193,1... | collective-permute-start | bytes 196616 | tf_op jit(solution)/shard_map/ppermute | solution.py:353
  73.9 0.7 copy-start.2
  74.6 19.3 %collective-permute-start.3 = (bf16[2,128,128]{2,1,0:T(8,128)(2,1)S(1)}, bf16[2,128,128]{2,1,0:T(8,128)(2,1)S(1)}, u32[]{:S(2)}, u32[]{:S(2)}) collective-permute-start(bf16[2,128,128]{2,1,0:T(8,128)(2,1)S(1)} %get-tuple-element.24), channel_id=1, source_target_pairs={{0,128},{64,192},{128,0},{192,64},{1,129},{65,193},{129,1},{193,65... | collective-permute-start | bytes 196616 | tf_op jit(solution)/shard_map/ppermute | solution.py:353
  75.8 18.1 %collective-permute-start.4 = (bf16[2,128,128]{2,1,0:T(8,128)(2,1)S(1)}, bf16[2,128,128]{2,1,0:T(8,128)(2,1)S(1)}, u32[]{:S(2)}, u32[]{:S(2)}) collective-permute-start(bf16[2,128,128]{2,1,0:T(8,128)(2,1)S(1)} %get-tuple-element.25), channel_id=1, source_target_pairs={{0,192},{64,0},{128,64},{192,128},{1,193},{65,1},{129,65},{193,129... | collective-permute-start | bytes 196616 | tf_op jit(solution)/shard_map/ppermute | solution.py:353
  78.1 1.0 copy-start.3

commit v4 on v3

--- a/solution.py
+++ b/solution.py
@@ -12,8 +12,10 @@
 LANES = 128
 WIDE = 8 * LANES
 WIRE = 16
-WIRE_ROWS = 72
+WIRE_ROWS = 64
 SUM_ROWS = 48
+PAR_ROWS = 48
+RATE_CENTRE = -5.4
 HALF = ORDER // 2
 BF = jnp.bfloat16
 F32 = jnp.float32
@@ -30,15 +32,32 @@
     return values.astype(BF).astype(F32)
 
 
-def swap_blocks(tile):
+def turn_rows(tile, forward):
+    if forward:
+        return pltpu.roll(tile, 0, 1, stride=WIRE, stride_axis=0)
     row = lax.broadcasted_iota(jnp.int32, (8, LANES), 0)
+    for bit in (1, 2, 4):
+        tile = jnp.where((row & bit) != 0, pltpu.roll(tile, LANES - WIRE * bit, 1), tile)
+    return tile
+
+
+def turn_columns(tile, forward):
     column = lax.broadcasted_iota(jnp.int32, (8, LANES), 1) // WIRE
     for bit in (1, 2, 4):
-        row_bit, column_bit = row & bit, column & bit
-        ahead = pltpu.roll(pltpu.roll(tile, 8 - bit, 0), WIRE * bit, 1)
-        back = pltpu.roll(pltpu.roll(tile, bit, 0), LANES - WIRE * bit, 1)
-        tile = jnp.where(row_bit == column_bit, tile, jnp.where(row_bit < column_bit, ahead, back))
+        tile = jnp.where((column & bit) != 0, pltpu.roll(tile, bit if forward else 8 - bit, 0), tile)
     return tile
+
+
+def rows_of_lines(tile):
+    return turn_rows(turn_columns(turn_rows(tile, True), False), True)
+
+
+def lines_of_rows(tile):
+    return turn_rows(turn_columns(turn_rows(tile, False), True), False)
+
+
+def wire_order(rows):
+    return jnp.concatenate([rows[(8 - b) % 8 : (8 - b) % 8 + 1] for b in range(8)], 0)
 
 
 def tile_rows(tile, lane):
@@ -77,30 +96,28 @@
 
 
 def flat_row(rows):
-    padded = jnp.concatenate([rows, jnp.zeros((8, LANES - WIRE), F32)], 1)
-    return swap_blocks(padded)[0:1]
+    padded = jnp.concatenate([wire_order(rows), jnp.zeros((8, LANES - WIRE), F32)], 1)
+    return jnp.sum(turn_rows(padded, True), axis=0, keepdims=True)
 
 
 def spread_kernel(short_weight, residue, log_decay, out):
     weights = jnp.concatenate([short_weight[i] for i in range(3)], 0)
-    rates = log_decay[...]
+    rates = log_decay[...] - RATE_CENTRE
     rates_high, weights_high = rounded(rates), rounded(weights)
     rates_low, weights_low = rates - rates_high, weights - weights_high
-    last = jnp.concatenate([weights_high[8:], weights_low[8:], jnp.zeros((6, WIRE), F32)], 0)
     tiles = [
-        rates_high[:8], rates_high[8:], rates_low[:8], rates_low[8:], residue[:8], residue[8:],
-        weights_high[:8], last, weights_low[:8],
+        rates_high[:8], rates_high[8:], rates_low[:8],
+        jnp.concatenate([rates_low[8:14], weights_high[8:], weights_low[8:]], 0),
+        residue[:8], residue[8:], weights_high[:8], weights_low[:8],
     ]
-    for q, tile in enumerate(tiles):
-        row = jnp.broadcast_to(flat_row(tile), (out.shape[0], LANES))
-        out[:, q * LANES : q * LANES + LANES] = row.astype(BF)
+    rows = jnp.concatenate([flat_row(tile) for tile in tiles], 0)
+    out[...] = jnp.broadcast_to(rows[None], out.shape).astype(BF)
 
 
 def collect_kernel(scale, arrived, residue, log_decay, tap_grad, residue_grad, decay_grad):
-    total = jnp.sum(arrived[...].astype(F32), axis=0, keepdims=True) * scale
-    first = lax.broadcasted_iota(jnp.int32, (8, LANES), 0) == 0
+    total = jnp.sum(arrived[...].astype(F32), axis=0) * scale
     tiles = [
-        swap_blocks(jnp.where(first, total[:, q * LANES : q * LANES + LANES], 0.0))[:, :WIRE]
+        wire_order(turn_rows(jnp.broadcast_to(total[q : q + 1], (8, LANES)), False)[:, :WIRE])
         for q in range(SUM_ROWS // 8)
     ]
     residue_grad[...] = jnp.concatenate(tiles[0:2], 0)
@@ -110,20 +127,19 @@
         tap_grad[i] = lines[3 * i : 3 * i + 3]
 
 
-def state_kernel(where, proj, above, cot, wire, par, send1, send2, send3, signal, xs, gs):
+def state_kernel(where, proj, above, cot, wire, par, send1, send2, send3, signal, xs, gs, wires):
     chunk = cot.shape[0]
-    arrived = wire[...].astype(F32)
+    wires[...] = wire[...].astype(F32).reshape(wires.shape)
+    early = lax.broadcasted_iota(jnp.int32, (8, LANES), 0) < 6
+
     for lane in range(8):
-        parts = [
-            swap_blocks(arrived[8 * lane : 8 * lane + 8, q * LANES : q * LANES + LANES])
-            for q in range(WIRE_ROWS // 8)
-        ]
+        parts = [rows_of_lines(wires[pl.ds(lane * 64 + q, 8, stride=8), :]) for q in range(8)]
         par[tile_rows(0, lane), :] = parts[4]
         par[tile_rows(1, lane), :] = parts[5]
-        par[tile_rows(2, lane), :] = parts[0] + parts[2]
-        par[tile_rows(3, lane), :] = parts[1] + parts[3]
-        par[tile_rows(4, lane), :] = parts[6] + parts[8]
-        par[tile_rows(5, lane), :] = jnp.broadcast_to(parts[7][0:1] + parts[7][1:2], (8, LANES))
+        par[tile_rows(2, lane), :] = parts[0] + parts[2] + RATE_CENTRE
+        par[tile_rows(3, lane), :] = parts[1] + jnp.where(early, parts[3], 0.0) + RATE_CENTRE
+        par[tile_rows(4, lane), :] = parts[6] + parts[7]
+        par[tile_rows(5, lane), :] = jnp.broadcast_to(parts[3][6:7] + parts[3][7:8], (8, LANES))
 
     @pl.loop(0, 8)
     def _(lane):
@@ -149,7 +165,7 @@
         return tuple(forward), tuple(backward)
 
     zero = tuple(jnp.zeros((8, LANES), F32) for _ in range(ORDER))
-    forward, backward = lax.fori_loop(0, chunk // 8, step, (zero, zero))
+    forward, backward = lax.fori_loop(0, chunk // 8, step, (zero, zero), unroll=2)
     for away, send in zip((1, 2, 3), (send1, send2, send3)):
         ahead = where[0] + away < 4
         for m in range(0, ORDER, 2):
@@ -159,7 +175,7 @@
 
 def final_kernel(*refs):
     (where, proj, above, below, cot, par, got1, got2, got3, *rest) = refs
-    (out, proj_grad, sums_out, signal, tails, fgrads, xs, gs, ys, bs, queries_s, keys_s, values_s, held, sums) = rest[-15:]
+    (out, proj_grad, sums_out, signal, tails, fgrads, xs, gs, ys, bs, queries_s, keys_s, values_s, held, sums, lines_s) = rest[-16:]
     chunk = cot.shape[0]
     tiles = chunk // 8
 
@@ -222,7 +238,7 @@
             return tuple(states), tuple(totals)
 
         zero = tuple(jnp.zeros((8, LANES), F32) for _ in modes)
-        states, totals = lax.fori_loop(0, tiles, forward, (tuple(entering), zero))
+        states, totals = lax.fori_loop(0, tiles, forward, (tuple(entering), zero), unroll=2)
         for i in range(2):
             rows = line_rows(chunk + i)
             states = [a * h + xs[rows, :] for a, h in zip(decay, states)]
@@ -239,7 +255,7 @@
                 store(bs, rows, tree([r * p for r, p in zip(gain, states)]))
             return tuple(states), tuple(counts)
 
-        _, counts = lax.fori_loop(0, tiles, backward, (tuple(leaving), zero))
+        _, counts = lax.fori_loop(0, tiles, backward, (tuple(leaving), zero), unroll=2)
         store(bs, line_rows(chunk), tree([r * p for r, p in zip(gain, leaving)]))
         after = [(p - gs[line_rows(chunk), :]) / a for a, p in zip(decay, leaving)]
         store(bs, line_rows(chunk + 1), tree([r * p for r, p in zip(gain, after)]))
@@ -278,12 +294,11 @@
         sums[tile_rows(4, lane), :] = jnp.concatenate(lines[:8], 0)
         sums[tile_rows(5, lane), :] = jnp.concatenate([lines[8], jnp.zeros((7, LANES), F32)], 0)
 
-    for lane in range(0, 8, 2):
-        rows = [
-            jnp.concatenate([swap_blocks(sums[tile_rows(q, k), :]) for q in range(SUM_ROWS // 8)], 1)
-            for k in (lane, lane + 1)
-        ]
-        sums_out[8 * lane : 8 * lane + 16, :] = jnp.concatenate(rows, 0).astype(BF)
+    for lane in range(8):
+        for q in range(SUM_ROWS // 8):
+            lines_s[pl.ds(lane * 64 + q, 8, stride=8), :] = lines_of_rows(sums[tile_rows(q, lane), :])
+
+    sums_out[...] = lines_s[...].reshape(64, 8, LANES)[:, : SUM_ROWS // 8].astype(BF)
 
 
 def body(names, proj, short_weight, residue, log_decay, cotangent):
@@ -299,7 +314,7 @@
 
     spread = pl.pallas_call(
         spread_kernel,
-        out_shape=jax.ShapeDtypeStruct((n_dev, WIRE_ROWS * own), BF),
+        out_shape=jax.ShapeDtypeStruct((n_dev, WIRE_ROWS // 8, 8 * own), BF),
         name="spread",
     )(short_weight, residue, log_decay)
     wire = lax.all_to_all(spread, devices, 0, 0, tiled=True)
@@ -317,7 +332,7 @@
     scalar = pl.BlockSpec(memory_space=pltpu.SMEM)
     anywhere = pl.BlockSpec(memory_space=pl.ANY)
     vmem = lambda *dims: pltpu.VMEM(dims, F32)
-    params = pltpu.CompilerParams(vmem_limit_bytes=48 * 1024 * 1024)
+    params = pltpu.CompilerParams(vmem_limit_bytes=32 * 1024 * 1024)
 
     def specs(run):
         def wide(*dims):
@@ -325,7 +340,7 @@
             return pl.BlockSpec(dims + (WIDE,), lambda i: (0,) * lead + (i + run * steps,))
 
         def rows(count):
-            return pl.BlockSpec((WIDE // own, count), lambda i: (i + run * steps, 0))
+            return pl.BlockSpec((WIDE // own, count // 8, 8 * own), lambda i: (i + run * steps, 0, 0))
 
         def whole(count):
             return pl.BlockSpec((None, count, LANES), lambda i: (i, 0, 0))
@@ -338,11 +353,13 @@
         par, *sent = pl.pallas_call(
             state_kernel,
             grid=(steps,),
-            in_specs=[scalar, wide(3, chunk), wide(3, 8), wide(chunk), rows(WIRE_ROWS * own)],
-            out_specs=[whole(8 * SUM_ROWS)] + [whole(8 * ORDER)] * 3,
-            out_shape=[shape((steps, 8 * SUM_ROWS, LANES), F32)]
+            in_specs=[scalar, wide(3, chunk), wide(3, 8), wide(chunk), rows(WIRE_ROWS)],
+            out_specs=[whole(8 * PAR_ROWS)] + [whole(8 * ORDER)] * 3,
+            out_shape=[shape((steps, 8 * PAR_ROWS, LANES), F32)]
             + [shape((steps, 8 * ORDER, LANES), BF)] * 3,
-            scratch_shapes=[vmem(3, chunk + 8, LANES), vmem(chunk * 8, LANES), vmem(chunk * 8, LANES)],
+            scratch_shapes=[
+                vmem(3, chunk + 8, LANES), vmem(chunk * 8, LANES), vmem(chunk * 8, LANES), vmem(512, LANES),
+            ],
             compiler_params=params,
             cost_estimate=pl.CostEstimate(flops=4 * 10**9, bytes_accessed=4 * 10**6, transcendentals=0),
             name="states",
@@ -358,7 +375,7 @@
     results = [
         shape((chunk, channels), BF),
         shape((3, chunk, channels), BF),
-        shape((n_dev, SUM_ROWS * own), BF),
+        shape((n_dev, SUM_ROWS // 8, 8 * own), BF),
     ]
     made = []
     longer = chunk + 8
@@ -367,17 +384,17 @@
         made = pl.pallas_call(
             final_kernel,
             grid=(steps,),
-            in_specs=[scalar, wide(3, chunk), wide(3, 8), wide(4, 8), wide(chunk), whole(8 * SUM_ROWS)]
+            in_specs=[scalar, wide(3, chunk), wide(3, 8), wide(4, 8), wide(chunk), whole(8 * PAR_ROWS)]
             + [whole(8 * ORDER)] * 3
             + [anywhere] * len(made),
-            out_specs=[wide(chunk), wide(3, chunk), rows(SUM_ROWS * own)],
+            out_specs=[wide(chunk), wide(3, chunk), rows(SUM_ROWS)],
             out_shape=results,
             scratch_shapes=[
                 vmem(8, 3, chunk + 16, LANES), vmem(8, LANES), vmem(3, longer, LANES),
                 vmem(longer * 8, LANES), vmem(longer * 8, LANES),
                 vmem(longer * 8, LANES), vmem(longer * 8, LANES),
                 vmem(8, longer, LANES), vmem(8, longer, LANES), vmem(8, longer, LANES),
-                vmem(chunk, HALF, 8, LANES), vmem(8 * SUM_ROWS, LANES),
+                vmem(chunk, HALF, 8, LANES), vmem(8 * SUM_ROWS, LANES), vmem(512, LANES),
             ],
             input_output_aliases={9 + i: i for i in range(len(made))},
             compiler_params=params,

time: 139 us -> 120 us (0.86)
  local copies, waits for them, and re-layouts: 14.5 us -> 5.01 us
  Pallas kernels: 47.1 us -> 40.9 us
  other arithmetic: 4.42 us -> 0.02 us
  blocking collectives: 25.8 us -> 30.2 us
  waiting for transfers between devices: 16.8 us -> 15 us
  starting transfers between devices: 29.1 us -> 27.6 us
    unnamed x14 -> x6, local copies, waits for them, and re-layouts: 13.3 us -> 3.12 us
    all_to_all x1, waiting for transfers between devices: 16.8 us -> 8.7 us  [body(): wire = lax.all_to_all(spread, devices, 0, 0, tiled=True)]
    ppermute x1, waiting for transfers between devices: 0.01 us -> 6.28 us  [body(): above = lax.ppermute(signal[:, chunk - 8:], ctx, right)]
    all_to_all x1, blocking collectives: 25.8 us -> 30.2 us  [body(): arrived = lax.all_to_all(parts, devices, 0, 0, tiled=True)]
    pallas_call x2, Pallas kernels: 13.6 us -> 9.32 us  [body(): pl.pallas_call(state_kernel, grid=(steps,), in_specs=[scalar, wide(3, chu...]
    all_to_all x2 -> x0, other arithmetic: 3.7 us -> none  [the longest x1 2.78 us: body(): wire = lax.all_to_all(spread, devices, 0, 0, tiled=True)]
    pallas_call x2, Pallas kernels: 29.6 us -> 27.7 us  [body(): pl.pallas_call(final_kernel, grid=(steps,), in_specs=[scalar, wide(3, chu...]
  transfers between devices with their start and end apart: 9 -> 9, of which waited for: 1 -> 2; matrix products, arithmetic and copies ran while one was open for 6% -> 2% of each run, Pallas kernels for 20% -> 19%
where the time goes in v4:
time: 120 us; the launch traced here: 119 us
  Pallas kernels  40.9 us (34%)
  blocking collectives  30.2 us (25%)
  starting transfers between devices  27.6 us (23%)
  waiting for transfers between devices  15 us (12%)
  local copies, waits for them, and re-layouts  5.01 us (4%)
    all_to_all x1, blocking collectives, body(): arrived = lax.all_to_all(parts, devices, 0, 0, tiled=True)  30.2 us
    pallas_call x2, Pallas kernels, body(): pl.pallas_call(final_kernel, grid=(steps,), in_specs=[scalar, wide(3, chu...  27.7 us
    all_to_all x1, starting transfers between devices, body(): wire = lax.all_to_all(spread, devices, 0, 0, tiled=True)  15.7 us
    pallas_call x2, Pallas kernels, body(): pl.pallas_call(state_kernel, grid=(steps,), in_specs=[scalar, wide(3, chu...  9.32 us
    all_to_all x1, waiting for transfers between devices, body(): wire = lax.all_to_all(spread, devices, 0, 0, tiled=True)  8.7 us
    ppermute x6, starting transfers between devices, body(): lax.ppermute(values, ctx, [(i, (i + k) % n_ctx) for i in range(n_ctx)])  7.25 us
    ppermute x1, waiting for transfers between devices, body(): above = lax.ppermute(signal[:, chunk - 8:], ctx, right)  6.28 us
    ppermute x1, starting transfers between devices, body(): above = lax.ppermute(signal[:, chunk - 8:], ctx, right)  3.42 us
  transfers between devices with their start and end apart: 9, of which 2 were waited for; matrix products, arithmetic and copies ran while one was open for 2% of the time, Pallas kernels for 19%

profile of v4, /device:TPU:1, one launch (start us, length us, event | category | flops | bytes accessed | tf_op | source)
XLA Modules:
  0.0 119.4 jit_solution(6187791291428027674)
XLA Ops:
  0.6 1.7 %spread.1 = bf16[256,8,128]{2,1,0:T(8,128)(2,1)} custom-call(f32[3,3,16]{2,1,0:T(4,128)} %short_weight.1, f32[16,16]{1,0:T(8,128)} %residue.3, f32[16,16]{1,0:T(8,128)} %log_decay.3), custom_call_target="tpu_custom_call" | custom-call | tf_op jit(solution)/shard_map/spread/pallas_call | solution.py:315
  2.3 15.7 %all-to-all-start = ((bf16[256,8,128]{2,1,0:T(8,128)(2,1)}), bf16[256,8,128]{2,1,0:T(8,128)(2,1)S(1)}, u32[]{:S(2)}, u32[]{:S(2)}) async-start(bf16[256,8,128]{2,1,0:T(8,128)(2,1)} %spread.1), calls=%async_computation | async-start | bytes 1048576 | tf_op jit(solution)/shard_map/all_to_all | solution.py:320
  17.9 1.1 fusion
  19.0 3.4 %collective-permute-start = (bf16[3,8,4096]{2,1,0:T(8,128)(2,1)S(1)}, bf16[3,8,4096]{2,1,0:T(8,128)(2,1)S(1)}, u32[]{:S(2)}, u32[]{:S(2)}) collective-permute-start(bf16[3,8,4096]{2,1,0:T(8,128)(2,1)S(1)} %get-tuple-element.40), channel_id=1, source_target_pairs={{0,64},{64,128},{128,192},{1,65},{65,129},{129,193},{2,66},{66,130... | collective-permute-start | bytes 589832 | tf_op jit(solution)/shard_map/ppermute | solution.py:326
  22.4 0.8 slice.12
  23.3 1.3 %collective-permute-start.1 = (bf16[4,8,4096]{2,1,0:T(8,128)(2,1)S(1)}, bf16[4,8,4096]{2,1,0:T(8,128)(2,1)S(1)}, u32[]{:S(2)}, u32[]{:S(2)}) collective-permute-start(bf16[4,8,4096]{2,1,0:T(8,128)(2,1)S(1)} %pad_maximum_fusion), channel_id=1, source_target_pairs={{64,0},{128,64},{192,128},{65,1},{129,65},{193,129},{66,2},{130,66... | collective-permute-start | bytes 786440 | tf_op jit(solution)/shard_map/ppermute | solution.py:327
  24.6 6.3 %collective-permute-done.above.refs_2_ = bf16[3,8,4096]{2,1,0:T(8,128)(2,1)S(1)} collective-permute-done((bf16[3,8,4096]{2,1,0:T(8,128)(2,1)S(1)}, bf16[3,8,4096]{2,1,0:T(8,128)(2,1)S(1)}, u32[]{:S(2)}, u32[]{:S(2)}) %collective-permute-start) | collective-permute-done | bytes 196640 | tf_op jit(solution)/shard_map/ppermute | solution.py:326
  30.9 8.7 %all-to-all-done.wire = bf16[256,8,128]{2,1,0:T(8,128)(2,1)S(1)} async-done(((bf16[256,8,128]{2,1,0:T(8,128)(2,1)}), bf16[256,8,128]{2,1,0:T(8,128)(2,1)S(1)}, u32[]{:S(2)}, u32[]{:S(2)}) %all-to-all-start) | async-done | bytes 524320 | tf_op jit(solution)/shard_map/all_to_all | solution.py:320
  39.6 0.0 copy-start
  39.6 1.9 %copy-done = bf16[1,128,3,4096]{3,1,2,0:T(8,128)(2,1)S(1)} copy-done((bf16[1,128,3,4096]{3,1,2,0:T(8,128)(2,1)S(1)}, bf16[1,128,3,4096]{3,1,2,0:T(8,128)(2,1)}, u32[]{:S(2)}) %copy-start) | copy-done | bytes 3145752
  41.5 0.0 copy-start.2
  41.5 1.2 %copy-done.2 = bf16[1,128,4096]{2,1,0:T(8,128)(2,1)S(1)} copy-done((bf16[1,128,4096]{2,1,0:T(8,128)(2,1)S(1)}, bf16[1,128,4096]{2,1,0:T(8,128)(2,1)}, u32[]{:S(2)}) %copy-start.2) | copy-done | bytes 1048600
  42.7 4.7 %states.3 = (f32[2,384,128]{2,1,0:T(8,128)S(1)}, bf16[2,128,128]{2,1,0:T(8,128)(2,1)S(1)}, bf16[2,128,128]{2,1,0:T(8,128)(2,1)S(1)}, bf16[2,128,128]{2,1,0:T(8,128)(2,1)S(1)}) custom-call(s32[1]{0:T(128)} %bitcast.where.refs_0_, bf16[3,128,4096]{2,1,0:T(8,128)(2,1)S(1)} %bitcast.10, bf16[3,8,4096]{2,1,0:T(8,128)(2,1)S(1)} %collective-permute-done.above.refs_2_, ...), custom_call_target="tpu_custom_call" | custom-call | flops 4000000000 | bytes 4000000 | tf_op jit(solution)/shard_map/states/pallas_call | solution.py:353
  47.4 0.9 collective-permute-start.5
  48.3 0.1 collective-permute-start.6
  48.3 0.0 copy-start.1
  48.3 2.4 %collective-permute-start.7 = (bf16[2,128,128]{2,1,0:T(8,128)(2,1)S(1)}, bf16[2,128,128]{2,1,0:T(8,128)(2,1)S(1)}, u32[]{:S(2)}, u32[]{:S(2)}) collective-permute-start(bf16[2,128,128]{2,1,0:T(8,128)(2,1)S(1)} %get-tuple-element.29), channel_id=1, source_target_pairs={{0,192},{64,0},{128,64},{192,128},{1,193},{65,1},{129,65},{193,129... | collective-permute-start | bytes 196616 | tf_op jit(solution)/shard_map/ppermute | solution.py:370
  50.7 4.7 %states.2 = (f32[2,384,128]{2,1,0:T(8,128)S(1)}, bf16[2,128,128]{2,1,0:T(8,128)(2,1)S(1)}, bf16[2,128,128]{2,1,0:T(8,128)(2,1)S(1)}, bf16[2,128,128]{2,1,0:T(8,128)(2,1)S(1)}) custom-call(s32[1]{0:T(128)} %bitcast.where.refs_0_, bf16[3,128,4096]{2,1,0:T(8,128)(2,1)S(1)} %bitcast.11, bf16[3,8,4096]{2,1,0:T(8,128)(2,1)S(1)} %collective-permute-done.above.refs_2_, ...), custom_call_target="tpu_custom_call" | custom-call | flops 4000000000 | bytes 4000000 | tf_op jit(solution)/shard_map/states/pallas_call | solution.py:353
  55.4 0.4 collective-permute-start.2
  55.8 0.0 collective-permute-done.1.refs_3_
  55.8 1.3 %collective-permute-start.3 = (bf16[2,128,128]{2,1,0:T(8,128)(2,1)S(1)}, bf16[2,128,128]{2,1,0:T(8,128)(2,1)S(1)}, u32[]{:S(2)}, u32[]{:S(2)}) collective-permute-start(bf16[2,128,128]{2,1,0:T(8,128)(2,1)S(1)} %get-tuple-element.24), channel_id=1, source_target_pairs={{0,128},{64,192},{128,0},{192,64},{1,129},{65,193},{129,1},{193,65... | collective-permute-start | bytes 196616 | tf_op jit(solution)/shard_map/ppermute | solution.py:370
  57.0 0.0 collective-permute-done.5.refs_6_
  57.1 2.3 %collective-permute-start.4 = (bf16[2,128,128]{2,1,0:T(8,128)(2,1)S(1)}, bf16[2,128,128]{2,1,0:T(8,128)(2,1)S(1)}, u32[]{:S(2)}, u32[]{:S(2)}) collective-permute-start(bf16[2,128,128]{2,1,0:T(8,128)(2,1)S(1)} %get-tuple-element.25), channel_id=1, source_target_pairs={{0,192},{64,0},{128,64},{192,128},{1,193},{65,1},{129,65},{193,129... | collective-permute-start | bytes 196616 | tf_op jit(solution)/shard_map/ppermute | solution.py:370
  59.3 0.0 collective-permute-done.6.refs_7_
  59.3 0.0 collective-permute-done.7.refs_8_
  59.3 0.0 copy-done.1
  59.3 13.9 %final.2 = (bf16[128,4096]{1,0:T(8,128)(2,1)}, bf16[3,128,4096]{2,1,0:T(8,128)(2,1)}, bf16[256,6,128]{2,1,0:T(8,128)(2,1)S(1)}) custom-call(s32[1]{0:T(128)} %bitcast.where.refs_0_, bf16[3,128,4096]{2,1,0:T(8,128)(2,1)S(1)} %bitcast.12, bf16[3,8,4096]{2,1,0:T(8,128)(2,1)S(1)} %collective-permute-done.above.refs_2_, ...), custom_call_target="tpu_custom_call" | custom-call | flops 8000000000 | bytes 8000000 | tf_op jit(solution)/shard_map/final/pallas_call | solution.py:384
  73.2 0.0 collective-permute-done.2.refs_6_
  73.2 0.0 collective-permute-done.3.refs_7_
  73.2 0.0 collective-permute-done.4.refs_8_
  73.2 13.9 %final.3 = (bf16[128,4096]{1,0:T(8,128)(2,1)}, bf16[3,128,4096]{2,1,0:T(8,128)(2,1)}, bf16[256,6,128]{2,1,0:T(8,128)(2,1)S(1)}) custom-call(s32[1]{0:T(128)} %bitcast.where.refs_0_, bf16[3,128,4096]{2,1,0:T(8,128)(2,1)S(1)} %bitcast.13, ...), custom_call_target="tpu_custom_call", output_to_operand_aliasing={{0}: (9, {}), {1}: (10, {}), {2}: (11, {})} | custom-call | flops 8000000000 | bytes 8000000 | tf_op jit(solution)/shard_map/final/pallas_call | solution.py:384
  87.1 30.2 %all_to_all.10.arrived = bf16[256,6,128]{2,1,0:T(8,128)(2,1)} all-to-all(bf16[256,6,128]{2,1,0:T(8,128)(2,1)S(1)} %get-tuple-element.35), channel_id=1, replica_groups=mesh['ctx'=4,'zero'=64] {'ctx','zero'}, dimensions={0} | all-to-all | bytes 786432 | tf_op jit(solution)/shard_map/all_to_all | solution.py:406
  117.3 2.2 %collect.1 = (f32[3,3,16]{2,1,0:T(4,128)}, f32[16,16]{1,0:T(8,128)}, f32[16,16]{1,0:T(8,128)}) custom-call(bf16[256,6,128]{2,1,0:T(8,128)(2,1)} %all_to_all.10.arrived, f32[16,16]{1,0:T(8,128)} %residue.3, f32[16,16]{1,0:T(8,128)} %log_decay.3), custom_call_target="tpu_custom_call" | custom-call | tf_op jit(solution)/shard_map/collect/pallas_call | solution.py:407
  (1 shorter events, 0.0 us)
Async XLA Ops:
  2.3 37.3 %all-to-all-start = ((bf16[256,8,128]{2,1,0:T(8,128)(2,1)}), bf16[256,8,128]{2,1,0:T(8,128)(2,1)S(1)}, u32[]{:S(2)}, u32[]{:S(2)}) async-start(bf16[256,8,128]{2,1,0:T(8,128)(2,1)} %spread.1), calls=%async_computation | async-start | bytes 1048576 | tf_op jit(solution)/shard_map/all_to_all | solution.py:320
  19.0 11.9 %collective-permute-start = (bf16[3,8,4096]{2,1,0:T(8,128)(2,1)S(1)}, bf16[3,8,4096]{2,1,0:T(8,128)(2,1)S(1)}, u32[]{:S(2)}, u32[]{:S(2)}) collective-permute-start(bf16[3,8,4096]{2,1,0:T(8,128)(2,1)S(1)} %get-tuple-element.40), channel_id=1, source_target_pairs={{0,64},{64,128},{128,192},{1,65},{65,129},{129,193},{2,66},{66,130... | collective-permute-start | bytes 589832 | tf_op jit(solution)/shard_map/ppermute | solution.py:326
  23.3 32.5 %collective-permute-start.1 = (bf16[4,8,4096]{2,1,0:T(8,128)(2,1)S(1)}, bf16[4,8,4096]{2,1,0:T(8,128)(2,1)S(1)}, u32[]{:S(2)}, u32[]{:S(2)}) collective-permute-start(bf16[4,8,4096]{2,1,0:T(8,128)(2,1)S(1)} %pad_maximum_fusion), channel_id=1, source_target_pairs={{64,0},{128,64},{192,128},{65,1},{129,65},{193,129},{66,2},{130,66... | collective-permute-start | bytes 786440 | tf_op jit(solution)/shard_map/ppermute | solution.py:327
  39.6 1.9 %copy-start = (bf16[1,128,3,4096]{3,1,2,0:T(8,128)(2,1)S(1)}, bf16[1,128,3,4096]{3,1,2,0:T(8,128)(2,1)}, u32[]{:S(2)}) copy-start(bf16[1,128,3,4096]{3,1,2,0:T(8,128)(2,1)} %param.5) | copy-start | bytes 9437188
  41.5 1.2 %copy-start.2 = (bf16[1,128,4096]{2,1,0:T(8,128)(2,1)S(1)}, bf16[1,128,4096]{2,1,0:T(8,128)(2,1)}, u32[]{:S(2)}) copy-start(bf16[1,128,4096]{2,1,0:T(8,128)(2,1)} %param.9) | copy-start | bytes 3145732
  47.4 9.7 %collective-permute-start.5 = (bf16[2,128,128]{2,1,0:T(8,128)(2,1)S(1)}, bf16[2,128,128]{2,1,0:T(8,128)(2,1)S(1)}, u32[]{:S(2)}, u32[]{:S(2)}) collective-permute-start(bf16[2,128,128]{2,1,0:T(8,128)(2,1)S(1)} %get-tuple-element.27), channel_id=1, source_target_pairs={{0,64},{64,128},{128,192},{192,0},{1,65},{65,129},{129,193},{193,1... | collective-permute-start | bytes 196616 | tf_op jit(solution)/shard_map/ppermute | solution.py:370
  48.3 11.1 %collective-permute-start.6 = (bf16[2,128,128]{2,1,0:T(8,128)(2,1)S(1)}, bf16[2,128,128]{2,1,0:T(8,128)(2,1)S(1)}, u32[]{:S(2)}, u32[]{:S(2)}) collective-permute-start(bf16[2,128,128]{2,1,0:T(8,128)(2,1)S(1)} %get-tuple-element.28), channel_id=1, source_target_pairs={{0,128},{64,192},{128,0},{192,64},{1,129},{65,193},{129,1},{193,65... | collective-permute-start | bytes 196616 | tf_op jit(solution)/shard_map/ppermute | solution.py:370
  48.3 11.0 %copy-start.1 = (bf16[1,128,3,4096]{3,1,2,0:T(8,128)(2,1)S(1)}, bf16[1,128,3,4096]{3,1,2,0:T(8,128)(2,1)}, u32[]{:S(2)}) copy-start(bf16[1,128,3,4096]{3,1,2,0:T(8,128)(2,1)} %param.5) | copy-start | bytes 9437188
  48.3 11.0 %collective-permute-start.7 = (bf16[2,128,128]{2,1,0:T(8,128)(2,1)S(1)}, bf16[2,128,128]{2,1,0:T(8,128)(2,1)S(1)}, u32[]{:S(2)}, u32[]{:S(2)}) collective-permute-start(bf16[2,128,128]{2,1,0:T(8,128)(2,1)S(1)} %get-tuple-element.29), channel_id=1, source_target_pairs={{0,192},{64,0},{128,64},{192,128},{1,193},{65,1},{129,65},{193,129... | collective-permute-start | bytes 196616 | tf_op jit(solution)/shard_map/ppermute | solution.py:370
  55.4 17.8 %collective-permute-start.2 = (bf16[2,128,128]{2,1,0:T(8,128)(2,1)S(1)}, bf16[2,128,128]{2,1,0:T(8,128)(2,1)S(1)}, u32[]{:S(2)}, u32[]{:S(2)}) collective-permute-start(bf16[2,128,128]{2,1,0:T(8,128)(2,1)S(1)} %get-tuple-element.23), channel_id=1, source_target_pairs={{0,64},{64,128},{128,192},{192,0},{1,65},{65,129},{129,193},{193,1... | collective-permute-start | bytes 196616 | tf_op jit(solution)/shard_map/ppermute | solution.py:370
  55.8 17.4 %collective-permute-start.3 = (bf16[2,128,128]{2,1,0:T(8,128)(2,1)S(1)}, bf16[2,128,128]{2,1,0:T(8,128)(2,1)S(1)}, u32[]{:S(2)}, u32[]{:S(2)}) collective-permute-start(bf16[2,128,128]{2,1,0:T(8,128)(2,1)S(1)} %get-tuple-element.24), channel_id=1, source_target_pairs={{0,128},{64,192},{128,0},{192,64},{1,129},{65,193},{129,1},{193,65... | collective-permute-start | bytes 196616 | tf_op jit(solution)/shard_map/ppermute | solution.py:370
  57.1 16.1 %collective-permute-start.4 = (bf16[2,128,128]{2,1,0:T(8,128)(2,1)S(1)}, bf16[2,128,128]{2,1,0:T(8,128)(2,1)S(1)}, u32[]{:S(2)}, u32[]{:S(2)}) collective-permute-start(bf16[2,128,128]{2,1,0:T(8,128)(2,1)S(1)} %get-tuple-element.25), channel_id=1, source_target_pairs={{0,192},{64,0},{128,64},{192,128},{1,193},{65,1},{129,65},{193,129... | collective-permute-start | bytes 196616 | tf_op jit(solution)/shard_map/ppermute | solution.py:370

commit v5 on v4

--- a/solution.py
+++ b/solution.py
@@ -36,9 +36,8 @@
     if forward:
         return pltpu.roll(tile, 0, 1, stride=WIRE, stride_axis=0)
     row = lax.broadcasted_iota(jnp.int32, (8, LANES), 0)
-    for bit in (1, 2, 4):
-        tile = jnp.where((row & bit) != 0, pltpu.roll(tile, LANES - WIRE * bit, 1), tile)
-    return tile
+    place = lax.broadcasted_iota(jnp.int32, (8, LANES), 1)
+    return jnp.take_along_axis(tile, (place + WIRE * row) % LANES, axis=1)
 
 
 def turn_columns(tile, forward):
@@ -81,7 +80,7 @@
 
 def load_signal(which, proj, above, signal, lane):
     rows = proj.shape[1]
-    signal[which, 0:8] = above[which, :, column(lane)].astype(F32)
+    signal[which, 6:8] = above[which, :, column(lane)].astype(F32)
     signal[which, 8 : 8 + rows] = proj[which, :, column(lane)].astype(F32)
 
 
@@ -89,6 +88,10 @@
     return tree(
         [weights[3 * which + j] * signal[which, 8 + start - j : 8 + start - j + rows] for j in range(2)]
     ) + weights[3 * which + 2] * signal[which, 6 + start : 6 + start + rows]
+
+
+def padded(rows):
+    return jnp.concatenate([rows.astype(F32), jnp.zeros((6, rows.shape[1]), F32)], 0)
 
 
 def decay_of(par):
@@ -127,9 +130,14 @@
         tap_grad[i] = lines[3 * i : 3 * i + 3]
 
 
-def state_kernel(where, proj, above, cot, wire, par, send1, send2, send3, signal, xs, gs, wires):
+def by_core(core, own, other):
+    return jnp.where(core == 0, own, other), jnp.where(core == 0, other, own)
+
+
+def state_kernel(where, proj, above, cot, wire, wire_pair, par, send1, send2, send3, signal, xs, gs, wires):
     chunk = cot.shape[0]
-    wires[...] = wire[...].astype(F32).reshape(wires.shape)
+    both = by_core(where[1], wire[...].astype(F32), wire_pair[...].astype(F32))
+    wires[...] = jnp.stack(both, axis=1).reshape(wires.shape)
     early = lax.broadcasted_iota(jnp.int32, (8, LANES), 0) < 6
 
     for lane in range(8):
@@ -141,7 +149,7 @@
         par[tile_rows(4, lane), :] = parts[6] + parts[7]
         par[tile_rows(5, lane), :] = jnp.broadcast_to(parts[3][6:7] + parts[3][7:8], (8, LANES))
 
-    @pl.loop(0, 8)
+    @pl.loop(0, 8, unroll=2)
     def _(lane):
         weights = tap_weights(par, lane)
         for i in range(3):
@@ -175,16 +183,16 @@
 
 def final_kernel(*refs):
     (where, proj, above, below, cot, par, got1, got2, got3, *rest) = refs
-    (out, proj_grad, sums_out, signal, tails, fgrads, xs, gs, ys, bs, queries_s, keys_s, values_s, held, sums, lines_s) = rest[-16:]
+    (out, proj_grad, sums_own, sums_pair, signal, tails, fgrads, xs, gs, ys, bs, queries_s, keys_s, values_s, held, sums, lines_s) = rest[-17:]
     chunk = cot.shape[0]
     tiles = chunk // 8
 
-    @pl.loop(0, 8)
+    @pl.loop(0, 8, unroll=2)
     def _(lane):
         weights = tap_weights(par, lane)
         for i in range(3):
             load_signal(i, proj, above, signal.at[lane], lane)
-            signal[lane, i, 8 + chunk :] = below[i, :, column(lane)].astype(F32)
+            signal[lane, i, 8 + chunk :] = padded(below[i, :, column(lane)])
         here = signal.at[lane]
         queries, keys, values = (taps(i, here, weights, 0, chunk + 8) for i in range(3))
         gated = rounded(keys * values)
@@ -196,7 +204,7 @@
             if tile < tiles:
                 upstream = cot[rows, column(lane)].astype(F32)
             else:
-                upstream = below[3, :, column(lane)].astype(F32)
+                upstream = padded(below[3, :, column(lane)])
             xs[tile_rows(tile, lane), :] = gated[rows]
             gs[tile_rows(tile, lane), :] = rounded(upstream * queries[rows])
 
@@ -265,11 +273,11 @@
 
     two = lax.broadcasted_iota(jnp.int32, (8, LANES), 0) < 2
 
-    @pl.loop(0, 8)
+    @pl.loop(0, 8, unroll=2)
     def _(lane):
         weights = tap_weights(par, lane)
         upstream = cot[:, column(lane)].astype(F32)
-        tail_up = below[3, :, column(lane)].astype(F32)
+        tail_up = padded(below[3, :, column(lane)])
         convolved = rounded(jnp.concatenate([ys[tile_rows(t, lane), :] for t in range(tiles)], 0))
         gated_grad = rounded(jnp.concatenate([bs[tile_rows(t, lane), :] for t in range(tiles)], 0))
         tail_conv = rounded(jnp.where(two, ys[tile_rows(tiles, lane), :], 0.0))
@@ -298,7 +306,8 @@
         for q in range(SUM_ROWS // 8):
             lines_s[pl.ds(lane * 64 + q, 8, stride=8), :] = lines_of_rows(sums[tile_rows(q, lane), :])
 
-    sums_out[...] = lines_s[...].reshape(64, 8, LANES)[:, : SUM_ROWS // 8].astype(BF)
+    lines = lines_s[...].reshape(32, 2, 8, LANES)[:, :, : SUM_ROWS // 8].astype(BF)
+    sums_own[...], sums_pair[...] = by_core(where[1], lines[:, 0], lines[:, 1])
 
 
 def body(names, proj, short_weight, residue, log_decay, cotangent):
@@ -310,21 +319,32 @@
     blocks = channels // WIDE
     runs = 2 if blocks % 2 == 0 else 1
     steps = blocks // runs
-    where = lax.axis_index(ctx).astype(jnp.int32).reshape(1)
+    zero = devices[1]
+    n_zero = n_dev // n_ctx
+    where = jnp.stack([lax.axis_index(ctx), lax.axis_index(zero) % 2]).astype(jnp.int32)
+    cores = [[i for i in range(n_dev) if i % 2 == c] for c in range(2)]
+
+    def from_all(values):
+        return lax.all_to_all(values, devices, 0, 0, tiled=True, axis_index_groups=cores)
+
+    def from_pair(values):
+        return lax.ppermute(values, zero, [(i, i ^ 1) for i in range(n_zero)])
+
 
     spread = pl.pallas_call(
         spread_kernel,
-        out_shape=jax.ShapeDtypeStruct((n_dev, WIRE_ROWS // 8, 8 * own), BF),
+        out_shape=jax.ShapeDtypeStruct((n_dev // 2, WIRE_ROWS // 8, 8 * own), BF),
         name="spread",
     )(short_weight, residue, log_decay)
-    wire = lax.all_to_all(spread, devices, 0, 0, tiled=True)
+    wire = from_all(spread)
+    wire_pair = from_pair(wire)
 
     signal = proj[0].transpose(1, 0, 2)
     upstream = cotangent[0]
     right = [(i, i + 1) for i in range(n_ctx - 1)]
     left = [(i + 1, i) for i in range(n_ctx - 1)]
-    above = lax.ppermute(signal[:, chunk - 8 :], ctx, right)
-    below = lax.ppermute(jnp.concatenate([signal[:, :8], upstream[None, :8]], 0), ctx, left)
+    above = lax.ppermute(signal[:, chunk - 2 :], ctx, right)
+    below = lax.ppermute(jnp.concatenate([signal[:, :2], upstream[None, :2]], 0), ctx, left)
 
     def shape(dims, kind):
         return jax.ShapeDtypeStruct(dims, kind)
@@ -340,7 +360,7 @@
             return pl.BlockSpec(dims + (WIDE,), lambda i: (0,) * lead + (i + run * steps,))
 
         def rows(count):
-            return pl.BlockSpec((WIDE // own, count // 8, 8 * own), lambda i: (i + run * steps, 0, 0))
+            return pl.BlockSpec((WIDE // own // 2, count // 8, 8 * own), lambda i: (i + run * steps, 0, 0))
 
         def whole(count):
             return pl.BlockSpec((None, count, LANES), lambda i: (i, 0, 0))
@@ -353,7 +373,7 @@
         par, *sent = pl.pallas_call(
             state_kernel,
             grid=(steps,),
-            in_specs=[scalar, wide(3, chunk), wide(3, 8), wide(chunk), rows(WIRE_ROWS)],
+            in_specs=[scalar, wide(3, chunk), wide(3, 2), wide(chunk), rows(WIRE_ROWS), rows(WIRE_ROWS)],
             out_specs=[whole(8 * PAR_ROWS)] + [whole(8 * ORDER)] * 3,
             out_shape=[shape((steps, 8 * PAR_ROWS, LANES), F32)]
             + [shape((steps, 8 * ORDER, LANES), BF)] * 3,
@@ -363,7 +383,7 @@
             compiler_params=params,
             cost_estimate=pl.CostEstimate(flops=4 * 10**9, bytes_accessed=4 * 10**6, transcendentals=0),
             name="states",
-        )(where, signal, above, upstream, wire)
+        )(where, signal, above, upstream, wire, wire_pair)
         pars.append(par)
         gots.append(
             [
@@ -375,8 +395,7 @@
     results = [
         shape((chunk, channels), BF),
         shape((3, chunk, channels), BF),
-        shape((n_dev, SUM_ROWS // 8, 8 * own), BF),
-    ]
+    ] + [shape((n_dev // 2, SUM_ROWS // 8, 8 * own), BF)] * 2
     made = []
     longer = chunk + 8
     for run in range(runs):
@@ -384,10 +403,10 @@
         made = pl.pallas_call(
             final_kernel,
             grid=(steps,),
-            in_specs=[scalar, wide(3, chunk), wide(3, 8), wide(4, 8), wide(chunk), whole(8 * PAR_ROWS)]
+            in_specs=[scalar, wide(3, chunk), wide(3, 2), wide(4, 2), wide(chunk), whole(8 * PAR_ROWS)]
             + [whole(8 * ORDER)] * 3
             + [anywhere] * len(made),
-            out_specs=[wide(chunk), wide(3, chunk), rows(SUM_ROWS)],
+            out_specs=[wide(chunk), wide(3, chunk), rows(SUM_ROWS), rows(SUM_ROWS)],
             out_shape=results,
             scratch_shapes=[
                 vmem(8, 3, chunk + 16, LANES), vmem(8, LANES), vmem(3, longer, LANES),
@@ -401,9 +420,10 @@
             cost_estimate=pl.CostEstimate(flops=8 * 10**9, bytes_accessed=8 * 10**6, transcendentals=0),
             name="final",
         )(where, signal, above, below, upstream, pars[run], *gots[run], *made)
-    out, proj_grad, parts = made
-
-    arrived = lax.all_to_all(parts, devices, 0, 0, tiled=True)
+    out, proj_grad, parts_own, parts_pair = made
+
+    pair_sum = parts_own.astype(F32) + from_pair(parts_pair).astype(F32)
+    arrived = from_all(pair_sum.astype(BF))
     tap_grad, residue_grad, decay_grad = pl.pallas_call(
         functools.partial(collect_kernel, 1.0 / seq),
         out_shape=[shape((3, SHORT, own), F32), shape((ORDER, own), F32), shape((ORDER, own), F32)],

time: 120 us -> 108 us (0.900)
  blocking collectives: 30.2 us -> 18.4 us
  waiting for transfers between devices: 15 us -> 7.88 us
  starting transfers between devices: 27.6 us -> 33.8 us
    all_to_all x1, blocking collectives: 30.2 us -> 18.4 us  [from_all(): lax.all_to_all(values, devices, 0, 0, tiled=True, axis_index_groups=cores)]
    ppermute x2 -> x4, waiting for transfers between devices: 6.29 us -> 1.17 us  [the longest x2 1.16 us: from_pair(): return lax.ppermute(values, zero, [(i, i ^ 1) for i in range(n_zero)])]
    ppermute x2 -> x4, starting transfers between devices: 4.71 us -> 8.89 us  [the longest x2 5.02 us: from_pair(): return lax.ppermute(values, zero, [(i, i ^ 1) for i in range(n_zero)])]
    all_to_all x1, waiting for transfers between devices: 8.7 us -> 6.7 us  [from_all(): lax.all_to_all(values, devices, 0, 0, tiled=True, axis_index_groups=cores)]
    ppermute x6, starting transfers between devices: 7.25 us -> 8.61 us  [body(): lax.ppermute(values, ctx, [(i, (i + k) % n_ctx) for i in range(n_ctx)])]
    unnamed x6 -> x4, local copies, waits for them, and re-layouts: 3.12 us -> 3.11 us
  transfers between devices with their start and end apart: 9 -> 11, of which waited for: 2 -> 2; matrix products, arithmetic and copies ran while one was open for 2% -> 2% of each run, Pallas kernels for 19% -> 22%
where the time goes in v5:
time: 108 us; the launch traced here: 107 us
  Pallas kernels  40.9 us (38%)
  starting transfers between devices  33.8 us (31%)
  blocking collectives  18.4 us (17%)
  waiting for transfers between devices  7.88 us (7%)
  local copies, waits for them, and re-layouts  5.07 us (5%)
    pallas_call x2, Pallas kernels, body(): pl.pallas_call(final_kernel, grid=(steps,), in_specs=[scalar, wide(3, chu...  27.5 us
    all_to_all x1, blocking collectives, from_all(): lax.all_to_all(values, devices, 0, 0, tiled=True, axis_index_groups=cores)  18.4 us
    all_to_all x1, starting transfers between devices, from_all(): lax.all_to_all(values, devices, 0, 0, tiled=True, axis_index_groups=cores)  16.3 us
    pallas_call x2, Pallas kernels, body(): pl.pallas_call(state_kernel, grid=(steps,), in_specs=[scalar, wide(3, chu...  10.1 us
    ppermute x6, starting transfers between devices, body(): lax.ppermute(values, ctx, [(i, (i + k) % n_ctx) for i in range(n_ctx)])  8.61 us
    all_to_all x1, waiting for transfers between devices, from_all(): lax.all_to_all(values, devices, 0, 0, tiled=True, axis_index_groups=cores)  6.7 us
    ppermute x2, starting transfers between devices, from_pair(): return lax.ppermute(values, zero, [(i, i ^ 1) for i in range(n_zero)])  5.02 us
    unnamed x4, local copies, waits for them, and re-layouts  3.11 us
  transfers between devices with their start and end apart: 11, of which 2 were waited for; matrix products, arithmetic and copies ran while one was open for 2% of the time, Pallas kernels for 22%

profile of v5, /device:TPU:1, one launch (start us, length us, event | category | flops | bytes accessed | tf_op | source)
XLA Modules:
  0.0 107.1 jit_solution(5067350080502104591)
XLA Ops:
  0.6 1.5 %spread.1 = bf16[128,8,128]{2,1,0:T(8,128)(2,1)} custom-call(f32[3,3,16]{2,1,0:T(4,128)} %short_weight.1, f32[16,16]{1,0:T(8,128)} %residue.3, f32[16,16]{1,0:T(8,128)} %log_decay.3), custom_call_target="tpu_custom_call" | custom-call | tf_op jit(solution)/shard_map/spread/pallas_call | solution.py:334
  2.2 16.3 %all-to-all-start = ((bf16[128,8,128]{2,1,0:T(8,128)(2,1)}), bf16[128,8,128]{2,1,0:T(8,128)(2,1)S(1)}, u32[]{:S(2)}, u32[]{:S(2)}) async-start(bf16[128,8,128]{2,1,0:T(8,128)(2,1)} %spread.1), calls=%async_computation | async-start | bytes 524288 | tf_op jit(solution)/shard_map/all_to_all | solution.py:328
  18.5 1.1 %fusion = (bf16[3,2,4096]{2,1,0:T(2,128)(2,1)S(1)}, bf16[3,2,4096]{2,1,0:T(2,128)(2,1)S(1)}) fusion(bf16[3,128,4096]{2,1,0:T(8,128)(2,1)} %bitcast.10), kind=kLoop, calls=%fused_computation.3 | loop fusion | bytes 196608 | tf_op jit(solution)/shard_map/slice | solution.py:347
  19.6 2.6 %collective-permute-start = (bf16[3,2,4096]{2,1,0:T(2,128)(2,1)S(1)}, bf16[3,2,4096]{2,1,0:T(2,128)(2,1)S(1)}, u32[]{:S(2)}, u32[]{:S(2)}) collective-permute-start(bf16[3,2,4096]{2,1,0:T(2,128)(2,1)S(1)} %get-tuple-element.44), channel_id=1, source_target_pairs={{0,64},{64,128},{128,192},{1,65},{65,129},{129,193},{2,66},{66,130... | collective-permute-start | bytes 147464 | tf_op jit(solution)/shard_map/ppermute | solution.py:346
  22.2 0.9 slice.12
  23.1 6.7 %all-to-all-done.wire = bf16[128,8,128]{2,1,0:T(8,128)(2,1)S(1)} async-done(((bf16[128,8,128]{2,1,0:T(8,128)(2,1)}), bf16[128,8,128]{2,1,0:T(8,128)(2,1)S(1)}, u32[]{:S(2)}, u32[]{:S(2)}) %all-to-all-start) | async-done | bytes 262176 | tf_op jit(solution)/shard_map/all_to_all | solution.py:328
  29.8 3.3 %collective-permute-start.2 = (bf16[128,8,128]{2,1,0:T(8,128)(2,1)S(1)}, bf16[128,8,128]{2,1,0:T(8,128)(2,1)S(1)}, u32[]{:S(2)}, u32[]{:S(2)}) collective-permute-start(bf16[128,8,128]{2,1,0:T(8,128)(2,1)S(1)} %all-to-all-done.wire), channel_id=1, source_target_pairs={{0,1},{1,0},{2,3},{3,2},{4,5},{5,4},{6,7},{7,6},{8,9},{9,8},{10,11... | collective-permute-start | bytes 786440 | tf_op jit(solution)/shard_map/ppermute | solution.py:331
  33.1 0.1 pad_maximum_fusion
  33.2 1.3 %collective-permute-start.1 = (bf16[4,2,4096]{2,1,0:T(2,128)(2,1)S(1)}, bf16[4,2,4096]{2,1,0:T(2,128)(2,1)S(1)}, u32[]{:S(2)}, u32[]{:S(2)}) collective-permute-start(bf16[4,2,4096]{2,1,0:T(2,128)(2,1)S(1)} %pad_maximum_fusion), channel_id=1, source_target_pairs={{64,0},{128,64},{192,128},{65,1},{129,65},{193,129},{66,2},{130,66... | collective-permute-start | bytes 196616 | tf_op jit(solution)/shard_map/ppermute | solution.py:347
  34.5 0.1 pad_add_fusion.where.refs_0_
  34.6 0.0 collective-permute-done.above.refs_2_
  34.6 0.0 collective-permute-done.2.wire_pair
  34.6 0.0 copy-start
  34.6 1.9 %copy-done = bf16[1,128,3,4096]{3,1,2,0:T(8,128)(2,1)S(1)} copy-done((bf16[1,128,3,4096]{3,1,2,0:T(8,128)(2,1)S(1)}, bf16[1,128,3,4096]{3,1,2,0:T(8,128)(2,1)}, u32[]{:S(2)}) %copy-start) | copy-done | bytes 3145752
  36.5 0.0 copy-start.1
  36.5 1.2 %copy-done.1 = bf16[1,128,4096]{2,1,0:T(8,128)(2,1)S(1)} copy-done((bf16[1,128,4096]{2,1,0:T(8,128)(2,1)S(1)}, bf16[1,128,4096]{2,1,0:T(8,128)(2,1)}, u32[]{:S(2)}) %copy-start.1) | copy-done | bytes 1048600
  37.7 5.1 %states.3 = (f32[2,384,128]{2,1,0:T(8,128)S(1)}, bf16[2,128,128]{2,1,0:T(8,128)(2,1)S(1)}, bf16[2,128,128]{2,1,0:T(8,128)(2,1)S(1)}, bf16[2,128,128]{2,1,0:T(8,128)(2,1)S(1)}) custom-call(s32[2]{0:T(128)S(1)} %pad_add_fusion.where.refs_0_, bf16[3,128,4096]{2,1,0:T(8,128)(2,1)S(1)} %bitcast.11, bf16[3,2,4096]{2,1,0:T(2,128)(2,1)S(1)} %collective-permute-done.above.refs_2_, ...), custom_call_target="tpu_custom_call" | custom-call | flops 4000000000 | bytes 4000000 | tf_op jit(solution)/shard_map/states/pallas_call | solution.py:373
  42.8 2.2 %collective-permute-start.6 = (bf16[2,128,128]{2,1,0:T(8,128)(2,1)S(1)}, bf16[2,128,128]{2,1,0:T(8,128)(2,1)S(1)}, u32[]{:S(2)}, u32[]{:S(2)}) collective-permute-start(bf16[2,128,128]{2,1,0:T(8,128)(2,1)S(1)} %get-tuple-element.29), channel_id=1, source_target_pairs={{0,64},{64,128},{128,192},{192,0},{1,65},{65,129},{129,193},{193,1... | collective-permute-start | bytes 196616 | tf_op jit(solution)/shard_map/ppermute | solution.py:390
  44.9 1.0 collective-permute-start.7
  46.0 2.0 %collective-permute-start.8 = (bf16[2,128,128]{2,1,0:T(8,128)(2,1)S(1)}, bf16[2,128,128]{2,1,0:T(8,128)(2,1)S(1)}, u32[]{:S(2)}, u32[]{:S(2)}) collective-permute-start(bf16[2,128,128]{2,1,0:T(8,128)(2,1)S(1)} %get-tuple-element.31), channel_id=1, source_target_pairs={{0,192},{64,0},{128,64},{192,128},{1,193},{65,1},{129,65},{193,129... | collective-permute-start | bytes 196616 | tf_op jit(solution)/shard_map/ppermute | solution.py:390
  48.0 5.1 %states.2 = (f32[2,384,128]{2,1,0:T(8,128)S(1)}, bf16[2,128,128]{2,1,0:T(8,128)(2,1)S(1)}, bf16[2,128,128]{2,1,0:T(8,128)(2,1)S(1)}, bf16[2,128,128]{2,1,0:T(8,128)(2,1)S(1)}) custom-call(s32[2]{0:T(128)S(1)} %pad_add_fusion.where.refs_0_, bf16[3,128,4096]{2,1,0:T(8,128)(2,1)S(1)} %bitcast.12, bf16[3,2,4096]{2,1,0:T(2,128)(2,1)S(1)} %collective-permute-done.above.refs_2_, ...), custom_call_target="tpu_custom_call" | custom-call | flops 4000000000 | bytes 4000000 | tf_op jit(solution)/shard_map/states/pallas_call | solution.py:373
  53.1 0.1 collective-permute-start.3
  53.2 0.0 collective-permute-done.1.refs_3_
  53.2 0.8 collective-permute-start.4
  53.9 0.0 collective-permute-done.6.refs_6_
  53.9 2.6 %collective-permute-start.5 = (bf16[2,128,128]{2,1,0:T(8,128)(2,1)S(1)}, bf16[2,128,128]{2,1,0:T(8,128)(2,1)S(1)}, u32[]{:S(2)}, u32[]{:S(2)}) collective-permute-start(bf16[2,128,128]{2,1,0:T(8,128)(2,1)S(1)} %get-tuple-element.27), channel_id=1, source_target_pairs={{0,192},{64,0},{128,64},{192,128},{1,193},{65,1},{129,65},{193,129... | collective-permute-start | bytes 196616 | tf_op jit(solution)/shard_map/ppermute | solution.py:390
  56.5 0.0 collective-permute-done.7.refs_7_
  56.5 0.0 collective-permute-done.8.refs_8_
  56.5 13.7 %final.2 = (bf16[128,4096]{1,0:T(8,128)(2,1)}, bf16[3,128,4096]{2,1,0:T(8,128)(2,1)}, bf16[128,6,128]{2,1,0:T(8,128)(2,1)S(1)}, bf16[128,6,128]{2,1,0:T(8,128)(2,1)S(1)}) custom-call(s32[2]{0:T(128)S(1)} %pad_add_fusion.where.refs_0_, bf16[3,128,4096]{2,1,0:T(8,128)(2,1)S(1)} %bitcast.13, bf16[3,2,4096]{2,1,0:T(2,128)(2,1)S(1)} %collective-permute-done.above.refs_2_, ...), custom_call_target="tpu_custom_call" | custom-call | flops 8000000000 | bytes 8000000 | tf_op jit(solution)/shard_map/final/pallas_call | solution.py:403
  70.2 0.0 collective-permute-done.3.refs_6_
  70.2 0.0 collective-permute-done.4.refs_7_
  70.2 0.0 collective-permute-done.5.refs_8_
  70.2 13.7 %final.3 = (bf16[128,4096]{1,0:T(8,128)(2,1)}, bf16[3,128,4096]{2,1,0:T(8,128)(2,1)}, bf16[128,6,128]{2,1,0:T(8,128)(2,1)S(1)}, bf16[128,6,128]{2,1,0:T(8,128)(2,1)S(1)}) custom-call(s32[2]{0:T(128)S(1)} %pad_add_fusion.where.refs_0_, bf16[3,128,4096]{2,1,0:T(8,128)(2,1)S(1)} %bitcast.14, ...), custom_call_target="tpu_custom_call", output_to_operand_aliasing={{0}: (9, {}), {1}: (10, {}), {2}: (11, {}), {3}: (12, {})} | custom-call | flops 8000000000 | bytes 8000000 | tf_op jit(solution)/shard_map/final/pallas_call | solution.py:403
  84.0 1.7 %collective-permute-start.9 = (bf16[128,6,128]{2,1,0:T(8,128)(2,1)S(1)}, bf16[128,6,128]{2,1,0:T(8,128)(2,1)S(1)}, u32[]{:S(2)}, u32[]{:S(2)}) collective-permute-start(bf16[128,6,128]{2,1,0:T(8,128)(2,1)S(1)} %get-tuple-element.39), channel_id=1, source_target_pairs={{0,1},{1,0},{2,3},{3,2},{4,5},{5,4},{6,7},{7,6},{8,9},{9,8},{10,11... | collective-permute-start | bytes 589832 | tf_op jit(solution)/shard_map/ppermute | solution.py:331
  85.7 1.2 %collective-permute-done.9 = bf16[128,6,128]{2,1,0:T(8,128)(2,1)S(1)} collective-permute-done((bf16[128,6,128]{2,1,0:T(8,128)(2,1)S(1)}, bf16[128,6,128]{2,1,0:T(8,128)(2,1)S(1)}, u32[]{:S(2)}, u32[]{:S(2)}) %collective-permute-start.9) | collective-permute-done | bytes 196640 | tf_op jit(solution)/shard_map/ppermute | solution.py:331
  86.8 0.1 add_convert_fusion
  86.9 18.4 %all_to_all.10.arrived = bf16[128,6,128]{2,1,0:T(8,128)(2,1)} all-to-all(bf16[128,6,128]{2,1,0:T(8,128)(2,1)S(1)} %add_convert_fusion), channel_id=1, replica_groups={{0,2,4,6,8,10,12,14,16,18,20,22,24,26,28,30,32,34,36,38,40,42,44,46,48,..., dimensions={0} | all-to-all | bytes 393216 | tf_op jit(solution)/shard_map/all_to_all | solution.py:328
  105.3 1.8 %collect.1 = (f32[3,3,16]{2,1,0:T(4,128)}, f32[16,16]{1,0:T(8,128)}, f32[16,16]{1,0:T(8,128)}) custom-call(bf16[128,6,128]{2,1,0:T(8,128)(2,1)} %all_to_all.10.arrived, f32[16,16]{1,0:T(8,128)} %residue.3, f32[16,16]{1,0:T(8,128)} %log_decay.3), custom_call_target="tpu_custom_call" | custom-call | tf_op jit(solution)/shard_map/collect/pallas_call | solution.py:427
Async XLA Ops:
  2.2 27.6 %all-to-all-start = ((bf16[128,8,128]{2,1,0:T(8,128)(2,1)}), bf16[128,8,128]{2,1,0:T(8,128)(2,1)S(1)}, u32[]{:S(2)}, u32[]{:S(2)}) async-start(bf16[128,8,128]{2,1,0:T(8,128)(2,1)} %spread.1), calls=%async_computation | async-start | bytes 524288 | tf_op jit(solution)/shard_map/all_to_all | solution.py:328
  19.6 15.0 %collective-permute-start = (bf16[3,2,4096]{2,1,0:T(2,128)(2,1)S(1)}, bf16[3,2,4096]{2,1,0:T(2,128)(2,1)S(1)}, u32[]{:S(2)}, u32[]{:S(2)}) collective-permute-start(bf16[3,2,4096]{2,1,0:T(2,128)(2,1)S(1)} %get-tuple-element.44), channel_id=1, source_target_pairs={{0,64},{64,128},{128,192},{1,65},{65,129},{129,193},{2,66},{66,130... | collective-permute-start | bytes 147464 | tf_op jit(solution)/shard_map/ppermute | solution.py:346
  29.8 4.8 %collective-permute-start.2 = (bf16[128,8,128]{2,1,0:T(8,128)(2,1)S(1)}, bf16[128,8,128]{2,1,0:T(8,128)(2,1)S(1)}, u32[]{:S(2)}, u32[]{:S(2)}) collective-permute-start(bf16[128,8,128]{2,1,0:T(8,128)(2,1)S(1)} %all-to-all-done.wire), channel_id=1, source_target_pairs={{0,1},{1,0},{2,3},{3,2},{4,5},{5,4},{6,7},{7,6},{8,9},{9,8},{10,11... | collective-permute-start | bytes 786440 | tf_op jit(solution)/shard_map/ppermute | solution.py:331
  33.2 20.0 %collective-permute-start.1 = (bf16[4,2,4096]{2,1,0:T(2,128)(2,1)S(1)}, bf16[4,2,4096]{2,1,0:T(2,128)(2,1)S(1)}, u32[]{:S(2)}, u32[]{:S(2)}) collective-permute-start(bf16[4,2,4096]{2,1,0:T(2,128)(2,1)S(1)} %pad_maximum_fusion), channel_id=1, source_target_pairs={{64,0},{128,64},{192,128},{65,1},{129,65},{193,129},{66,2},{130,66... | collective-permute-start | bytes 196616 | tf_op jit(solution)/shard_map/ppermute | solution.py:347
  34.6 1.9 %copy-start = (bf16[1,128,3,4096]{3,1,2,0:T(8,128)(2,1)S(1)}, bf16[1,128,3,4096]{3,1,2,0:T(8,128)(2,1)}, u32[]{:S(2)}) copy-start(bf16[1,128,3,4096]{3,1,2,0:T(8,128)(2,1)} %param.5) | copy-start | bytes 9437188
  36.5 1.2 %copy-start.1 = (bf16[1,128,4096]{2,1,0:T(8,128)(2,1)S(1)}, bf16[1,128,4096]{2,1,0:T(8,128)(2,1)}, u32[]{:S(2)}) copy-start(bf16[1,128,4096]{2,1,0:T(8,128)(2,1)} %param.9) | copy-start | bytes 3145732
  42.8 11.2 %collective-permute-start.6 = (bf16[2,128,128]{2,1,0:T(8,128)(2,1)S(1)}, bf16[2,128,128]{2,1,0:T(8,128)(2,1)S(1)}, u32[]{:S(2)}, u32[]{:S(2)}) collective-permute-start(bf16[2,128,128]{2,1,0:T(8,128)(2,1)S(1)} %get-tuple-element.29), channel_id=1, source_target_pairs={{0,64},{64,128},{128,192},{192,0},{1,65},{65,129},{129,193},{193,1... | collective-permute-start | bytes 196616 | tf_op jit(solution)/shard_map/ppermute | solution.py:390
  44.9 11.6 %collective-permute-start.7 = (bf16[2,128,128]{2,1,0:T(8,128)(2,1)S(1)}, bf16[2,128,128]{2,1,0:T(8,128)(2,1)S(1)}, u32[]{:S(2)}, u32[]{:S(2)}) collective-permute-start(bf16[2,128,128]{2,1,0:T(8,128)(2,1)S(1)} %get-tuple-element.30), channel_id=1, source_target_pairs={{0,128},{64,192},{128,0},{192,64},{1,129},{65,193},{129,1},{193,65... | collective-permute-start | bytes 196616 | tf_op jit(solution)/shard_map/ppermute | solution.py:390
  46.0 10.5 %collective-permute-start.8 = (bf16[2,128,128]{2,1,0:T(8,128)(2,1)S(1)}, bf16[2,128,128]{2,1,0:T(8,128)(2,1)S(1)}, u32[]{:S(2)}, u32[]{:S(2)}) collective-permute-start(bf16[2,128,128]{2,1,0:T(8,128)(2,1)S(1)} %get-tuple-element.31), channel_id=1, source_target_pairs={{0,192},{64,0},{128,64},{192,128},{1,193},{65,1},{129,65},{193,129... | collective-permute-start | bytes 196616 | tf_op jit(solution)/shard_map/ppermute | solution.py:390
  53.1 17.2 %collective-permute-start.3 = (bf16[2,128,128]{2,1,0:T(8,128)(2,1)S(1)}, bf16[2,128,128]{2,1,0:T(8,128)(2,1)S(1)}, u32[]{:S(2)}, u32[]{:S(2)}) collective-permute-start(bf16[2,128,128]{2,1,0:T(8,128)(2,1)S(1)} %get-tuple-element.25), channel_id=1, source_target_pairs={{0,64},{64,128},{128,192},{192,0},{1,65},{65,129},{129,193},{193,1... | collective-permute-start | bytes 196616 | tf_op jit(solution)/shard_map/ppermute | solution.py:390
  53.2 17.1 %collective-permute-start.4 = (bf16[2,128,128]{2,1,0:T(8,128)(2,1)S(1)}, bf16[2,128,128]{2,1,0:T(8,128)(2,1)S(1)}, u32[]{:S(2)}, u32[]{:S(2)}) collective-permute-start(bf16[2,128,128]{2,1,0:T(8,128)(2,1)S(1)} %get-tuple-element.26), channel_id=1, source_target_pairs={{0,128},{64,192},{128,0},{192,64},{1,129},{65,193},{129,1},{193,65... | collective-permute-start | bytes 196616 | tf_op jit(solution)/shard_map/ppermute | solution.py:390
  53.9 16.3 %collective-permute-start.5 = (bf16[2,128,128]{2,1,0:T(8,128)(2,1)S(1)}, bf16[2,128,128]{2,1,0:T(8,128)(2,1)S(1)}, u32[]{:S(2)}, u32[]{:S(2)}) collective-permute-start(bf16[2,128,128]{2,1,0:T(8,128)(2,1)S(1)} %get-tuple-element.27), channel_id=1, source_target_pairs={{0,192},{64,0},{128,64},{192,128},{1,193},{65,1},{129,65},{193,129... | collective-permute-start | bytes 196616 | tf_op jit(solution)/shard_map/ppermute | solution.py:390
  84.0 2.8 %collective-permute-start.9 = (bf16[128,6,128]{2,1,0:T(8,128)(2,1)S(1)}, bf16[128,6,128]{2,1,0:T(8,128)(2,1)S(1)}, u32[]{:S(2)}, u32[]{:S(2)}) collective-permute-start(bf16[128,6,128]{2,1,0:T(8,128)(2,1)S(1)} %get-tuple-element.39), channel_id=1, source_target_pairs={{0,1},{1,0},{2,3},{3,2},{4,5},{5,4},{6,7},{7,6},{8,9},{9,8},{10,11... | collective-permute-start | bytes 589832 | tf_op jit(solution)/shard_map/ppermute | solution.py:331

commit v6 on v5

--- a/solution.py
+++ b/solution.py
@@ -90,8 +90,17 @@
     ) + weights[3 * which + 2] * signal[which, 6 + start : 6 + start + rows]
 
 
-def padded(rows):
-    return jnp.concatenate([rows.astype(F32), jnp.zeros((6, rows.shape[1]), F32)], 0)
+def head_rows(parts):
+    row = lax.broadcasted_iota(jnp.int32, (8, LANES), 0)
+    made = parts[0]
+    for i in range(1, 4):
+        made = jnp.where(row >= 2 * i, pltpu.roll(parts[i], 2 * i, 0), made)
+    return made
+
+
+def padded(tails, lane, which):
+    rows = tails[pl.ds(pl.multiple_of(lane * 8, 8), 8), :][2 * which : 2 * which + 2]
+    return jnp.concatenate([rows, jnp.zeros((6, LANES), F32)], 0)
 
 
 def decay_of(par):
@@ -134,7 +143,7 @@
     return jnp.where(core == 0, own, other), jnp.where(core == 0, other, own)
 
 
-def state_kernel(where, proj, above, cot, wire, wire_pair, par, send1, send2, send3, signal, xs, gs, wires):
+def state_kernel(where, proj, above, cot, wire, wire_pair, par, send1, send2, send3, signal, xs, gs, wires, halo):
     chunk = cot.shape[0]
     both = by_core(where[1], wire[...].astype(F32), wire_pair[...].astype(F32))
     wires[...] = jnp.stack(both, axis=1).reshape(wires.shape)
@@ -156,7 +165,10 @@
             load_signal(i, proj, above, signal, lane)
         queries, keys, values = (taps(i, signal, weights, 0, chunk) for i in range(3))
         gated = rounded(keys * values)
-        gate_grad = rounded(cot[:, column(lane)].astype(F32) * queries)
+        upstream = cot[:, column(lane)].astype(F32)
+        gate_grad = rounded(upstream * queries)
+        first = [signal[i, 8:16] for i in range(3)] + [upstream[0:8]]
+        halo[pl.ds(pl.multiple_of(lane * 8, 8), 8), :] = head_rows(first)
         for tile in range(chunk // 8):
             xs[tile_rows(tile, lane), :] = gated[8 * tile : 8 * tile + 8]
             gs[tile_rows(tile, lane), :] = gate_grad[8 * tile : 8 * tile + 8]
@@ -174,6 +186,7 @@
 
     zero = tuple(jnp.zeros((8, LANES), F32) for _ in range(ORDER))
     forward, backward = lax.fori_loop(0, chunk // 8, step, (zero, zero), unroll=2)
+    send3[8 * ORDER :, :] = halo[...].astype(BF)
     for away, send in zip((1, 2, 3), (send1, send2, send3)):
         ahead = where[0] + away < 4
         for m in range(0, ORDER, 2):
@@ -182,17 +195,19 @@
 
 
 def final_kernel(*refs):
-    (where, proj, above, below, cot, par, got1, got2, got3, *rest) = refs
+    (where, proj, above, cot, par, got1, got2, got3, *rest) = refs
     (out, proj_grad, sums_own, sums_pair, signal, tails, fgrads, xs, gs, ys, bs, queries_s, keys_s, values_s, held, sums, lines_s) = rest[-17:]
     chunk = cot.shape[0]
     tiles = chunk // 8
+    follows = jnp.where(where[0] < 3, 1.0, 0.0)
+    tails[...] = got3[8 * ORDER :, :].astype(F32) * follows
 
     @pl.loop(0, 8, unroll=2)
     def _(lane):
         weights = tap_weights(par, lane)
         for i in range(3):
             load_signal(i, proj, above, signal.at[lane], lane)
-            signal[lane, i, 8 + chunk :] = padded(below[i, :, column(lane)])
+            signal[lane, i, 8 + chunk :] = padded(tails, lane, i)
         here = signal.at[lane]
         queries, keys, values = (taps(i, here, weights, 0, chunk + 8) for i in range(3))
         gated = rounded(keys * values)
@@ -204,7 +219,7 @@
             if tile < tiles:
                 upstream = cot[rows, column(lane)].astype(F32)
             else:
-                upstream = padded(below[3, :, column(lane)])
+                upstream = padded(tails, lane, 3)
             xs[tile_rows(tile, lane), :] = gated[rows]
             gs[tile_rows(tile, lane), :] = rounded(upstream * queries[rows])
 
@@ -277,7 +292,7 @@
     def _(lane):
         weights = tap_weights(par, lane)
         upstream = cot[:, column(lane)].astype(F32)
-        tail_up = padded(below[3, :, column(lane)])
+        tail_up = padded(tails, lane, 3)
         convolved = rounded(jnp.concatenate([ys[tile_rows(t, lane), :] for t in range(tiles)], 0))
         gated_grad = rounded(jnp.concatenate([bs[tile_rows(t, lane), :] for t in range(tiles)], 0))
         tail_conv = rounded(jnp.where(two, ys[tile_rows(tiles, lane), :], 0.0))
@@ -336,15 +351,11 @@
         out_shape=jax.ShapeDtypeStruct((n_dev // 2, WIRE_ROWS // 8, 8 * own), BF),
         name="spread",
     )(short_weight, residue, log_decay)
+    signal, spread = lax.optimization_barrier((proj[0].transpose(1, 0, 2), spread))
     wire = from_all(spread)
-    wire_pair = from_pair(wire)
-
-    signal = proj[0].transpose(1, 0, 2)
+
     upstream = cotangent[0]
-    right = [(i, i + 1) for i in range(n_ctx - 1)]
-    left = [(i + 1, i) for i in range(n_ctx - 1)]
-    above = lax.ppermute(signal[:, chunk - 2 :], ctx, right)
-    below = lax.ppermute(jnp.concatenate([signal[:, :2], upstream[None, :2]], 0), ctx, left)
+    above = lax.ppermute(signal[:, chunk - 2 :], ctx, [(i, i + 1) for i in range(n_ctx - 1)])
 
     def shape(dims, kind):
         return jax.ShapeDtypeStruct(dims, kind)
@@ -365,25 +376,37 @@
         def whole(count):
             return pl.BlockSpec((None, count, LANES), lambda i: (i, 0, 0))
 
-        return wide, rows, whole
-
+        def local(*dims):
+            lead = len(dims)
+            return pl.BlockSpec(dims + (WIDE,), lambda i: (0,) * lead + (i,))
+
+        return wide, rows, whole, local
+
+    width = steps * WIDE
+    signals = [signal[:, :, run * width : run * width + width] for run in range(runs)]
+    upstreams = [upstream[:, run * width : run * width + width] for run in range(runs)]
+
+    wire, above, signals, upstreams = lax.optimization_barrier((wire, above, signals, upstreams))
+    wire_pair = from_pair(wire)
+    sizes = (8 * ORDER, 8 * ORDER, 8 * ORDER + 64)
     pars, gots = [], []
     for run in range(runs):
-        wide, rows, whole = specs(run)
+        wide, rows, whole, local = specs(run)
         par, *sent = pl.pallas_call(
             state_kernel,
             grid=(steps,),
-            in_specs=[scalar, wide(3, chunk), wide(3, 2), wide(chunk), rows(WIRE_ROWS), rows(WIRE_ROWS)],
-            out_specs=[whole(8 * PAR_ROWS)] + [whole(8 * ORDER)] * 3,
+            in_specs=[scalar, local(3, chunk), wide(3, 2), local(chunk), rows(WIRE_ROWS), rows(WIRE_ROWS)],
+            out_specs=[whole(8 * PAR_ROWS)] + [whole(n) for n in sizes],
             out_shape=[shape((steps, 8 * PAR_ROWS, LANES), F32)]
-            + [shape((steps, 8 * ORDER, LANES), BF)] * 3,
+            + [shape((steps, n, LANES), BF) for n in sizes],
             scratch_shapes=[
                 vmem(3, chunk + 8, LANES), vmem(chunk * 8, LANES), vmem(chunk * 8, LANES), vmem(512, LANES),
+                vmem(64, LANES),
             ],
             compiler_params=params,
             cost_estimate=pl.CostEstimate(flops=4 * 10**9, bytes_accessed=4 * 10**6, transcendentals=0),
             name="states",
-        )(where, signal, above, upstream, wire, wire_pair)
+        )(where, signals[run], above, upstreams[run], wire, wire_pair)
         pars.append(par)
         gots.append(
             [
@@ -399,27 +422,27 @@
     made = []
     longer = chunk + 8
     for run in range(runs):
-        wide, rows, whole = specs(run)
+        wide, rows, whole, local = specs(run)
         made = pl.pallas_call(
             final_kernel,
             grid=(steps,),
-            in_specs=[scalar, wide(3, chunk), wide(3, 2), wide(4, 2), wide(chunk), whole(8 * PAR_ROWS)]
-            + [whole(8 * ORDER)] * 3
+            in_specs=[scalar, local(3, chunk), wide(3, 2), local(chunk), whole(8 * PAR_ROWS)]
+            + [whole(n) for n in sizes]
             + [anywhere] * len(made),
             out_specs=[wide(chunk), wide(3, chunk), rows(SUM_ROWS), rows(SUM_ROWS)],
             out_shape=results,
             scratch_shapes=[
-                vmem(8, 3, chunk + 16, LANES), vmem(8, LANES), vmem(3, longer, LANES),
+                vmem(8, 3, chunk + 16, LANES), vmem(64, LANES), vmem(3, longer, LANES),
                 vmem(longer * 8, LANES), vmem(longer * 8, LANES),
                 vmem(longer * 8, LANES), vmem(longer * 8, LANES),
                 vmem(8, longer, LANES), vmem(8, longer, LANES), vmem(8, longer, LANES),
                 vmem(chunk, HALF, 8, LANES), vmem(8 * SUM_ROWS, LANES), vmem(512, LANES),
             ],
-            input_output_aliases={9 + i: i for i in range(len(made))},
+            input_output_aliases={8 + i: i for i in range(len(made))},
             compiler_params=params,
             cost_estimate=pl.CostEstimate(flops=8 * 10**9, bytes_accessed=8 * 10**6, transcendentals=0),
             name="final",
-        )(where, signal, above, below, upstream, pars[run], *gots[run], *made)
+        )(where, signals[run], above, upstreams[run], pars[run], *gots[run], *made)
     out, proj_grad, parts_own, parts_pair = made
 
     pair_sum = parts_own.astype(F32) + from_pair(parts_pair).astype(F32)

time: 108 us -> 105 us (0.972)
  starting transfers between devices: 33.8 us -> 31.7 us
  waiting for transfers between devices: 7.88 us -> 6.73 us
    all_to_all x1, waiting for transfers between devices: 6.7 us -> 4.33 us  [from_all(): lax.all_to_all(values, devices, 0, 0, tiled=True, axis_index_groups=cores)]
    slice x2 -> x3, local copies, waits for them, and re-layouts: 1.96 us -> 4.17 us  [the longest x1 2.11 us: body(): signal[:, :, run * width:run * width + width]]
    unnamed x4 -> x8, local copies, waits for them, and re-layouts: 3.11 us -> 1.05 us
    ppermute x6, starting transfers between devices: 8.61 us -> 7.25 us  [body(): lax.ppermute(values, ctx, [(i, (i + k) % n_ctx) for i in range(n_ctx)])]
    ppermute x2, waiting for transfers between devices: 1.16 us -> 2.38 us  [from_pair(): return lax.ppermute(values, zero, [(i, i ^ 1) for i in range(n_zero)])]
    ppermute x2 -> x1, starting transfers between devices: 3.87 us -> 2.71 us  [body(): lax.ppermute(signal[:, chunk - 2:], ctx, [(i, i + 1) for i in range(n_ctx...]
  transfers between devices with their start and end apart: 11 -> 10, of which waited for: 2 -> 3; matrix products, arithmetic and copies ran while one was open for 2% -> 4% of each run, Pallas kernels for 22% -> 18%
where the time goes in v6:
time: 105 us; the launch traced here: 104 us
  Pallas kernels  41.7 us (40%)
  starting transfers between devices  31.7 us (30%)
  blocking collectives  18 us (17%)
  waiting for transfers between devices  6.73 us (6%)
  local copies, waits for them, and re-layouts  5.22 us (5%)
    pallas_call x2, Pallas kernels, body(): pl.pallas_call(final_kernel, grid=(steps,), in_specs=[scalar, local(3, ch...  27.5 us
    all_to_all x1, blocking collectives, from_all(): lax.all_to_all(values, devices, 0, 0, tiled=True, axis_index_groups=cores)  18 us
    all_to_all x1, starting transfers between devices, from_all(): lax.all_to_all(values, devices, 0, 0, tiled=True, axis_index_groups=cores)  16.3 us
    pallas_call x2, Pallas kernels, body(): pl.pallas_call(state_kernel, grid=(steps,), in_specs=[scalar, local(3, ch...  10.9 us
    ppermute x6, starting transfers between devices, body(): lax.ppermute(values, ctx, [(i, (i + k) % n_ctx) for i in range(n_ctx)])  7.25 us
    ppermute x2, starting transfers between devices, from_pair(): return lax.ppermute(values, zero, [(i, i ^ 1) for i in range(n_zero)])  5.39 us
    all_to_all x1, waiting for transfers between devices, from_all(): lax.all_to_all(values, devices, 0, 0, tiled=True, axis_index_groups=cores)  4.33 us
    ppermute x1, starting transfers between devices, body(): lax.ppermute(signal[:, chunk - 2:], ctx, [(i, i + 1) for i in range(n_ctx...  2.71 us
  transfers between devices with their start and end apart: 10, of which 3 were waited for; matrix products, arithmetic and copies ran while one was open for 4% of the time, Pallas kernels for 18%

profile of v6, /device:TPU:1, one launch (start us, length us, event | category | flops | bytes accessed | tf_op | source)
XLA Modules:
  0.0 104.2 jit_solution(10922522042166085121)
XLA Ops:
  0.6 1.5 %spread.1 = bf16[128,8,128]{2,1,0:T(8,128)(2,1)} custom-call(f32[3,3,16]{2,1,0:T(4,128)} %short_weight.1, f32[16,16]{1,0:T(8,128)} %residue.3, f32[16,16]{1,0:T(8,128)} %log_decay.3), custom_call_target="tpu_custom_call" | custom-call | tf_op jit(solution)/shard_map/spread/pallas_call | solution.py:349
  2.2 16.3 %all-to-all-start = ((bf16[128,8,128]{2,1,0:T(8,128)(2,1)}), bf16[128,8,128]{2,1,0:T(8,128)(2,1)S(1)}, u32[]{:S(2)}, u32[]{:S(2)}) async-start(bf16[128,8,128]{2,1,0:T(8,128)(2,1)} %spread.1), calls=%async_computation | async-start | bytes 524288 | tf_op jit(solution)/shard_map/all_to_all | solution.py:343
  18.5 1.0 slice.15
  19.5 0.0 copy-start.3
  19.5 2.7 %collective-permute-start = (bf16[3,2,4096]{2,1,0:T(2,128)(2,1)S(1)}, bf16[3,2,4096]{2,1,0:T(2,128)(2,1)S(1)}, u32[]{:S(2)}, u32[]{:S(2)}) collective-permute-start(bf16[3,2,4096]{2,1,0:T(2,128)(2,1)S(1)} %slice.15), channel_id=1, source_target_pairs={{0,64},{64,128},{128,192},{1,65},{65,129},{129,193},{2,66},{66,130... | collective-permute-start | bytes 147464 | tf_op jit(solution)/shard_map/ppermute | solution.py:358
  22.2 2.1 %fusion = (bf16[3,128,2048]{2,1,0:T(8,128)(2,1)S(1)}, bf16[3,128,2048]{2,1,0:T(8,128)(2,1)S(1)}) fusion(bf16[3,128,4096]{2,1,0:T(8,128)(2,1)} %bitcast.11), kind=kLoop, calls=%fused_computation.2 | loop fusion | bytes 6291456 | tf_op jit(solution)/shard_map/slice | solution.py:386
  24.3 0.0 copy-done.3
  24.3 1.1 %fusion.1 = (bf16[128,2048]{1,0:T(8,128)(2,1)}, bf16[128,2048]{1,0:T(8,128)(2,1)}) fusion(bf16[128,4096]{1,0:T(8,128)(2,1)S(1)} %bitcast.12), kind=kLoop, calls=%fused_computation.3 | loop fusion | bytes 2097152 | tf_op jit(solution)/shard_map/slice | solution.py:387
  25.4 0.0 collective-permute-done.above.refs_2_
  25.4 4.3 %all-to-all-done.wire = bf16[128,8,128]{2,1,0:T(8,128)(2,1)S(1)} async-done(((bf16[128,8,128]{2,1,0:T(8,128)(2,1)}), bf16[128,8,128]{2,1,0:T(8,128)(2,1)S(1)}, u32[]{:S(2)}, u32[]{:S(2)}) %all-to-all-start) | async-done | bytes 262176 | tf_op jit(solution)/shard_map/all_to_all | solution.py:343
  29.8 3.3 %collective-permute-start.1 = (bf16[128,8,128]{2,1,0:T(8,128)(2,1)S(1)}, bf16[128,8,128]{2,1,0:T(8,128)(2,1)}, u32[]{:S(2)}, u32[]{:S(2)}) collective-permute-start(bf16[128,8,128]{2,1,0:T(8,128)(2,1)S(1)} %all-to-all-done.wire), channel_id=1, source_target_pairs={{0,1},{1,0},{2,3},{3,2},{4,5},{5,4},{6,7},{7,6},{8,9},{9,8},{10,11... | collective-permute-start | bytes 786440 | tf_op jit(solution)/shard_map/ppermute | solution.py:346
  33.1 0.1 pad_add_fusion.where.refs_0_
  33.2 0.0 copy-start
  33.2 1.2 %collective-permute-done.1.wire_pair = bf16[128,8,128]{2,1,0:T(8,128)(2,1)} collective-permute-done((bf16[128,8,128]{2,1,0:T(8,128)(2,1)S(1)}, bf16[128,8,128]{2,1,0:T(8,128)(2,1)}, u32[]{:S(2)}, u32[]{:S(2)}) %collective-permute-start.1) | collective-permute-done | bytes 262176 | tf_op jit(solution)/shard_map/ppermute | solution.py:346
  34.4 0.0 copy-start.1
  34.4 1.0 copy-done.1
  35.4 5.4 %states.3 = (f32[2,384,128]{2,1,0:T(8,128)S(1)}, bf16[2,128,128]{2,1,0:T(8,128)(2,1)S(1)}, bf16[2,128,128]{2,1,0:T(8,128)(2,1)S(1)}, bf16[2,192,128]{2,1,0:T(8,128)(2,1)S(1)}) custom-call(s32[2]{0:T(128)S(1)} %pad_add_fusion.where.refs_0_, bf16[3,128,2048]{2,1,0:T(8,128)(2,1)S(1)} %get-tuple-element.42.proj.refs_1_, ...), custom_call_target="tpu_custom_call" | custom-call | flops 4000000000 | bytes 4000000 | tf_op jit(solution)/shard_map/states/pallas_call | solution.py:395
  40.9 1.0 collective-permute-start.5
  41.9 0.5 collective-permute-start.6
  42.4 0.0 copy-start.2
  42.4 1.9 %collective-permute-start.7 = (bf16[2,192,128]{2,1,0:T(8,128)(2,1)S(1)}, bf16[2,192,128]{2,1,0:T(8,128)(2,1)S(1)}, u32[]{:S(2)}, u32[]{:S(2)}) collective-permute-start(bf16[2,192,128]{2,1,0:T(8,128)(2,1)S(1)} %get-tuple-element.47), channel_id=1, source_target_pairs={{0,192},{64,0},{128,64},{192,128},{1,193},{65,1},{129,65},{193,129... | collective-permute-start | bytes 294920 | tf_op jit(solution)/shard_map/ppermute | solution.py:413
  44.3 0.0 copy-done
  44.3 5.4 %states.2 = (f32[2,384,128]{2,1,0:T(8,128)S(1)}, bf16[2,128,128]{2,1,0:T(8,128)(2,1)S(1)}, bf16[2,128,128]{2,1,0:T(8,128)(2,1)S(1)}, bf16[2,192,128]{2,1,0:T(8,128)(2,1)S(1)}) custom-call(s32[2]{0:T(128)S(1)} %pad_add_fusion.where.refs_0_, bf16[3,128,2048]{2,1,0:T(8,128)(2,1)S(1)} %get-tuple-element.34.proj.refs_1_, ...), custom_call_target="tpu_custom_call" | custom-call | flops 4000000000 | bytes 4000000 | tf_op jit(solution)/shard_map/states/pallas_call | solution.py:395
  49.8 0.3 collective-permute-start.2
  50.1 1.2 %collective-permute-start.3 = (bf16[2,128,128]{2,1,0:T(8,128)(2,1)S(1)}, bf16[2,128,128]{2,1,0:T(8,128)(2,1)S(1)}, u32[]{:S(2)}, u32[]{:S(2)}) collective-permute-start(bf16[2,128,128]{2,1,0:T(8,128)(2,1)S(1)} %get-tuple-element.40), channel_id=1, source_target_pairs={{0,128},{64,192},{128,0},{192,64},{1,129},{65,193},{129,1},{193,65... | collective-permute-start | bytes 196616 | tf_op jit(solution)/shard_map/ppermute | solution.py:413
  51.3 0.0 collective-permute-done.5.refs_5_
  51.3 2.3 %collective-permute-start.4 = (bf16[2,192,128]{2,1,0:T(8,128)(2,1)S(1)}, bf16[2,192,128]{2,1,0:T(8,128)(2,1)S(1)}, u32[]{:S(2)}, u32[]{:S(2)}) collective-permute-start(bf16[2,192,128]{2,1,0:T(8,128)(2,1)S(1)} %get-tuple-element.41), channel_id=1, source_target_pairs={{0,192},{64,0},{128,64},{192,128},{1,193},{65,1},{129,65},{193,129... | collective-permute-start | bytes 294920 | tf_op jit(solution)/shard_map/ppermute | solution.py:413
  53.6 0.0 collective-permute-done.6.refs_6_
  53.6 0.0 collective-permute-done.7.refs_7_
  53.6 0.0 copy-done.2
  53.6 13.7 %final.2 = (bf16[128,4096]{1,0:T(8,128)(2,1)}, bf16[3,128,4096]{2,1,0:T(8,128)(2,1)}, bf16[128,6,128]{2,1,0:T(8,128)(2,1)S(1)}, bf16[128,6,128]{2,1,0:T(8,128)(2,1)S(1)}) custom-call(s32[2]{0:T(128)S(1)} %pad_add_fusion.where.refs_0_, bf16[3,128,2048]{2,1,0:T(8,128)(2,1)S(1)} %get-tuple-element.42.proj.refs_1_, ...), custom_call_target="tpu_custom_call" | custom-call | flops 8000000000 | bytes 8000000 | tf_op jit(solution)/shard_map/final/pallas_call | solution.py:426
  67.3 0.0 collective-permute-done.2.refs_5_
  67.3 0.0 collective-permute-done.3.refs_6_
  67.3 0.0 collective-permute-done.4.refs_7_
  67.3 13.7 %final.3 = (bf16[128,4096]{1,0:T(8,128)(2,1)}, bf16[3,128,4096]{2,1,0:T(8,128)(2,1)}, bf16[128,6,128]{2,1,0:T(8,128)(2,1)S(1)}, bf16[128,6,128]{2,1,0:T(8,128)(2,1)S(1)}) custom-call(s32[2]{0:T(128)S(1)} %pad_add_fusion.where.refs_0_, ...), custom_call_target="tpu_custom_call", output_to_operand_aliasing={{0}: (8, {}), {1}: (9, {}), {2}: (10, {}), {3}: (11, {})} | custom-call | flops 8000000000 | bytes 8000000 | tf_op jit(solution)/shard_map/final/pallas_call | solution.py:426
  81.1 2.1 %collective-permute-start.8 = (bf16[128,6,128]{2,1,0:T(8,128)(2,1)S(1)}, bf16[128,6,128]{2,1,0:T(8,128)(2,1)S(1)}, u32[]{:S(2)}, u32[]{:S(2)}) collective-permute-start(bf16[128,6,128]{2,1,0:T(8,128)(2,1)S(1)} %get-tuple-element.55), channel_id=1, source_target_pairs={{0,1},{1,0},{2,3},{3,2},{4,5},{5,4},{6,7},{7,6},{8,9},{9,8},{10,11... | collective-permute-start | bytes 589832 | tf_op jit(solution)/shard_map/ppermute | solution.py:346
  83.1 1.2 %collective-permute-done.8 = bf16[128,6,128]{2,1,0:T(8,128)(2,1)S(1)} collective-permute-done((bf16[128,6,128]{2,1,0:T(8,128)(2,1)S(1)}, bf16[128,6,128]{2,1,0:T(8,128)(2,1)S(1)}, u32[]{:S(2)}, u32[]{:S(2)}) %collective-permute-start.8) | collective-permute-done | bytes 196640 | tf_op jit(solution)/shard_map/ppermute | solution.py:346
  84.3 0.1 add_convert_fusion
  84.4 18.0 %all_to_all.10.arrived = bf16[128,6,128]{2,1,0:T(8,128)(2,1)} all-to-all(bf16[128,6,128]{2,1,0:T(8,128)(2,1)S(1)} %add_convert_fusion), channel_id=1, replica_groups={{0,2,4,6,8,10,12,14,16,18,20,22,24,26,28,30,32,34,36,38,40,42,44,46,48,..., dimensions={0} | all-to-all | bytes 393216 | tf_op jit(solution)/shard_map/all_to_all | solution.py:343
  102.4 1.8 %collect.1 = (f32[3,3,16]{2,1,0:T(4,128)}, f32[16,16]{1,0:T(8,128)}, f32[16,16]{1,0:T(8,128)}) custom-call(bf16[128,6,128]{2,1,0:T(8,128)(2,1)} %all_to_all.10.arrived, f32[16,16]{1,0:T(8,128)} %residue.3, f32[16,16]{1,0:T(8,128)} %log_decay.3), custom_call_target="tpu_custom_call" | custom-call | tf_op jit(solution)/shard_map/collect/pallas_call | solution.py:450
Async XLA Ops:
  2.2 27.6 %all-to-all-start = ((bf16[128,8,128]{2,1,0:T(8,128)(2,1)}), bf16[128,8,128]{2,1,0:T(8,128)(2,1)S(1)}, u32[]{:S(2)}, u32[]{:S(2)}) async-start(bf16[128,8,128]{2,1,0:T(8,128)(2,1)} %spread.1), calls=%async_computation | async-start | bytes 524288 | tf_op jit(solution)/shard_map/all_to_all | solution.py:343
  19.5 4.8 %copy-start.3 = (bf16[1,128,4096]{2,1,0:T(8,128)(2,1)S(1)}, bf16[1,128,4096]{2,1,0:T(8,128)(2,1)}, u32[]{:S(2)}) copy-start(bf16[1,128,4096]{2,1,0:T(8,128)(2,1)} %param.9) | copy-start | bytes 3145732
  19.5 5.9 %collective-permute-start = (bf16[3,2,4096]{2,1,0:T(2,128)(2,1)S(1)}, bf16[3,2,4096]{2,1,0:T(2,128)(2,1)S(1)}, u32[]{:S(2)}, u32[]{:S(2)}) collective-permute-start(bf16[3,2,4096]{2,1,0:T(2,128)(2,1)S(1)} %slice.15), channel_id=1, source_target_pairs={{0,64},{64,128},{128,192},{1,65},{65,129},{129,193},{2,66},{66,130... | collective-permute-start | bytes 147464 | tf_op jit(solution)/shard_map/ppermute | solution.py:358
  29.8 4.6 %collective-permute-start.1 = (bf16[128,8,128]{2,1,0:T(8,128)(2,1)S(1)}, bf16[128,8,128]{2,1,0:T(8,128)(2,1)}, u32[]{:S(2)}, u32[]{:S(2)}) collective-permute-start(bf16[128,8,128]{2,1,0:T(8,128)(2,1)S(1)} %all-to-all-done.wire), channel_id=1, source_target_pairs={{0,1},{1,0},{2,3},{3,2},{4,5},{5,4},{6,7},{7,6},{8,9},{9,8},{10,11... | collective-permute-start | bytes 786440 | tf_op jit(solution)/shard_map/ppermute | solution.py:346
  33.2 11.2 %copy-start = (bf16[128,2048]{1,0:T(8,128)(2,1)S(1)}, bf16[128,2048]{1,0:T(8,128)(2,1)}, u32[]{:S(2)}) copy-start(bf16[128,2048]{1,0:T(8,128)(2,1)} %get-tuple-element.36.cot.refs_3_) | copy-start | bytes 1572868
  34.4 1.0 copy-start.1
  40.9 10.4 %collective-permute-start.5 = (bf16[2,128,128]{2,1,0:T(8,128)(2,1)S(1)}, bf16[2,128,128]{2,1,0:T(8,128)(2,1)S(1)}, u32[]{:S(2)}, u32[]{:S(2)}) collective-permute-start(bf16[2,128,128]{2,1,0:T(8,128)(2,1)S(1)} %get-tuple-element.45), channel_id=1, source_target_pairs={{0,64},{64,128},{128,192},{192,0},{1,65},{65,129},{129,193},{193,1... | collective-permute-start | bytes 196616 | tf_op jit(solution)/shard_map/ppermute | solution.py:413
  41.9 11.7 %collective-permute-start.6 = (bf16[2,128,128]{2,1,0:T(8,128)(2,1)S(1)}, bf16[2,128,128]{2,1,0:T(8,128)(2,1)S(1)}, u32[]{:S(2)}, u32[]{:S(2)}) collective-permute-start(bf16[2,128,128]{2,1,0:T(8,128)(2,1)S(1)} %get-tuple-element.46), channel_id=1, source_target_pairs={{0,128},{64,192},{128,0},{192,64},{1,129},{65,193},{129,1},{193,65... | collective-permute-start | bytes 196616 | tf_op jit(solution)/shard_map/ppermute | solution.py:413
  42.4 11.2 %copy-start.2 = (bf16[128,2048]{1,0:T(8,128)(2,1)S(1)}, bf16[128,2048]{1,0:T(8,128)(2,1)}, u32[]{:S(2)}) copy-start(bf16[128,2048]{1,0:T(8,128)(2,1)} %get-tuple-element.43.cot.refs_3_) | copy-start | bytes 1572868
  42.4 11.2 %collective-permute-start.7 = (bf16[2,192,128]{2,1,0:T(8,128)(2,1)S(1)}, bf16[2,192,128]{2,1,0:T(8,128)(2,1)S(1)}, u32[]{:S(2)}, u32[]{:S(2)}) collective-permute-start(bf16[2,192,128]{2,1,0:T(8,128)(2,1)S(1)} %get-tuple-element.47), channel_id=1, source_target_pairs={{0,192},{64,0},{128,64},{192,128},{1,193},{65,1},{129,65},{193,129... | collective-permute-start | bytes 294920 | tf_op jit(solution)/shard_map/ppermute | solution.py:413
  49.8 17.5 %collective-permute-start.2 = (bf16[2,128,128]{2,1,0:T(8,128)(2,1)S(1)}, bf16[2,128,128]{2,1,0:T(8,128)(2,1)S(1)}, u32[]{:S(2)}, u32[]{:S(2)}) collective-permute-start(bf16[2,128,128]{2,1,0:T(8,128)(2,1)S(1)} %get-tuple-element.39), channel_id=1, source_target_pairs={{0,64},{64,128},{128,192},{192,0},{1,65},{65,129},{129,193},{193,1... | collective-permute-start | bytes 196616 | tf_op jit(solution)/shard_map/ppermute | solution.py:413
  50.1 17.2 %collective-permute-start.3 = (bf16[2,128,128]{2,1,0:T(8,128)(2,1)S(1)}, bf16[2,128,128]{2,1,0:T(8,128)(2,1)S(1)}, u32[]{:S(2)}, u32[]{:S(2)}) collective-permute-start(bf16[2,128,128]{2,1,0:T(8,128)(2,1)S(1)} %get-tuple-element.40), channel_id=1, source_target_pairs={{0,128},{64,192},{128,0},{192,64},{1,129},{65,193},{129,1},{193,65... | collective-permute-start | bytes 196616 | tf_op jit(solution)/shard_map/ppermute | solution.py:413
  51.3 16.0 %collective-permute-start.4 = (bf16[2,192,128]{2,1,0:T(8,128)(2,1)S(1)}, bf16[2,192,128]{2,1,0:T(8,128)(2,1)S(1)}, u32[]{:S(2)}, u32[]{:S(2)}) collective-permute-start(bf16[2,192,128]{2,1,0:T(8,128)(2,1)S(1)} %get-tuple-element.41), channel_id=1, source_target_pairs={{0,192},{64,0},{128,64},{192,128},{1,193},{65,1},{129,65},{193,129... | collective-permute-start | bytes 294920 | tf_op jit(solution)/shard_map/ppermute | solution.py:413
  81.1 3.2 %collective-permute-start.8 = (bf16[128,6,128]{2,1,0:T(8,128)(2,1)S(1)}, bf16[128,6,128]{2,1,0:T(8,128)(2,1)S(1)}, u32[]{:S(2)}, u32[]{:S(2)}) collective-permute-start(bf16[128,6,128]{2,1,0:T(8,128)(2,1)S(1)} %get-tuple-element.55), channel_id=1, source_target_pairs={{0,1},{1,0},{2,3},{3,2},{4,5},{5,4},{6,7},{7,6},{8,9},{9,8},{10,11... | collective-permute-start | bytes 589832 | tf_op jit(solution)/shard_map/ppermute | solution.py:346

commit v7 on v6

--- a/solution.py
+++ b/solution.py
@@ -146,7 +146,7 @@
 def state_kernel(where, proj, above, cot, wire, wire_pair, par, send1, send2, send3, signal, xs, gs, wires, halo):
     chunk = cot.shape[0]
     both = by_core(where[1], wire[...].astype(F32), wire_pair[...].astype(F32))
-    wires[...] = jnp.stack(both, axis=1).reshape(wires.shape)
+    wires[0:512, :] = jnp.stack(both, axis=1).reshape(512, LANES)
     early = lax.broadcasted_iota(jnp.int32, (8, LANES), 0) < 6
 
     for lane in range(8):
@@ -321,7 +321,7 @@
         for q in range(SUM_ROWS // 8):
             lines_s[pl.ds(lane * 64 + q, 8, stride=8), :] = lines_of_rows(sums[tile_rows(q, lane), :])
 
-    lines = lines_s[...].reshape(32, 2, 8, LANES)[:, :, : SUM_ROWS // 8].astype(BF)
+    lines = lines_s[0:512, :].reshape(32, 2, 8, LANES)[:, :, : SUM_ROWS // 8].astype(BF)
     sums_own[...], sums_pair[...] = by_core(where[1], lines[:, 0], lines[:, 1])
 
 
@@ -400,7 +400,7 @@
             out_shape=[shape((steps, 8 * PAR_ROWS, LANES), F32)]
             + [shape((steps, n, LANES), BF) for n in sizes],
             scratch_shapes=[
-                vmem(3, chunk + 8, LANES), vmem(chunk * 8, LANES), vmem(chunk * 8, LANES), vmem(512, LANES),
+                vmem(3, chunk + 8, LANES), vmem(chunk * 8 + 8, LANES), vmem(chunk * 8 + 8, LANES), vmem(520, LANES),
                 vmem(64, LANES),
             ],
             compiler_params=params,
@@ -433,10 +433,10 @@
             out_shape=results,
             scratch_shapes=[
                 vmem(8, 3, chunk + 16, LANES), vmem(64, LANES), vmem(3, longer, LANES),
-                vmem(longer * 8, LANES), vmem(longer * 8, LANES),
-                vmem(longer * 8, LANES), vmem(longer * 8, LANES),
+                vmem(longer * 8 + 8, LANES), vmem(longer * 8 + 8, LANES),
+                vmem(longer * 8 + 8, LANES), vmem(longer * 8 + 8, LANES),
                 vmem(8, longer, LANES), vmem(8, longer, LANES), vmem(8, longer, LANES),
-                vmem(chunk, HALF, 8, LANES), vmem(8 * SUM_ROWS, LANES), vmem(512, LANES),
+                vmem(chunk, HALF, 8, LANES), vmem(8 * SUM_ROWS, LANES), vmem(520, LANES),
             ],
             input_output_aliases={8 + i: i for i in range(len(made))},
             compiler_params=params,

time: 105 us -> 105 us (level)
  no operation moved by 1% of the time
where the time goes in v7:
time: 105 us; the launch traced here: 104 us
  Pallas kernels  41.6 us (40%)
  starting transfers between devices  31.7 us (30%)
  blocking collectives  18 us (17%)
  waiting for transfers between devices  6.73 us (6%)
  local copies, waits for them, and re-layouts  5.22 us (5%)
    pallas_call x2, Pallas kernels, body(): pl.pallas_call(final_kernel, grid=(steps,), in_specs=[scalar, local(3, ch...  27.4 us
    all_to_all x1, blocking collectives, from_all(): lax.all_to_all(values, devices, 0, 0, tiled=True, axis_index_groups=cores)  18 us
    all_to_all x1, starting transfers between devices, from_all(): lax.all_to_all(values, devices, 0, 0, tiled=True, axis_index_groups=cores)  16.3 us
    pallas_call x2, Pallas kernels, body(): pl.pallas_call(state_kernel, grid=(steps,), in_specs=[scalar, local(3, ch...  10.9 us
    ppermute x6, starting transfers between devices, body(): lax.ppermute(values, ctx, [(i, (i + k) % n_ctx) for i in range(n_ctx)])  7.25 us
    ppermute x2, starting transfers between devices, from_pair(): return lax.ppermute(values, zero, [(i, i ^ 1) for i in range(n_zero)])  5.39 us
    all_to_all x1, waiting for transfers between devices, from_all(): lax.all_to_all(values, devices, 0, 0, tiled=True, axis_index_groups=cores)  4.33 us
    ppermute x1, starting transfers between devices, body(): lax.ppermute(signal[:, chunk - 2:], ctx, [(i, i + 1) for i in range(n_ctx...  2.71 us
  transfers between devices with their start and end apart: 10, of which 3 were waited for; matrix products, arithmetic and copies ran while one was open for 4% of the time, Pallas kernels for 18%

profile of v7, /device:TPU:1, one launch (start us, length us, event | category | flops | bytes accessed | tf_op | source)
XLA Modules:
  0.0 104.2 jit_solution(13097587420684775492)
XLA Ops:
  0.6 1.5 %spread.1 = bf16[128,8,128]{2,1,0:T(8,128)(2,1)} custom-call(f32[3,3,16]{2,1,0:T(4,128)} %short_weight.1, f32[16,16]{1,0:T(8,128)} %residue.3, f32[16,16]{1,0:T(8,128)} %log_decay.3), custom_call_target="tpu_custom_call" | custom-call | tf_op jit(solution)/shard_map/spread/pallas_call | solution.py:349
  2.2 16.3 %all-to-all-start = ((bf16[128,8,128]{2,1,0:T(8,128)(2,1)}), bf16[128,8,128]{2,1,0:T(8,128)(2,1)S(1)}, u32[]{:S(2)}, u32[]{:S(2)}) async-start(bf16[128,8,128]{2,1,0:T(8,128)(2,1)} %spread.1), calls=%async_computation | async-start | bytes 524288 | tf_op jit(solution)/shard_map/all_to_all | solution.py:343
  18.5 1.0 slice.15
  19.5 0.0 copy-start.3
  19.5 2.7 %collective-permute-start = (bf16[3,2,4096]{2,1,0:T(2,128)(2,1)S(1)}, bf16[3,2,4096]{2,1,0:T(2,128)(2,1)S(1)}, u32[]{:S(2)}, u32[]{:S(2)}) collective-permute-start(bf16[3,2,4096]{2,1,0:T(2,128)(2,1)S(1)} %slice.15), channel_id=1, source_target_pairs={{0,64},{64,128},{128,192},{1,65},{65,129},{129,193},{2,66},{66,130... | collective-permute-start | bytes 147464 | tf_op jit(solution)/shard_map/ppermute | solution.py:358
  22.2 2.1 %fusion = (bf16[3,128,2048]{2,1,0:T(8,128)(2,1)S(1)}, bf16[3,128,2048]{2,1,0:T(8,128)(2,1)S(1)}) fusion(bf16[3,128,4096]{2,1,0:T(8,128)(2,1)} %bitcast.11), kind=kLoop, calls=%fused_computation.2 | loop fusion | bytes 6291456 | tf_op jit(solution)/shard_map/slice | solution.py:386
  24.3 0.0 copy-done.3
  24.3 1.1 %fusion.1 = (bf16[128,2048]{1,0:T(8,128)(2,1)}, bf16[128,2048]{1,0:T(8,128)(2,1)}) fusion(bf16[128,4096]{1,0:T(8,128)(2,1)S(1)} %bitcast.12), kind=kLoop, calls=%fused_computation.3 | loop fusion | bytes 2097152 | tf_op jit(solution)/shard_map/slice | solution.py:387
  25.4 0.0 collective-permute-done.above.refs_2_
  25.4 4.3 %all-to-all-done.wire = bf16[128,8,128]{2,1,0:T(8,128)(2,1)S(1)} async-done(((bf16[128,8,128]{2,1,0:T(8,128)(2,1)}), bf16[128,8,128]{2,1,0:T(8,128)(2,1)S(1)}, u32[]{:S(2)}, u32[]{:S(2)}) %all-to-all-start) | async-done | bytes 262176 | tf_op jit(solution)/shard_map/all_to_all | solution.py:343
  29.8 3.3 %collective-permute-start.1 = (bf16[128,8,128]{2,1,0:T(8,128)(2,1)S(1)}, bf16[128,8,128]{2,1,0:T(8,128)(2,1)}, u32[]{:S(2)}, u32[]{:S(2)}) collective-permute-start(bf16[128,8,128]{2,1,0:T(8,128)(2,1)S(1)} %all-to-all-done.wire), channel_id=1, source_target_pairs={{0,1},{1,0},{2,3},{3,2},{4,5},{5,4},{6,7},{7,6},{8,9},{9,8},{10,11... | collective-permute-start | bytes 786440 | tf_op jit(solution)/shard_map/ppermute | solution.py:346
  33.1 0.1 pad_add_fusion.where.refs_0_
  33.2 0.0 copy-start
  33.2 1.2 %collective-permute-done.1.wire_pair = bf16[128,8,128]{2,1,0:T(8,128)(2,1)} collective-permute-done((bf16[128,8,128]{2,1,0:T(8,128)(2,1)S(1)}, bf16[128,8,128]{2,1,0:T(8,128)(2,1)}, u32[]{:S(2)}, u32[]{:S(2)}) %collective-permute-start.1) | collective-permute-done | bytes 262176 | tf_op jit(solution)/shard_map/ppermute | solution.py:346
  34.4 0.0 copy-start.1
  34.4 1.0 copy-done.1
  35.4 5.4 %states.3 = (f32[2,384,128]{2,1,0:T(8,128)S(1)}, bf16[2,128,128]{2,1,0:T(8,128)(2,1)S(1)}, bf16[2,128,128]{2,1,0:T(8,128)(2,1)S(1)}, bf16[2,192,128]{2,1,0:T(8,128)(2,1)S(1)}) custom-call(s32[2]{0:T(128)S(1)} %pad_add_fusion.where.refs_0_, bf16[3,128,2048]{2,1,0:T(8,128)(2,1)S(1)} %get-tuple-element.42.proj.refs_1_, ...), custom_call_target="tpu_custom_call" | custom-call | flops 4000000000 | bytes 4000000 | tf_op jit(solution)/shard_map/states/pallas_call | solution.py:395
  40.9 1.0 collective-permute-start.5
  41.9 0.5 collective-permute-start.6
  42.4 0.0 copy-start.2
  42.4 1.9 %collective-permute-start.7 = (bf16[2,192,128]{2,1,0:T(8,128)(2,1)S(1)}, bf16[2,192,128]{2,1,0:T(8,128)(2,1)S(1)}, u32[]{:S(2)}, u32[]{:S(2)}) collective-permute-start(bf16[2,192,128]{2,1,0:T(8,128)(2,1)S(1)} %get-tuple-element.47), channel_id=1, source_target_pairs={{0,192},{64,0},{128,64},{192,128},{1,193},{65,1},{129,65},{193,129... | collective-permute-start | bytes 294920 | tf_op jit(solution)/shard_map/ppermute | solution.py:413
  44.3 0.0 copy-done
  44.3 5.4 %states.2 = (f32[2,384,128]{2,1,0:T(8,128)S(1)}, bf16[2,128,128]{2,1,0:T(8,128)(2,1)S(1)}, bf16[2,128,128]{2,1,0:T(8,128)(2,1)S(1)}, bf16[2,192,128]{2,1,0:T(8,128)(2,1)S(1)}) custom-call(s32[2]{0:T(128)S(1)} %pad_add_fusion.where.refs_0_, bf16[3,128,2048]{2,1,0:T(8,128)(2,1)S(1)} %get-tuple-element.34.proj.refs_1_, ...), custom_call_target="tpu_custom_call" | custom-call | flops 4000000000 | bytes 4000000 | tf_op jit(solution)/shard_map/states/pallas_call | solution.py:395
  49.8 0.3 collective-permute-start.2
  50.1 1.2 %collective-permute-start.3 = (bf16[2,128,128]{2,1,0:T(8,128)(2,1)S(1)}, bf16[2,128,128]{2,1,0:T(8,128)(2,1)S(1)}, u32[]{:S(2)}, u32[]{:S(2)}) collective-permute-start(bf16[2,128,128]{2,1,0:T(8,128)(2,1)S(1)} %get-tuple-element.40), channel_id=1, source_target_pairs={{0,128},{64,192},{128,0},{192,64},{1,129},{65,193},{129,1},{193,65... | collective-permute-start | bytes 196616 | tf_op jit(solution)/shard_map/ppermute | solution.py:413
  51.3 0.0 collective-permute-done.5.refs_5_
  51.3 2.3 %collective-permute-start.4 = (bf16[2,192,128]{2,1,0:T(8,128)(2,1)S(1)}, bf16[2,192,128]{2,1,0:T(8,128)(2,1)S(1)}, u32[]{:S(2)}, u32[]{:S(2)}) collective-permute-start(bf16[2,192,128]{2,1,0:T(8,128)(2,1)S(1)} %get-tuple-element.41), channel_id=1, source_target_pairs={{0,192},{64,0},{128,64},{192,128},{1,193},{65,1},{129,65},{193,129... | collective-permute-start | bytes 294920 | tf_op jit(solution)/shard_map/ppermute | solution.py:413
  53.6 0.0 collective-permute-done.6.refs_6_
  53.6 0.0 collective-permute-done.7.refs_7_
  53.6 0.0 copy-done.2
  53.6 13.7 %final.2 = (bf16[128,4096]{1,0:T(8,128)(2,1)}, bf16[3,128,4096]{2,1,0:T(8,128)(2,1)}, bf16[128,6,128]{2,1,0:T(8,128)(2,1)S(1)}, bf16[128,6,128]{2,1,0:T(8,128)(2,1)S(1)}) custom-call(s32[2]{0:T(128)S(1)} %pad_add_fusion.where.refs_0_, bf16[3,128,2048]{2,1,0:T(8,128)(2,1)S(1)} %get-tuple-element.42.proj.refs_1_, ...), custom_call_target="tpu_custom_call" | custom-call | flops 8000000000 | bytes 8000000 | tf_op jit(solution)/shard_map/final/pallas_call | solution.py:426
  67.3 0.0 collective-permute-done.2.refs_5_
  67.3 0.0 collective-permute-done.3.refs_6_
  67.3 0.0 collective-permute-done.4.refs_7_
  67.3 13.7 %final.3 = (bf16[128,4096]{1,0:T(8,128)(2,1)}, bf16[3,128,4096]{2,1,0:T(8,128)(2,1)}, bf16[128,6,128]{2,1,0:T(8,128)(2,1)S(1)}, bf16[128,6,128]{2,1,0:T(8,128)(2,1)S(1)}) custom-call(s32[2]{0:T(128)S(1)} %pad_add_fusion.where.refs_0_, ...), custom_call_target="tpu_custom_call", output_to_operand_aliasing={{0}: (8, {}), {1}: (9, {}), {2}: (10, {}), {3}: (11, {})} | custom-call | flops 8000000000 | bytes 8000000 | tf_op jit(solution)/shard_map/final/pallas_call | solution.py:426
  81.0 2.1 %collective-permute-start.8 = (bf16[128,6,128]{2,1,0:T(8,128)(2,1)S(1)}, bf16[128,6,128]{2,1,0:T(8,128)(2,1)S(1)}, u32[]{:S(2)}, u32[]{:S(2)}) collective-permute-start(bf16[128,6,128]{2,1,0:T(8,128)(2,1)S(1)} %get-tuple-element.55), channel_id=1, source_target_pairs={{0,1},{1,0},{2,3},{3,2},{4,5},{5,4},{6,7},{7,6},{8,9},{9,8},{10,11... | collective-permute-start | bytes 589832 | tf_op jit(solution)/shard_map/ppermute | solution.py:346
  83.1 1.2 %collective-permute-done.8 = bf16[128,6,128]{2,1,0:T(8,128)(2,1)S(1)} collective-permute-done((bf16[128,6,128]{2,1,0:T(8,128)(2,1)S(1)}, bf16[128,6,128]{2,1,0:T(8,128)(2,1)S(1)}, u32[]{:S(2)}, u32[]{:S(2)}) %collective-permute-start.8) | collective-permute-done | bytes 196640 | tf_op jit(solution)/shard_map/ppermute | solution.py:346
  84.2 0.1 add_convert_fusion
  84.3 18.0 %all_to_all.10.arrived = bf16[128,6,128]{2,1,0:T(8,128)(2,1)} all-to-all(bf16[128,6,128]{2,1,0:T(8,128)(2,1)S(1)} %add_convert_fusion), channel_id=1, replica_groups={{0,2,4,6,8,10,12,14,16,18,20,22,24,26,28,30,32,34,36,38,40,42,44,46,48,..., dimensions={0} | all-to-all | bytes 393216 | tf_op jit(solution)/shard_map/all_to_all | solution.py:343
  102.4 1.8 %collect.1 = (f32[3,3,16]{2,1,0:T(4,128)}, f32[16,16]{1,0:T(8,128)}, f32[16,16]{1,0:T(8,128)}) custom-call(bf16[128,6,128]{2,1,0:T(8,128)(2,1)} %all_to_all.10.arrived, f32[16,16]{1,0:T(8,128)} %residue.3, f32[16,16]{1,0:T(8,128)} %log_decay.3), custom_call_target="tpu_custom_call" | custom-call | tf_op jit(solution)/shard_map/collect/pallas_call | solution.py:450
Async XLA Ops:
  2.2 27.6 %all-to-all-start = ((bf16[128,8,128]{2,1,0:T(8,128)(2,1)}), bf16[128,8,128]{2,1,0:T(8,128)(2,1)S(1)}, u32[]{:S(2)}, u32[]{:S(2)}) async-start(bf16[128,8,128]{2,1,0:T(8,128)(2,1)} %spread.1), calls=%async_computation | async-start | bytes 524288 | tf_op jit(solution)/shard_map/all_to_all | solution.py:343
  19.5 4.8 %copy-start.3 = (bf16[1,128,4096]{2,1,0:T(8,128)(2,1)S(1)}, bf16[1,128,4096]{2,1,0:T(8,128)(2,1)}, u32[]{:S(2)}) copy-start(bf16[1,128,4096]{2,1,0:T(8,128)(2,1)} %param.9) | copy-start | bytes 3145732
  19.5 5.9 %collective-permute-start = (bf16[3,2,4096]{2,1,0:T(2,128)(2,1)S(1)}, bf16[3,2,4096]{2,1,0:T(2,128)(2,1)S(1)}, u32[]{:S(2)}, u32[]{:S(2)}) collective-permute-start(bf16[3,2,4096]{2,1,0:T(2,128)(2,1)S(1)} %slice.15), channel_id=1, source_target_pairs={{0,64},{64,128},{128,192},{1,65},{65,129},{129,193},{2,66},{66,130... | collective-permute-start | bytes 147464 | tf_op jit(solution)/shard_map/ppermute | solution.py:358
  29.8 4.6 %collective-permute-start.1 = (bf16[128,8,128]{2,1,0:T(8,128)(2,1)S(1)}, bf16[128,8,128]{2,1,0:T(8,128)(2,1)}, u32[]{:S(2)}, u32[]{:S(2)}) collective-permute-start(bf16[128,8,128]{2,1,0:T(8,128)(2,1)S(1)} %all-to-all-done.wire), channel_id=1, source_target_pairs={{0,1},{1,0},{2,3},{3,2},{4,5},{5,4},{6,7},{7,6},{8,9},{9,8},{10,11... | collective-permute-start | bytes 786440 | tf_op jit(solution)/shard_map/ppermute | solution.py:346
  33.2 11.2 %copy-start = (bf16[128,2048]{1,0:T(8,128)(2,1)S(1)}, bf16[128,2048]{1,0:T(8,128)(2,1)}, u32[]{:S(2)}) copy-start(bf16[128,2048]{1,0:T(8,128)(2,1)} %get-tuple-element.36.cot.refs_3_) | copy-start | bytes 1572868
  34.4 1.0 %copy-start.1 = (bf16[128,2048]{1,0:T(8,128)(2,1)S(1)}, bf16[128,2048]{1,0:T(8,128)(2,1)}, u32[]{:S(2)}) copy-start(bf16[128,2048]{1,0:T(8,128)(2,1)} %get-tuple-element.43.cot.refs_3_) | copy-start | bytes 1572868
  40.9 10.4 %collective-permute-start.5 = (bf16[2,128,128]{2,1,0:T(8,128)(2,1)S(1)}, bf16[2,128,128]{2,1,0:T(8,128)(2,1)S(1)}, u32[]{:S(2)}, u32[]{:S(2)}) collective-permute-start(bf16[2,128,128]{2,1,0:T(8,128)(2,1)S(1)} %get-tuple-element.45), channel_id=1, source_target_pairs={{0,64},{64,128},{128,192},{192,0},{1,65},{65,129},{129,193},{193,1... | collective-permute-start | bytes 196616 | tf_op jit(solution)/shard_map/ppermute | solution.py:413
  41.9 11.7 %collective-permute-start.6 = (bf16[2,128,128]{2,1,0:T(8,128)(2,1)S(1)}, bf16[2,128,128]{2,1,0:T(8,128)(2,1)S(1)}, u32[]{:S(2)}, u32[]{:S(2)}) collective-permute-start(bf16[2,128,128]{2,1,0:T(8,128)(2,1)S(1)} %get-tuple-element.46), channel_id=1, source_target_pairs={{0,128},{64,192},{128,0},{192,64},{1,129},{65,193},{129,1},{193,65... | collective-permute-start | bytes 196616 | tf_op jit(solution)/shard_map/ppermute | solution.py:413
  42.4 11.1 %copy-start.2 = (bf16[128,2048]{1,0:T(8,128)(2,1)S(1)}, bf16[128,2048]{1,0:T(8,128)(2,1)}, u32[]{:S(2)}) copy-start(bf16[128,2048]{1,0:T(8,128)(2,1)} %get-tuple-element.43.cot.refs_3_) | copy-start | bytes 1572868
  42.4 11.1 %collective-permute-start.7 = (bf16[2,192,128]{2,1,0:T(8,128)(2,1)S(1)}, bf16[2,192,128]{2,1,0:T(8,128)(2,1)S(1)}, u32[]{:S(2)}, u32[]{:S(2)}) collective-permute-start(bf16[2,192,128]{2,1,0:T(8,128)(2,1)S(1)} %get-tuple-element.47), channel_id=1, source_target_pairs={{0,192},{64,0},{128,64},{192,128},{1,193},{65,1},{129,65},{193,129... | collective-permute-start | bytes 294920 | tf_op jit(solution)/shard_map/ppermute | solution.py:413
  49.8 17.5 %collective-permute-start.2 = (bf16[2,128,128]{2,1,0:T(8,128)(2,1)S(1)}, bf16[2,128,128]{2,1,0:T(8,128)(2,1)S(1)}, u32[]{:S(2)}, u32[]{:S(2)}) collective-permute-start(bf16[2,128,128]{2,1,0:T(8,128)(2,1)S(1)} %get-tuple-element.39), channel_id=1, source_target_pairs={{0,64},{64,128},{128,192},{192,0},{1,65},{65,129},{129,193},{193,1... | collective-permute-start | bytes 196616 | tf_op jit(solution)/shard_map/ppermute | solution.py:413
  50.1 17.2 %collective-permute-start.3 = (bf16[2,128,128]{2,1,0:T(8,128)(2,1)S(1)}, bf16[2,128,128]{2,1,0:T(8,128)(2,1)S(1)}, u32[]{:S(2)}, u32[]{:S(2)}) collective-permute-start(bf16[2,128,128]{2,1,0:T(8,128)(2,1)S(1)} %get-tuple-element.40), channel_id=1, source_target_pairs={{0,128},{64,192},{128,0},{192,64},{1,129},{65,193},{129,1},{193,65... | collective-permute-start | bytes 196616 | tf_op jit(solution)/shard_map/ppermute | solution.py:413
  51.3 16.0 %collective-permute-start.4 = (bf16[2,192,128]{2,1,0:T(8,128)(2,1)S(1)}, bf16[2,192,128]{2,1,0:T(8,128)(2,1)S(1)}, u32[]{:S(2)}, u32[]{:S(2)}) collective-permute-start(bf16[2,192,128]{2,1,0:T(8,128)(2,1)S(1)} %get-tuple-element.41), channel_id=1, source_target_pairs={{0,192},{64,0},{128,64},{192,128},{1,193},{65,1},{129,65},{193,129... | collective-permute-start | bytes 294920 | tf_op jit(solution)/shard_map/ppermute | solution.py:413
  81.0 3.2 %collective-permute-start.8 = (bf16[128,6,128]{2,1,0:T(8,128)(2,1)S(1)}, bf16[128,6,128]{2,1,0:T(8,128)(2,1)S(1)}, u32[]{:S(2)}, u32[]{:S(2)}) collective-permute-start(bf16[128,6,128]{2,1,0:T(8,128)(2,1)S(1)} %get-tuple-element.55), channel_id=1, source_target_pairs={{0,1},{1,0},{2,3},{3,2},{4,5},{5,4},{6,7},{7,6},{8,9},{9,8},{10,11... | collective-permute-start | bytes 589832 | tf_op jit(solution)/shard_map/ppermute | solution.py:346
